TPU v7x, 32 devices: a whole 2x2x4 slice. The times are simulated.
32 devices in a mesh: seq: 8 (over y, x, core), wt: 4 (over z).
Axes of the slice: x: 2, y: 2, z: 4, core: 2. Of those that a mesh axis runs over, the one named last changes fastest.
Arguments:
- inputs: bfloat16 [4, 1024, 2560], P('wt', 'seq'), may hold values from -6 to 6
- segment: int32 [4, 1024], P('wt', 'seq'), may hold values from 0 to 32, as said below
- mixer_gain: float32 [2560], replicated, may hold values from 0.5 to 1.5
- input_weight: bfloat16 [2560, 2560], P(None, 'wt'), may hold values from -0.125 to 0.125
- branch_weight: bfloat16 [2560, 2560], P(None, 'wt'), may hold values from -0.125 to 0.125
- conv_weight: float32 [2560, 4], replicated, may hold values from -3 to 3
- recur_gate: bfloat16 [2560, 256], replicated, may hold values from -0.375 to 0.375
- input_gate: bfloat16 [2560, 256], replicated, may hold values from -0.375 to 0.375
- recur_bias: float32 [2560], replicated, may hold values from -6 to 6
- input_bias: float32 [2560], replicated, may hold values from -6 to 6
- decay_rate: float32 [2560], replicated, may hold values from -14 to -4
- output_weight: bfloat16 [2560, 2560], P(None, 'wt'), may hold values from -0.3125 to 0.3125
- second_gain: float32 [2560], replicated, may hold values from 0.5 to 1.5
- gate_weight: bfloat16 [2560, 7680], P(None, 'wt'), may hold values from -0.125 to 0.125
- up_weight: bfloat16 [2560, 7680], P(None, 'wt'), may hold values from -0.125 to 0.125
- down_weight: bfloat16 [2560, 7680], P(None, 'wt'), may hold values from -0.125 to 0.125
- cotangent: float32 [4, 1024, 2560], P('wt', 'seq'), may hold values from -6 to 6
Outputs:
- block_out: bfloat16 [4, 1024, 2560], P('wt', 'seq')
- input_grad: float32 [4, 1024, 2560], P('wt', 'seq')
- mixer_gain_grad: float32 [2560], P(('seq', 'wt'))
- input_weight_grad: float32 [2560, 2560], P(('seq', 'wt'))
- branch_weight_grad: float32 [2560, 2560], P(('seq', 'wt'))
- conv_weight_grad: float32 [2560, 4], P(('seq', 'wt'))
- recur_gate_grad: float32 [2560, 256], P(('seq', 'wt'))
- input_gate_grad: float32 [2560, 256], P(('seq', 'wt'))
- recur_bias_grad: float32 [2560], P(('seq', 'wt'))
- input_bias_grad: float32 [2560], P(('seq', 'wt'))
- decay_rate_grad: float32 [2560], P(('seq', 'wt'))
- output_weight_grad: float32 [2560, 2560], P(('seq', 'wt'))
- second_gain_grad: float32 [2560], P(('seq', 'wt'))
- gate_weight_grad: float32 [2560, 7680], P(('seq', 'wt'))
- up_weight_grad: float32 [2560, 7680], P(('seq', 'wt'))
- down_weight_grad: float32 [2560, 7680], P(('seq', 'wt'))
Inputs may be any that keep to these rules, and one draw needn't show every extreme that they name: `segment`: in every sequence the numbers start at 0 and rise by 0 or 1 from one position to the next. In each group of 1 sequence of one index of wt, one sequence, drawn from the seed, keeps document 0 up to its last 64 positions and starts exactly 32 new documents among those positions; every other sequence holds exactly 129 documents.
All inputs are finite; a program needn't handle non-finite values.
Results may differ from a plain program's by a relative error of at most 0.02.
Values may be sent and summed in bfloat16 or wider, within the bound.
A program may use at most 768 MiB of HBM per device.

v0:
```python
import jax
import jax.numpy as jnp
from jax import lax
from jax.sharding import PartitionSpec as P

EPSILON = 1e-06


def from_behind(x, axis, by):
    devices = lax.axis_size(axis)
    pairs = [(i, i + by) for i in range(devices) if 0 <= i + by < devices]
    return lax.ppermute(x, axis, pairs)


def gelu_tanh(values):
    return jax.nn.gelu(values, approximate=True)


def rms_scale(values, gain_row):
    return (
        values * lax.rsqrt(jnp.mean(values * values, axis=-1, keepdims=True) + EPSILON) * gain_row
    )


def combine(earlier_pair, later_pair):
    return (earlier_pair[0] * later_pair[0], later_pair[0] * earlier_pair[1] + later_pair[1])


def gate_split(values, gate_rows):
    head_size = gate_rows.shape[1]
    head_count = gate_rows.shape[0] // head_size
    return (
        values.reshape(values.shape[0], head_count, head_size),
        gate_rows.reshape(head_count, head_size, head_size),
    )


def block_product(values, gate_rows):
    blocks, gate_table = gate_split(values, gate_rows)
    mixed_heads = jnp.einsum("thi,hij->thj", blocks, gate_table, preferred_element_type=jnp.float32)
    return mixed_heads.reshape(values.shape[0], -1)


def block_back(slopes, gate_rows):
    blocks, gate_table = gate_split(slopes, gate_rows)
    mixed_heads = jnp.einsum("thj,hij->thi", blocks, gate_table, preferred_element_type=jnp.float32)
    return mixed_heads.reshape(slopes.shape[0], -1)


def block_grad(values, slopes, gate_rows):
    left_side, gate_table = gate_split(values, gate_rows)
    right_side, gate_table = gate_split(slopes, gate_rows)
    summed = jnp.einsum("thi,thj->hij", left_side, right_side, preferred_element_type=jnp.float32)
    return summed.reshape(gate_rows.shape)


def conv_apply(extended, conv_weight, same_doc):
    conv_reach = conv_weight.shape[1] - 1
    part_len = same_doc.shape[1]
    conv_sum = jnp.zeros((extended.shape[0], part_len, extended.shape[2]), jnp.float32)
    for offset in range(conv_reach + 1):
        window = extended[:, conv_reach - offset : conv_reach - offset + part_len, :]
        conv_sum = conv_sum + window * same_doc[:, :, offset : offset + 1] * conv_weight[:, offset]
    return conv_sum


def gate_math(c_value, recur_mm, input_mm, recur_bias, input_bias, decay_rate, reset_mask):
    recur_act = jax.nn.sigmoid(recur_mm + recur_bias)
    input_act = jax.nn.sigmoid(input_mm + input_bias)
    log_coef = -8.0 * jax.nn.softplus(decay_rate) * recur_act
    in_scale = jnp.where(reset_mask, 1.0, jnp.sqrt(-jnp.expm1(2.0 * log_coef)))
    return (log_coef, in_scale * c_value * input_act)


def mixer_weights(input_weight, branch_weight, output_weight):
    return (
        lax.all_gather(input_weight, "wt", axis=1, tiled=True),
        lax.all_gather(branch_weight, "wt", axis=1, tiled=True),
        lax.all_gather(output_weight, "wt", axis=1, tiled=True),
    )


def ffn_weights(gate_weight, up_weight, down_weight):
    return (
        lax.all_gather(gate_weight, "wt", axis=1, tiled=True),
        lax.all_gather(up_weight, "wt", axis=1, tiled=True),
        lax.all_gather(down_weight, "wt", axis=1, tiled=True),
    )


def to_channels(stacked):
    return lax.all_to_all(stacked, "seq", split_axis=3, concat_axis=2, tiled=True)


def from_channels(stacked):
    return lax.all_to_all(stacked, "seq", split_axis=2, concat_axis=3, tiled=True)


def on_device(
    inputs,
    segment,
    mixer_gain,
    input_weight,
    branch_weight,
    conv_weight,
    recur_gate,
    input_gate,
    recur_bias,
    input_bias,
    decay_rate,
    output_weight,
    second_gain,
    gate_weight,
    up_weight,
    down_weight,
    cotangent,
):
    seq_count, part_len, model_width = inputs.shape
    row_count = seq_count * part_len
    conv_reach = conv_weight.shape[1] - 1
    lru_width = conv_weight.shape[0]
    doc_all = lax.all_gather(segment, "seq", axis=1, tiled=True)
    row_start = lax.axis_index("seq") * part_len
    lead_pad = jnp.full((seq_count, conv_reach), -1, jnp.int32)
    doc_window = lax.dynamic_slice_in_dim(
        jnp.concatenate([lead_pad, doc_all], axis=1), row_start, part_len + conv_reach, 1
    )
    doc_here = doc_window[:, conv_reach:]
    same_doc = jnp.stack(
        [
            doc_window[:, conv_reach - offset : conv_reach - offset + part_len] == doc_here
            for offset in range(conv_reach + 1)
        ],
        axis=-1,
    ).astype(jnp.float32)
    reset_mask = (doc_window[:, conv_reach - 1 : conv_reach - 1 + part_len] != doc_here).reshape(
        row_count, 1
    )
    doc_before = jnp.concatenate([jnp.full((seq_count, 1), -1, jnp.int32), doc_all[:, :-1]], axis=1)
    keep_state = (doc_all == doc_before).astype(jnp.float32)[:, :, None]
    flat_in = inputs.astype(jnp.float32).reshape(row_count, model_width)
    mixer_norm, mixer_pull = jax.vjp(rms_scale, flat_in, mixer_gain)
    normed = mixer_norm.astype(jnp.bfloat16)
    full_in, full_branch, full_out = mixer_weights(input_weight, branch_weight, output_weight)
    u_value = jnp.dot(normed, full_in, preferred_element_type=jnp.float32).astype(jnp.bfloat16)
    y_value = jnp.dot(normed, full_branch, preferred_element_type=jnp.float32)
    u_seq = u_value.reshape(seq_count, part_len, lru_width)
    rim_rows = from_behind(u_seq[:, part_len - conv_reach :, :], "seq", 1)
    extended = jnp.concatenate([rim_rows, u_seq], axis=1).astype(jnp.float32)

    def conv_local(extended_in, weight_in):
        return conv_apply(extended_in, weight_in, same_doc)

    conv_out, conv_pull = jax.vjp(conv_local, extended, conv_weight)
    c_value = conv_out.reshape(row_count, lru_width).astype(jnp.bfloat16)
    recur_mm = block_product(c_value, recur_gate)
    input_mm = block_product(c_value, input_gate)

    def gate_local(c_in, recur_in, input_in, recur_shift, input_shift, decay_in):
        return gate_math(c_in, recur_in, input_in, recur_shift, input_shift, decay_in, reset_mask)

    (log_coef, b_value), gate_pull = jax.vjp(
        gate_local,
        c_value.astype(jnp.float32),
        recur_mm,
        input_mm,
        recur_bias,
        input_bias,
        decay_rate,
    )
    sent_pair = jnp.stack([log_coef.astype(jnp.bfloat16), b_value.astype(jnp.bfloat16)]).reshape(
        2, seq_count, part_len, lru_width
    )
    arrived = to_channels(sent_pair)
    coef_all = jnp.exp(arrived[0].astype(jnp.float32)) * keep_state
    state_seq = lax.associative_scan(combine, (coef_all, arrived[1].astype(jnp.float32)), axis=1)[1]
    state_back = from_channels(state_seq.astype(jnp.bfloat16)[None])
    h_value = state_back[0].reshape(row_count, lru_width).astype(jnp.float32)
    y_gelu, gelu_pull = jax.vjp(gelu_tanh, y_value)
    o_value = (h_value * y_gelu).astype(jnp.bfloat16)
    z_value = jnp.einsum("tl,dl->td", o_value, full_out, preferred_element_type=jnp.float32)
    mid_resid = flat_in + z_value
    second_norm, second_pull = jax.vjp(rms_scale, mid_resid, second_gain)
    second_low = second_norm.astype(jnp.bfloat16)
    gate_use, up_use, down_use = ffn_weights(gate_weight, up_weight, down_weight)
    g_value = jnp.dot(second_low, gate_use, preferred_element_type=jnp.float32)
    v_value = jnp.dot(second_low, up_use, preferred_element_type=jnp.float32)

    def glu_local(g_in, v_in):
        return gelu_tanh(g_in) * v_in

    hidden_full, glu_pull = jax.vjp(glu_local, g_value, v_value)
    hidden = hidden_full.astype(jnp.bfloat16)
    ffn_term = jnp.einsum("tf,df->td", hidden, down_use, preferred_element_type=jnp.float32)
    block_out = (
        (mid_resid + ffn_term).astype(jnp.bfloat16).reshape(seq_count, part_len, model_width)
    )
    out_slope = cotangent.reshape(row_count, model_width)
    slope_low = out_slope.astype(jnp.bfloat16)
    gate_use, up_use, down_use = ffn_weights(gate_weight, up_weight, down_weight)
    hidden_slope = jnp.dot(slope_low, down_use, preferred_element_type=jnp.float32)
    down_term = jnp.einsum("td,tf->df", slope_low, hidden, preferred_element_type=jnp.float32)
    g_slope, v_slope = glu_pull(hidden_slope)
    g_low = g_slope.astype(jnp.bfloat16)
    v_low = v_slope.astype(jnp.bfloat16)
    gate_term = jnp.einsum("td,tf->df", second_low, g_low, preferred_element_type=jnp.float32)
    up_term = jnp.einsum("td,tf->df", second_low, v_low, preferred_element_type=jnp.float32)
    norm_term = jnp.einsum(
        "tf,df->td", g_low, gate_use, preferred_element_type=jnp.float32
    ) + jnp.einsum("tf,df->td", v_low, up_use, preferred_element_type=jnp.float32)
    gate_grad, up_grad, down_grad = (
        lax.psum_scatter(gate_term, ("seq", "wt"), scatter_dimension=0, tiled=True),
        lax.psum_scatter(up_term, ("seq", "wt"), scatter_dimension=0, tiled=True),
        lax.psum_scatter(down_term, ("seq", "wt"), scatter_dimension=0, tiled=True),
    )
    mid_from_norm, second_gain_grad = second_pull(norm_term)
    mid_slope = out_slope + mid_from_norm
    full_in, full_branch, full_out = mixer_weights(input_weight, branch_weight, output_weight)
    z_low = mid_slope.astype(jnp.bfloat16)
    o_slope = jnp.dot(z_low, full_out, preferred_element_type=jnp.float32)
    h_low = (o_slope * y_gelu).astype(jnp.bfloat16)
    y_low = gelu_pull(o_slope * h_value)[0].astype(jnp.bfloat16)
    h_arrived = to_channels(h_low.reshape(1, seq_count, part_len, lru_width))[0].astype(jnp.float32)
    coef_next = jnp.concatenate([coef_all[:, 1:], jnp.zeros_like(coef_all[:, :1])], axis=1)
    adjoint = lax.associative_scan(combine, (coef_next, h_arrived), axis=1, reverse=True)[1]
    state_prev = jnp.concatenate([jnp.zeros_like(state_seq[:, :1]), state_seq[:, :-1]], axis=1)
    log_slope = adjoint * state_prev * coef_all
    back_pair = from_channels(
        jnp.stack([log_slope.astype(jnp.bfloat16), adjoint.astype(jnp.bfloat16)])
    )
    log_back = back_pair[0].reshape(row_count, lru_width).astype(jnp.float32)
    b_back = back_pair[1].reshape(row_count, lru_width).astype(jnp.float32)
    c_slope, recur_slope, input_slope, recur_bias_grad, input_bias_grad, decay_grad = gate_pull(
        (log_back, b_back)
    )
    recur_low = recur_slope.astype(jnp.bfloat16)
    input_low = input_slope.astype(jnp.bfloat16)
    c_total = c_slope + block_back(recur_low, recur_gate) + block_back(input_low, input_gate)
    recur_gate_grad = block_grad(c_value, recur_low, recur_gate)
    input_gate_grad = block_grad(c_value, input_low, input_gate)
    ext_slope, conv_grad = conv_pull(c_total.reshape(seq_count, part_len, lru_width))
    rim_back = from_behind(ext_slope[:, :conv_reach, :], "seq", -1)
    lead_zero = jnp.zeros((seq_count, part_len - conv_reach, lru_width), jnp.float32)
    u_slope = ext_slope[:, conv_reach:, :] + jnp.concatenate([lead_zero, rim_back], axis=1)
    u_low = u_slope.reshape(row_count, lru_width).astype(jnp.bfloat16)
    normed_slope = jnp.einsum(
        "tl,dl->td", u_low, full_in, preferred_element_type=jnp.float32
    ) + jnp.einsum("tl,dl->td", y_low, full_branch, preferred_element_type=jnp.float32)
    in_slope, mixer_gain_grad = mixer_pull(normed_slope)
    input_grad = (mid_slope + in_slope).reshape(seq_count, part_len, model_width)
    input_term = jnp.einsum("td,tl->dl", normed, u_low, preferred_element_type=jnp.float32)
    branch_term = jnp.einsum("td,tl->dl", normed, y_low, preferred_element_type=jnp.float32)
    out_term = jnp.einsum("td,tl->dl", z_low, o_value, preferred_element_type=jnp.float32)
    reduced = (
        lax.psum_scatter(mixer_gain_grad, ("seq", "wt"), scatter_dimension=0, tiled=True),
        lax.psum_scatter(input_term, ("seq", "wt"), scatter_dimension=0, tiled=True),
        lax.psum_scatter(branch_term, ("seq", "wt"), scatter_dimension=0, tiled=True),
        lax.psum_scatter(conv_grad, ("seq", "wt"), scatter_dimension=0, tiled=True),
        lax.psum_scatter(recur_gate_grad, ("seq", "wt"), scatter_dimension=0, tiled=True),
        lax.psum_scatter(input_gate_grad, ("seq", "wt"), scatter_dimension=0, tiled=True),
        lax.psum_scatter(recur_bias_grad, ("seq", "wt"), scatter_dimension=0, tiled=True),
        lax.psum_scatter(input_bias_grad, ("seq", "wt"), scatter_dimension=0, tiled=True),
        lax.psum_scatter(decay_grad, ("seq", "wt"), scatter_dimension=0, tiled=True),
        lax.psum_scatter(out_term, ("seq", "wt"), scatter_dimension=0, tiled=True),
        lax.psum_scatter(second_gain_grad, ("seq", "wt"), scatter_dimension=0, tiled=True),
    )
    return (
        block_out,
        input_grad,
        reduced[0],
        reduced[1],
        reduced[2],
        reduced[3],
        reduced[4],
        reduced[5],
        reduced[6],
        reduced[7],
        reduced[8],
        reduced[9],
        reduced[10],
        gate_grad,
        up_grad,
        down_grad,
    )


def solution(mesh):
    return jax.shard_map(
        on_device,
        mesh=mesh,
        in_specs=(
            P("wt", "seq", None),
            P("wt", "seq"),
            P(),
            P(None, "wt"),
            P(None, "wt"),
            P(),
            P(),
            P(),
            P(),
            P(),
            P(),
            P(None, "wt"),
            P(),
            P(None, "wt"),
            P(None, "wt"),
            P(None, "wt"),
            P("wt", "seq", None),
        ),
        out_specs=(
            P("wt", "seq", None),
            P("wt", "seq", None),
            P(("seq", "wt")),
            P(("seq", "wt"), None),
            P(("seq", "wt"), None),
            P(("seq", "wt"), None),
            P(("seq", "wt"), None),
            P(("seq", "wt"), None),
            P(("seq", "wt")),
            P(("seq", "wt")),
            P(("seq", "wt")),
            P(("seq", "wt"), None),
            P(("seq", "wt")),
            P(("seq", "wt"), None),
            P(("seq", "wt"), None),
            P(("seq", "wt"), None),
        ),
        check_vma=False,
    )
```

profile of v0, /device:TPU:10, one launch (start us, length us, event | category | flops | bytes accessed | tf_op | source)
XLA Modules:
  0.0 7287.7 jit_solution(12653838389027789866)
XLA Ops:
  21.1 213.7 %all-gather.7.cloned.1.call-done = bf16[2560,2560]{1,0:T(8,128)(2,1)} async-done(((bf16[2560,640]{1,0:T(8,128)(2,1)}), bf16[2560,2560]{1,0:T(8,128)(2,1)}) %all-gather.7.cloned.1.call-update) | async-done | bytes 13107216 | tf_op jit(solution)/shard_map/all_gather | solution.py:77
  279.3 16.6 all-to-all-done
  317.7 33.2 slice.659
  350.9 32.9 slice.589
  383.8 33.2 slice.588
  583.9 104.1 %all-gather.11.cloned.1.call-done = bf16[2560,2560]{1,0:T(8,128)(2,1)} async-done(((bf16[2560,640]{1,0:T(8,128)(2,1)}), bf16[2560,2560]{1,0:T(8,128)(2,1)}) %all-gather.11.cloned.1.call-update) | async-done | bytes 13107216 | tf_op jit(solution)/shard_map/all_gather | solution.py:79
  698.5 646.4 %all-gather.13.cloned.1.call-done = bf16[2560,7680]{1,0:T(8,128)(2,1)} async-done(((bf16[2560,1920]{1,0:T(8,128)(2,1)}), bf16[2560,7680]{1,0:T(8,128)(2,1)}) %all-gather.13.cloned.1.call-update) | async-done | bytes 39321616 | tf_op jit(solution)/shard_map/all_gather | solution.py:85
  1344.9 20.2 fusion.145
  1365.1 636.8 %all-gather.15.cloned.1.call-done = bf16[2560,7680]{1,0:T(8,128)(2,1)} async-done(((bf16[2560,1920]{1,0:T(8,128)(2,1)}), bf16[2560,7680]{1,0:T(8,128)(2,1)}) %all-gather.15.cloned.1.call-update) | async-done | bytes 39321616 | tf_op jit(solution)/shard_map/all_gather | solution.py:86
  2001.9 20.2 fusion.146
  2022.1 636.8 %all-gather.17.cloned.1.call-done = bf16[2560,7680]{1,0:T(8,128)(2,1)} async-done(((bf16[2560,1920]{1,0:T(8,128)(2,1)}), bf16[2560,7680]{1,0:T(8,128)(2,1)}) %all-gather.17.cloned.1.call-update) | async-done | bytes 39321616 | tf_op jit(solution)/shard_map/all_gather | solution.py:87
  2658.9 21.8 multiply_convert_fusion
  2680.7 19.5 fusion.147
  2700.2 20.4 multiply_reduce_fusion
  2734.3 15.3 reduce.16
  2797.3 33.0 slice.740
  2830.2 33.2 slice.668
  2863.4 32.9 slice.666
  3062.4 18.5 all-to-all-done.3
  3165.1 28.2 fusion.150
  3194.9 28.2 fusion.151
  3225.0 28.3 convolution_bitcast_fusion
  3253.4 76.2 %copy.521 = f32[2560,7680]{1,0:T(8,128)} copy(f32[2560,7680]{0,1:T(8,128)} %convolution_bitcast_fusion) | data formatting | bytes 157286400
  3343.8 19.6 fusion.9
  3385.2 45.5 all-reduce.57
  3438.0 87.6 %reduce-scatter.20.cloned.1.call-done = f32[80,256]{1,0:T(8,128)} async-done(((f32[2560,256]{1,0:T(8,128)}), f32[80,256]{1,0:T(8,128)}) %reduce-scatter.20.cloned.1.call-update) | async-done | bytes 81936 | tf_op jit(solution)/shard_map/reduce_scatter | solution.py:260
  3525.6 567.8 %reduce-scatter.16.cloned.1.call-done = f32[80,2560]{1,0:T(8,128)} async-done(((f32[2560,2560]{1,0:T(8,128)}), f32[80,2560]{1,0:T(8,128)}) %reduce-scatter.16.cloned.1.call-update) | async-done | bytes 819216 | tf_op jit(solution)/shard_map/reduce_scatter | solution.py:257
  4093.4 561.8 %reduce-scatter.22.cloned.1.call-done = f32[80,2560]{1,0:T(8,128)} async-done(((f32[2560,2560]{1,0:T(8,128)}), f32[80,2560]{1,0:T(8,128)}) %reduce-scatter.22.cloned.1.call-update) | async-done | bytes 819216 | tf_op jit(solution)/shard_map/reduce_scatter | solution.py:264
  4655.2 561.7 %reduce-scatter.14.cloned.1.call-done = f32[80,2560]{1,0:T(8,128)} async-done(((f32[2560,2560]{1,0:T(8,128)}), f32[80,2560]{1,0:T(8,128)}) %reduce-scatter.14.cloned.1.call-update) | async-done | bytes 819216 | tf_op jit(solution)/shard_map/reduce_scatter | solution.py:256
  5216.8 689.9 %reduce-scatter.24.cloned.1.call-done = f32[80,7680]{1,0:T(8,128)} async-done(((f32[2560,7680]{1,0:T(8,128)}), f32[80,7680]{1,0:T(8,128)}) %reduce-scatter.24.cloned.1.call-update) | async-done | bytes 2457616 | tf_op jit(solution)/shard_map/reduce_scatter | solution.py:212
  5906.7 687.1 %reduce-scatter.26.cloned.1.call-done = f32[80,7680]{1,0:T(8,128)} async-done(((f32[2560,7680]{1,0:T(8,128)}), f32[80,7680]{1,0:T(8,128)}) %reduce-scatter.26.cloned.1.call-update) | async-done | bytes 2457616 | tf_op jit(solution)/shard_map/reduce_scatter | solution.py:213
  6593.9 687.0 %reduce-scatter.30.cloned.1.call-done = f32[80,7680]{1,0:T(8,128)} async-done(((f32[2560,7680]{1,0:T(8,128)}), f32[80,7680]{1,0:T(8,128)}) %reduce-scatter.30.cloned.1.call-update) | async-done | bytes 2457616
  (664 shorter events, 614.0 us)
Async XLA Ops:
  7.2 252.4 %copy-start = (bf16[2560,256]{1,0:T(8,128)(2,1)S(1)}, bf16[2560,256]{1,0:T(8,128)(2,1)}, u32[]{:S(2)}) copy-start(bf16[2560,256]{1,0:T(8,128)(2,1)} %param.24) | copy-start | bytes 3932164
  7.2 227.6 %all-gather.7.cloned.1.call-start = ((), (), s32[]{:S(2)}) async-start(), calls=%async_computation.13 | async-start | bytes 16384000 | tf_op jit(solution)/shard_map/all_gather | solution.py:77
  7.9 567.2 %all-gather.9.cloned.1.call-start = ((), (), s32[]{:S(2)}) async-start(), calls=%async_computation.14 | async-start | bytes 16384000 | tf_op jit(solution)/shard_map/all_gather | solution.py:78
  8.7 679.3 %all-gather.11.cloned.1.call-start = ((), (), s32[]{:S(2)}) async-start(), calls=%async_computation.15 | async-start | bytes 16384000 | tf_op jit(solution)/shard_map/all_gather | solution.py:79
  9.4 1335.5 %all-gather.13.cloned.1.call-start = ((), (), s32[]{:S(2)}) async-start(), calls=%async_computation.16 | async-start | bytes 49152000 | tf_op jit(solution)/shard_map/all_gather | solution.py:85
  10.0 1991.9 %all-gather.15.cloned.1.call-start = ((), (), s32[]{:S(2)}) async-start(), calls=%async_computation.17 | async-start | bytes 49152000 | tf_op jit(solution)/shard_map/all_gather | solution.py:86
  10.6 224.2 %copy-start.48 = (f32[2560]{0:T(1024)S(1)}, f32[2560]{0:T(1024)}, u32[]{:S(2)}) copy-start(f32[2560]{0:T(1024)} %param.19) | copy-start | bytes 30724
  10.6 2648.2 %all-gather.17.cloned.1.call-start = ((), (), s32[]{:S(2)}) async-start(), calls=%async_computation.18 | async-start | bytes 49152000 | tf_op jit(solution)/shard_map/all_gather | solution.py:87
  20.9 220.6 %copy-start.87 = (f32[128]{0:T(128)}, f32[128]{0:T(128)S(1)}, u32[]{:S(2)}) copy-start(f32[128]{0:T(128)S(1)} %fusion.105) | copy-start | bytes 1540
  21.0 246.8 %copy-start.103 = (pred[128]{0:T(512)(128)(4,1)}, pred[128]{0:T(512)(128)(4,1)S(1)}, u32[]{:S(2)}) copy-start(pred[128]{0:T(512)(128)(4,1)S(1)} %get-tuple-element.222) | copy-start | bytes 388
  21.0 246.7 %copy-start.106 = (f32[128]{0:T(128)}, f32[128]{0:T(128)S(1)}, u32[]{:S(2)}) copy-start(f32[128]{0:T(128)S(1)} %get-tuple-element.227) | copy-start | bytes 1540
  21.1 246.7 %copy-start.108 = (f32[128]{0:T(128)}, f32[128]{0:T(128)S(1)}, u32[]{:S(2)}) copy-start(f32[128]{0:T(128)S(1)} %get-tuple-element.228) | copy-start | bytes 1540
  21.1 246.7 %copy-start.110 = (f32[128]{0:T(128)}, f32[128]{0:T(128)S(1)}, u32[]{:S(2)}) copy-start(f32[128]{0:T(128)S(1)} %get-tuple-element.229) | copy-start | bytes 1540
  21.1 246.7 %copy-start.112 = (f32[128]{0:T(128)}, f32[128]{0:T(128)S(1)}, u32[]{:S(2)}) copy-start(f32[128]{0:T(128)S(1)} %get-tuple-element.230) | copy-start | bytes 1540
  21.1 246.7 %copy-start.60 = (f32[2560]{0:T(1024)}, f32[2560]{0:T(1024)S(1)}, u32[]{:S(2)}) copy-start(f32[2560]{0:T(1024)S(1)} %fusion.96) | copy-start | bytes 30724
  21.1 222.3 %copy-start.96 = (f32[2560,4]{0,1:T(4,128)S(1)}, f32[2560,4]{0,1:T(4,128)}, u32[]{:S(2)}) copy-start(f32[2560,4]{0,1:T(4,128)} %param.22) | copy-start | bytes 122884
  241.5 5.1 collective-permute-start
  274.7 21.2 all-to-all-start
  697.3 2023.3 %copy-start.6 = (f32[128,2560]{1,0:T(8,128)}, f32[128,2560]{1,0:T(8,128)S(1)}, u32[]{:S(2)}) copy-start(f32[128,2560]{1,0:T(8,128)S(1)} %get-tuple-element.234) | copy-start | bytes 3932164
  2752.2 41.7 all-to-all-start.2
  3056.8 24.1 all-to-all-start.3
  3061.2 375.3 %reduce-scatter.28.cloned.1.call-start = ((), (), s32[]{:S(2)}) async-start(), calls=%async_computation.26 | async-start | bytes 1351680
  3118.0 320.0 %reduce-scatter.18.cloned.1.call-start = ((), (), s32[]{:S(2)}) async-start(), calls=%async_computation.21 | async-start | bytes 2703360 | tf_op jit(solution)/shard_map/reduce_scatter | solution.py:259
  3120.1 405.5 %reduce-scatter.20.cloned.1.call-start = ((), (), s32[]{:S(2)}) async-start(), calls=%async_computation.22 | async-start | bytes 2703360 | tf_op jit(solution)/shard_map/reduce_scatter | solution.py:260
  3123.2 970.2 %reduce-scatter.16.cloned.1.call-start = ((), (), s32[]{:S(2)}) async-start(), calls=%async_computation.20 | async-start | bytes 27033600 | tf_op jit(solution)/shard_map/reduce_scatter | solution.py:257
  3134.8 1520.3 %reduce-scatter.22.cloned.1.call-start = ((), (), s32[]{:S(2)}) async-start(), calls=%async_computation.23 | async-start | bytes 27033600 | tf_op jit(solution)/shard_map/reduce_scatter | solution.py:264
  3147.0 2069.8 %reduce-scatter.14.cloned.1.call-start = ((), (), s32[]{:S(2)}) async-start(), calls=%async_computation.19 | async-start | bytes 27033600 | tf_op jit(solution)/shard_map/reduce_scatter | solution.py:256
  3149.0 3.6 collective-permute-start.1
  3163.4 2743.4 %reduce-scatter.24.cloned.1.call-start = ((), (), s32[]{:S(2)}) async-start(), calls=%async_computation.24 | async-start | bytes 81100800 | tf_op jit(solution)/shard_map/reduce_scatter | solution.py:212
  3193.4 3400.5 %reduce-scatter.26.cloned.1.call-start = ((), (), s32[]{:S(2)}) async-start(), calls=%async_computation.25 | async-start | bytes 81100800 | tf_op jit(solution)/shard_map/reduce_scatter | solution.py:213
  3223.2 4057.7 %reduce-scatter.30.cloned.1.call-start = ((), (), s32[]{:S(2)}) async-start(), calls=%async_computation.27 | async-start | bytes 81100800
  3433.7 3847.2 %copy-start.1 = (bf16[2560,256]{1,0:T(8,128)(2,1)S(1)}, bf16[2560,256]{1,0:T(8,128)(2,1)}, u32[]{:S(2)}) copy-start(bf16[2560,256]{1,0:T(8,128)(2,1)} %param.24) | copy-start | bytes 3932164
  (118 other events, 740.5 us)
Sparse Core Ops, SparseCore 0:
  9.6 225.1 all-gather.6
  236.4 224.9 all-gather.8
  463.0 224.9 all-gather.10
  689.4 655.4 all-gather.12
  1346.4 655.4 all-gather.14
  2003.4 655.4 all-gather.16
  3118.1 124.8 reduce-scatter.27
  3245.9 137.9 reduce-scatter.17
  3386.8 138.7 reduce-scatter.19
  3528.4 564.8 reduce-scatter.15
  4096.4 558.7 reduce-scatter.21
  4658.0 558.7 reduce-scatter.13
  5225.0 681.7 reduce-scatter.23
  5914.7 679.0 reduce-scatter.25
  6601.8 679.0 reduce-scatter.29
where the time goes:
time: 7310 us; the launch traced here: 7290 us
  waiting for transfers between devices  6120 us (84%)
  local copies, waits for them, and re-layouts  634 us (9%)
  matrix products  305 us (4%)
  other arithmetic  122 us (2%)
    unnamed x17, waiting for transfers between devices  691 us
    reduce_scatter x1, waiting for transfers between devices, on_device(): lax.psum_scatter(gate_term, ('seq', 'wt'), scatter_dimension=0, tiled=True)  690 us
    reduce_scatter x1, waiting for transfers between devices, on_device(): lax.psum_scatter(up_term, ('seq', 'wt'), scatter_dimension=0, tiled=True)  687 us
    all_gather x1, waiting for transfers between devices, ffn_weights(): lax.all_gather(gate_weight, 'wt', axis=1, tiled=True)  646 us
    all_gather x1, waiting for transfers between devices, ffn_weights(): lax.all_gather(up_weight, 'wt', axis=1, tiled=True)  637 us
    all_gather x1, waiting for transfers between devices, ffn_weights(): lax.all_gather(down_weight, 'wt', axis=1, tiled=True)  637 us
    reduce_scatter x1, waiting for transfers between devices, on_device(): lax.psum_scatter(branch_term, ('seq', 'wt'), scatter_dimension=0, tiled=T...  568 us
    reduce_scatter x1, waiting for transfers between devices, on_device(): lax.psum_scatter(out_term, ('seq', 'wt'), scatter_dimension=0, tiled=True)  562 us
  transfers between devices with their start and end apart: 20, of which 16 were waited for; matrix products, arithmetic and copies ran while one was open for 9% of the time, Pallas kernels for 0%

commit v1 on v0

v1 whole, which is shorter than its diff:
```python
import jax
import jax.numpy as jnp
from jax import lax
from jax.experimental import pallas as pl
from jax.experimental.pallas import tpu as pltpu
from jax.sharding import Mesh
from jax.sharding import PartitionSpec as P

EPSILON = 1e-06
LOW = jnp.bfloat16
FULL = jnp.float32


def dot(left, right, left_dim=1, right_dim=0):
    return lax.dot_general(
        left, right, (((left_dim,), (right_dim,)), ((), ())), preferred_element_type=FULL
    )


def gelu_both(values):
    slope = jnp.sqrt(2.0 / jnp.pi).astype(FULL)
    inner = jnp.tanh(slope * (values + 0.044715 * values * values * values))
    gelu = 0.5 * values * (1.0 + inner)
    grad = 0.5 * (1.0 + inner) + 0.5 * values * (1.0 - inner * inner) * slope * (
        1.0 + 3.0 * 0.044715 * values * values
    )
    return gelu, grad


def shard_weight(weight, shards, inner):
    rows, width = weight.shape
    part = rows // (shards * inner)
    me = lax.axis_index("si") * inner + lax.axis_index("sj")
    mine = lax.dynamic_slice_in_dim(weight, me * part, part, 0)
    every = lax.all_gather(mine, "wt", axis=0)
    here = lax.all_to_all(every, "si", split_axis=0, concat_axis=0, tiled=True)
    both = lax.all_gather(here, "sj", axis=1)
    return both.reshape(rows, width)


def head_rows(gate_rows, shards):
    head = gate_rows.shape[1]
    width = gate_rows.shape[0] // shards
    heads = -(-width // head)
    first = (lax.axis_index("si") * width) // head
    table = gate_rows.reshape(-1, head, head)
    return lax.dynamic_slice_in_dim(table, first, heads, 0)


def edge_swap(values, edge):
    me = lax.axis_index("si")
    shards = lax.axis_size("si")
    odd = me % 2 == 1
    mine = jnp.where(odd, values[:, :edge], values[:, -edge:])
    other = lax.ppermute(mine, "si", [(i, i ^ 1) for i in range(shards)])
    return jnp.where(
        odd,
        jnp.concatenate([other, values], axis=1),
        jnp.concatenate([values, other], axis=1),
    )


def own_part(values, edge):
    odd = lax.axis_index("si") % 2 == 1
    return jnp.where(odd, values[:, edge:], values[:, :-edge])


def heads_dot(values, table, transposed=False):
    heads, head, _ = table.shape
    return jnp.concatenate(
        [
            dot(values[:, n * head : (n + 1) * head], table[n], 1, 1 if transposed else 0)
            for n in range(heads)
        ],
        axis=1,
    )


def heads_grad(values, slopes, head):
    return jnp.concatenate(
        [
            dot(values[:, n * head : (n + 1) * head], slopes[:, n * head : (n + 1) * head], 0, 0)
            for n in range(values.shape[1] // head)
        ],
        axis=0,
    )


def scan_rows(coef, value, reverse):
    rows = coef.shape[0]
    place = lax.broadcasted_iota(jnp.int32, coef.shape, 0)
    step = 1
    while step < rows:
        if reverse:
            inside = place < rows - step
            by = rows - step
        else:
            inside = place >= step
            by = step
        far_coef = jnp.where(inside, pltpu.roll(coef, by, 0), 1.0)
        far_value = jnp.where(inside, pltpu.roll(value, by, 0), 0.0)
        value = coef * far_value + value
        coef = coef * far_coef
        step *= 2
    return coef, value


def gates_kernel(odd, c_ref, c_own, table_r, table_i, rows_ref, mask_ref, r_ref, ii_ref, a_ref, h_ref):
    c_head = c_ref[...]
    ra = jnp.dot(c_head, table_r[0], preferred_element_type=FULL)
    ia = jnp.dot(c_head, table_i[0], preferred_element_type=FULL)
    r = jax.nn.sigmoid(ra + rows_ref[0:1, :])
    ii = jax.nn.sigmoid(ia + rows_ref[1:2, :])
    keep = mask_ref[:, 0:1]
    log_a = rows_ref[2:3, :] * r
    decay = jnp.exp(2.0 * log_a)
    gap = jnp.where(2.0 * log_a > -0.01, -expm1_small(2.0 * log_a), 1.0 - decay)
    mult = jnp.where(keep == 0.0, 1.0, jnp.sqrt(gap))
    b = (mult * c_own[...].astype(FULL) * ii).astype(LOW).astype(FULL)
    a = jnp.exp(log_a.astype(LOW).astype(FULL)) * keep
    cum_a, h_loc = scan_rows(a, b, False)
    r_ref[...] = r
    ii_ref[...] = ii
    a_ref[...] = cum_a
    h_ref[...] = h_loc


def expm1_small(values):
    return values * (
        1.0 + values * (0.5 + values * (1.0 / 6.0 + values * (1.0 / 24.0 + values / 120.0)))
    )


def gates_scan(c_ext, table_r, table_i, rows8, mask, odd, part_len, width):
    rows = c_ext.shape[0]
    head = table_r.shape[1]
    half = 128
    per = head // half
    grid = (rows // part_len, width // half)
    spec = pltpu.PrefetchScalarGridSpec(
        num_scalar_prefetch=1,
        grid=grid,
        in_specs=[
            pl.BlockSpec((part_len, head), lambda m, n, s: (m, (n + s[0]) // per)),
            pl.BlockSpec((part_len, half), lambda m, n, s: (m, n + s[0])),
            pl.BlockSpec((1, head, half), lambda m, n, s: ((n + s[0]) // per, 0, (n + s[0]) % per)),
            pl.BlockSpec((1, head, half), lambda m, n, s: ((n + s[0]) // per, 0, (n + s[0]) % per)),
            pl.BlockSpec((8, half), lambda m, n, s: (0, n)),
            pl.BlockSpec((part_len, mask.shape[1]), lambda m, n, s: (m, 0)),
        ],
        out_specs=[pl.BlockSpec((part_len, half), lambda m, n, s: (m, n))] * 4,
    )
    return pl.pallas_call(
        gates_kernel,
        grid_spec=spec,
        out_shape=[jax.ShapeDtypeStruct((rows, width), FULL)] * 4,
    )(odd, c_ext, c_ext, table_r, table_i, rows8, mask)


def back_kernel(dh_ref, a_ref, rem_ref, e_ref):
    rows = dh_ref.shape[0]
    place = lax.broadcasted_iota(jnp.int32, dh_ref.shape, 0)
    a_next = jnp.where(place < rows - 1, pltpu.roll(a_ref[...], rows - 1, 0), 1.0)
    rem, e_loc = scan_rows(a_next, dh_ref[...].astype(FULL), True)
    rem_ref[...] = rem
    e_ref[...] = e_loc


def back_scan(dh, a, part_len):
    rows, width = a.shape
    half = 128
    block = pl.BlockSpec((part_len, half), lambda m, n: (m, n))
    return pl.pallas_call(
        back_kernel,
        grid=(rows // part_len, width // half),
        in_specs=[block, block],
        out_specs=[block, block],
        out_shape=[jax.ShapeDtypeStruct((rows, width), FULL)] * 2,
    )(dh, a)


def on_device(
    inputs,
    segment,
    mixer_gain,
    input_weight,
    branch_weight,
    conv_weight,
    recur_gate,
    input_gate,
    recur_bias,
    input_bias,
    decay_rate,
    output_weight,
    second_gain,
    gate_weight,
    up_weight,
    down_weight,
    cotangent,
):
    shards = lax.axis_size("si")
    inner = lax.axis_size("sj")
    me_i = lax.axis_index("si")
    me_j = lax.axis_index("sj")
    part_len, model = inputs.shape[1:]
    lru = conv_weight.shape[0]
    taps = conv_weight.shape[1]
    width = lru // shards
    head = recur_gate.shape[1]
    edge = width % head
    rows = shards * part_len

    def mine(vector):
        return lax.dynamic_slice_in_dim(vector, me_i * width, width, 0)

    doc_all = lax.all_gather(segment[0], ("si", "sj"), axis=0, tiled=True)
    length = doc_all.shape[0]
    same_all = jnp.stack(
        [
            jnp.concatenate([jnp.full((k,), -1, jnp.int32), doc_all[: length - k]]) == doc_all
            for k in range(taps)
        ],
        axis=-1,
    ).astype(FULL)

    def chunks_of(j):
        cut = same_all.reshape(shards, inner, part_len, taps)
        return lax.dynamic_index_in_dim(cut, j, 1, keepdims=False)

    same = chunks_of(me_j)
    keep = same[:, :, 1].reshape(rows, 1)
    reset = keep == 0.0

    flat = inputs[0].astype(FULL)
    scale1 = lax.rsqrt(jnp.mean(flat * flat, axis=-1, keepdims=True) + EPSILON)
    normed = (flat * scale1 * mixer_gain).astype(LOW)
    win = shard_weight(input_weight, shards, inner)
    wbr = shard_weight(branch_weight, shards, inner)
    wout = shard_weight(output_weight, shards, inner)
    xn = lax.all_gather(normed, "si", axis=0, tiled=True)
    slope = cotangent[0]
    dm_all = lax.all_gather(slope.astype(LOW), "wt", axis=0, tiled=True)

    u = dot(xn, win).astype(LOW)
    y = dot(xn, wbr)
    u3 = u.reshape(shards, part_len, width)
    tail = u3[:, part_len - (taps - 1) :, :]
    before = lax.ppermute(tail, "sj", [(j, (j + 1) % inner) for j in range(inner)])
    shifted = jnp.concatenate([jnp.zeros_like(before[:1]), before[:-1]], axis=0)
    before = jnp.where(me_j == 0, shifted, before)
    extended = jnp.concatenate([before, u3], axis=1).astype(FULL)
    conv_mine = mine(conv_weight)
    windows = [
        extended[:, taps - 1 - k : taps - 1 - k + part_len, :] * same[:, :, k : k + 1]
        for k in range(taps)
    ]
    conv = sum(windows[k] * conv_mine[:, k] for k in range(taps))
    c_low = conv.reshape(rows, width).astype(LOW)
    c_ext = edge_swap(c_low, edge)
    recur_table = head_rows(recur_gate, shards)
    input_table = head_rows(input_gate, shards)
    c = c_low.astype(FULL)
    rate = mine(decay_rate)
    soft = -8.0 * jax.nn.softplus(rate)
    odd = (me_i % 2).astype(jnp.int32).reshape(1) * (edge // 128)
    rows8 = jnp.concatenate(
        [jnp.stack([mine(recur_bias), mine(input_bias), soft]), jnp.zeros((5, width), FULL)]
    )
    r, ii, cum_a, h_loc = gates_scan(
        c_ext, recur_table, input_table, rows8, keep, odd, part_len, width
    )
    log_a = soft * r
    mult = jnp.where(reset, 1.0, jnp.sqrt(-jnp.expm1(2.0 * log_a)))
    a = jnp.exp(log_a.astype(LOW).astype(FULL)) * keep
    a3 = a.reshape(shards, part_len, width)
    cum_a = cum_a.reshape(a3.shape)
    h_loc = h_loc.reshape(a3.shape)
    ends = lax.all_gather(jnp.stack([cum_a[:, -1], h_loc[:, -1]]), "sj", axis=2)
    ends = ends.reshape(2, shards * inner, width)
    carry = jnp.zeros((width,), FULL)
    starts = []
    for n in range(shards * inner):
        starts.append(carry)
        carry = ends[0, n] * carry + ends[1, n]
    h_in = lax.dynamic_index_in_dim(
        jnp.stack(starts).reshape(shards, inner, width), me_j, 1, keepdims=True
    )
    h = h_loc + cum_a * h_in
    h_prev = jnp.concatenate([h_in, h[:, :-1]], axis=1).reshape(rows, width)
    hr = h.reshape(rows, width).astype(LOW).astype(FULL)
    gelu_y, grad_y = gelu_both(y)
    o = (hr * gelu_y).astype(LOW)
    z_part = dot(o, wout, 1, 1).astype(LOW)
    z = lax.psum_scatter(z_part, "si", scatter_dimension=0, tiled=True)
    x1 = flat + z.astype(FULL)
    scale2 = lax.rsqrt(jnp.mean(x1 * x1, axis=-1, keepdims=True) + EPSILON)
    xn2 = lax.all_gather((x1 * scale2 * second_gain).astype(LOW), "wt", axis=0, tiled=True)

    g = dot(xn2, gate_weight)
    v = dot(xn2, up_weight)
    gelu_g, grad_g = gelu_both(g)
    hidden = (gelu_g * v).astype(LOW)
    ffn_part = dot(hidden, down_weight, 1, 1).astype(LOW)
    ffn = lax.psum_scatter(ffn_part, "wt", scatter_dimension=0, tiled=True)
    block_out = (x1 + ffn.astype(FULL)).astype(LOW)[None]
    dhidden = dot(dm_all, down_weight)
    dg = (dhidden * v * grad_g).astype(LOW)
    dv = (dhidden * gelu_g).astype(LOW)
    dxn2_part = (dot(dg, gate_weight, 1, 1) + dot(dv, up_weight, 1, 1)).astype(LOW)
    dxn2 = lax.psum_scatter(dxn2_part, "wt", scatter_dimension=0, tiled=True).astype(FULL)

    def ffn_reduce(term):
        kept = lax.psum_scatter(term.astype(LOW), ("si", "sj"), scatter_dimension=0, tiled=True)
        wide = lax.all_to_all(kept, "wt", split_axis=0, concat_axis=1, tiled=True)
        return wide.astype(FULL)

    down_grad = ffn_reduce(dot(dm_all, hidden, 0, 0))
    gate_grad = ffn_reduce(dot(xn2, dg, 0, 0))
    up_grad = ffn_reduce(dot(xn2, dv, 0, 0))

    q2 = dxn2 * second_gain
    dx1 = slope + scale2 * (q2 - x1 * scale2 * scale2 * jnp.mean(q2 * x1, axis=-1, keepdims=True))
    second_gain_grad = jnp.sum(dxn2 * x1 * scale2, axis=0)
    dz = lax.all_gather(dx1.astype(LOW), "si", axis=0, tiled=True)
    do = dot(dz, wout)

    def mixer_reduce(term):
        cut = term.astype(LOW).reshape(shards, inner * shards, -1, width).transpose(1, 0, 2, 3)
        kept = lax.psum_scatter(cut, ("sj", "wt"), scatter_dimension=0, tiled=False)
        wide = lax.all_to_all(kept, "si", split_axis=0, concat_axis=2, tiled=True)
        return wide[0].astype(FULL)

    out_grad = mixer_reduce(dot(dz, o, 0, 0))
    dh = (do * gelu_y).astype(LOW)
    dy = (do * hr * grad_y).astype(LOW)
    branch_grad = mixer_reduce(dot(xn, dy, 0, 0))

    rem, e_loc = back_scan(dh, a, part_len)
    rem = rem.reshape(a3.shape)
    e_loc = e_loc.reshape(a3.shape)
    heads_out = jnp.stack([cum_a[:, -1], a3[:, 0] * e_loc[:, 0]])
    firsts = lax.all_gather(heads_out, "sj", axis=2).reshape(2, shards * inner, width)
    carry = jnp.zeros((width,), FULL)
    nexts = []
    for n in reversed(range(shards * inner)):
        nexts.append(carry)
        carry = firsts[0, n] * carry + firsts[1, n]
    e_in = lax.dynamic_index_in_dim(
        jnp.stack(nexts[::-1]).reshape(shards, inner, width), me_j, 1, keepdims=True
    )
    e = (e_loc + rem * e_in).reshape(rows, width)
    dla = (e * h_prev * a).astype(LOW).astype(FULL)
    dbr = e.astype(LOW).astype(FULL)
    dmult = jnp.where(reset, 0.0, -jnp.exp(2.0 * log_a) / mult)
    dlog_a = dla + dbr * c * ii * dmult
    dra_f = soft * dlog_a * r * (1.0 - r)
    dia_f = dbr * mult * c * ii * (1.0 - ii)
    recur_bias_grad = jnp.sum(dra_f, axis=0)
    input_bias_grad = jnp.sum(dia_f, axis=0)
    decay_grad = jnp.sum(-8.0 * dlog_a * r, axis=0) * jax.nn.sigmoid(rate)
    slopes = jnp.concatenate([dra_f.astype(LOW), dia_f.astype(LOW)], axis=0)
    slopes = edge_swap(slopes, edge)
    dra, dia = slopes[:rows], slopes[rows:]
    recur_gate_grad = heads_grad(c_ext, dra, head)
    input_gate_grad = heads_grad(c_ext, dia, head)
    mixed = heads_dot(dra, recur_table, True) + heads_dot(dia, input_table, True)
    dc = (dbr * mult * ii + own_part(mixed, edge)).reshape(shards, part_len, width)
    conv_grad = jnp.stack([jnp.sum(windows[k] * dc, axis=(0, 1)) for k in range(taps)], axis=-1)
    lead = lax.ppermute(dc[:, : taps - 1], "sj", [(j, (j - 1) % inner) for j in range(inner)])
    moved = jnp.concatenate([lead[1:], jnp.zeros_like(lead[:1])], axis=0)
    lead = jnp.where(me_j == inner - 1, moved, lead)
    next_j = (me_j + 1) % inner
    same_next = chunks_of(next_j)[:, : taps - 1]
    shifted = jnp.concatenate([same_next[1:], jnp.zeros_like(same_next[:1])], axis=0)
    same_next = jnp.where(me_j == inner - 1, shifted, same_next)
    dc_ext = jnp.concatenate([dc, lead], axis=1)
    same_ext = jnp.concatenate([same, same_next], axis=1)
    du = sum(
        (dc_ext * same_ext[:, :, k : k + 1])[:, k : k + part_len] * conv_mine[:, k]
        for k in range(taps)
    )
    du = du.reshape(rows, width).astype(LOW)
    dxn_part = (dot(du, win, 1, 1) + dot(dy, wbr, 1, 1)).astype(LOW)
    dxn = lax.psum_scatter(dxn_part, "si", scatter_dimension=0, tiled=True).astype(FULL)
    input_weight_grad = mixer_reduce(dot(xn, du, 0, 0))
    q1 = dxn * mixer_gain
    input_grad = dx1 + scale1 * (
        q1 - flat * scale1 * scale1 * jnp.mean(q1 * flat, axis=-1, keepdims=True)
    )
    mixer_gain_grad = jnp.sum(dxn * flat * scale1, axis=0)

    small = jnp.concatenate(
        [
            own_part(recur_gate_grad.T, edge).T,
            own_part(input_gate_grad.T, edge).T,
            conv_grad,
            recur_bias_grad[:, None],
            input_bias_grad[:, None],
            decay_grad[:, None],
        ],
        axis=1,
    )
    small = lax.psum_scatter(small, ("sj", "wt"), scatter_dimension=0, tiled=True)
    gains = jnp.stack([mixer_gain_grad, second_gain_grad], axis=1)
    gains = lax.psum_scatter(gains, ("si", "sj", "wt"), scatter_dimension=0, tiled=True)
    at = 2 * head + taps
    return (
        block_out,
        input_grad[None],
        gains[:, 0],
        input_weight_grad,
        branch_grad,
        small[:, 2 * head : at],
        small[:, :head],
        small[:, head : 2 * head],
        small[:, at],
        small[:, at + 1],
        small[:, at + 2],
        out_grad,
        gains[:, 1],
        gate_grad,
        up_grad,
        down_grad,
    )


def solution(mesh):
    shards = mesh.shape["wt"]
    inner = mesh.shape["seq"] // shards
    cut = Mesh(mesh.devices.reshape(shards, inner, shards), ("si", "sj", "wt"))
    seq = ("si", "sj")
    tokens = P("wt", seq, None)
    columns = P(None, "wt")
    row = P(("si", "sj", "wt"))
    flat_rows = P(("si", "sj", "wt"), None)
    return jax.shard_map(
        on_device,
        mesh=cut,
        in_specs=(
            tokens,
            P("wt", seq),
            P(),
            columns,
            columns,
            P(),
            P(),
            P(),
            P(),
            P(),
            P(),
            columns,
            P(),
            columns,
            columns,
            columns,
            tokens,
        ),
        out_specs=(
            tokens,
            tokens,
            row,
            flat_rows,
            flat_rows,
            flat_rows,
            flat_rows,
            flat_rows,
            row,
            row,
            row,
            flat_rows,
            row,
            flat_rows,
            flat_rows,
            flat_rows,
        ),
        check_vma=False,
    )
```

time: 7310 us -> 1380 us (0.19)
  waiting for transfers between devices: 6120 us -> 925 us
  local copies, waits for them, and re-layouts: 634 us -> 70.1 us
  matrix products: 305 us -> 147 us
  other arithmetic: 122 us -> 36.4 us
    reduce_scatter x7 -> x8, waiting for transfers between devices: 3160 us -> 466 us  [the longest x3 210 us: ffn_reduce(): lax.psum_scatter(term.astype(LOW), ('si', 'sj'), scatter_dimension=0, til...]
    all_gather x6 -> x10, waiting for transfers between devices: 2240 us -> 204 us  [the longest x3 62.8 us: shard_weight(): every = lax.all_gather(mine, 'wt', axis=0)]
    unnamed x17 -> x22, waiting for transfers between devices: 691 us -> 246 us
    slice x129 -> x18, local copies, waits for them, and re-layouts: 411 us -> 7.09 us  [the longest x2 1.79 us: on_device(): ends = lax.all_gather(jnp.stack([cum_a[:, -1], h_loc[:, -1]]), 'sj', axis=2)]
    dot_general x24 -> x30, matrix products: 305 us -> 147 us  [dot(): lax.dot_general(left, right, (((left_dim,), (right_dim,)), ((), ())), pre...]
    unnamed x282 -> x109, local copies, waits for them, and re-layouts: 121 us -> 30 us
  transfers between devices with their start and end apart: 20 -> 30, of which waited for: 16 -> 22; matrix products, arithmetic and copies ran while one was open for 9% -> 13% of each run, Pallas kernels for 0% -> 1%
where the time goes in v1:
time: 1380 us; the launch traced here: 1350 us
  waiting for transfers between devices  925 us (67%)
  matrix products  147 us (11%)
  blocking collectives  90.8 us (7%)
  local copies, waits for them, and re-layouts  70.1 us (5%)
  starting transfers between devices  41.4 us (3%)
  other arithmetic  36.4 us (3%)
  Pallas kernels  26.4 us (2%)
  between operations  15.7 us (1%)
    unnamed x22, waiting for transfers between devices  246 us
    reduce_scatter x3, waiting for transfers between devices, ffn_reduce(): lax.psum_scatter(term.astype(LOW), ('si', 'sj'), scatter_dimension=0, til...  210 us
    dot_general x30, matrix products, dot(): lax.dot_general(left, right, (((left_dim,), (right_dim,)), ((), ())), pre...  147 us
    reduce_scatter x1, waiting for transfers between devices, on_device(): ffn = lax.psum_scatter(ffn_part, 'wt', scatter_dimension=0, tiled=True)  71.4 us
    all_gather x3, waiting for transfers between devices, shard_weight(): every = lax.all_gather(mine, 'wt', axis=0)  62.8 us
    reduce_scatter x1, waiting for transfers between devices, on_device(): lax.psum_scatter(small, ('sj', 'wt'), scatter_dimension=0, tiled=True)  59.8 us
    reduce_scatter x1, waiting for transfers between devices, on_device(): lax.psum_scatter(dxn2_part, 'wt', scatter_dimension=0, tiled=True)  52 us
    all_gather x1, waiting for transfers between devices, on_device(): lax.all_gather((x1 * scale2 * second_gain).astype(LOW), 'wt', axis=0, til...  50.6 us
  transfers between devices with their start and end apart: 30, of which 22 were waited for; matrix products, arithmetic and copies ran while one was open for 13% of the time, Pallas kernels for 1%

profile of v1, /device:TPU:10, one launch (start us, length us, event | category | flops | bytes accessed | tf_op | source)
XLA Modules:
  0.0 1353.7 jit_solution(15932452060690534476)
XLA Ops:
  15.2 33.3 %all-gather.28.cloned.1.call-done = bf16[1280,640]{1,0:T(8,128)(2,1)} async-done(((bf16[320,640]{1,0:T(8,128)(2,1)}), bf16[1280,640]{1,0:T(8,128)(2,1)}) %all-gather.28.cloned.1.call-update) | async-done | bytes 1638416 | tf_op jit(solution)/shard_map/all_gather | solution.py:35
  48.4 24.4 %all_to_all.81 = bf16[4,320,640]{2,1,0:T(8,128)(2,1)} all-to-all(bf16[4,320,640]{2,1,0:T(8,128)(2,1)} %bitcast.431), channel_id=1, replica_groups=mesh['si'=4,'sj'=2,'wt'=4] {'si'}, dimensions={0} | all-to-all | bytes 3276800 | tf_op jit(solution)/shard_map/all_to_all | solution.py:36
  72.9 14.8 %all-gather.32.cloned.1.call-done = bf16[1280,640]{1,0:T(8,128)(2,1)} async-done(((bf16[320,640]{1,0:T(8,128)(2,1)}), bf16[1280,640]{1,0:T(8,128)(2,1)}) %all-gather.32.cloned.1.call-update) | async-done | bytes 1638416 | tf_op jit(solution)/shard_map/all_gather | solution.py:35
  87.6 24.4 %all_to_all.82 = bf16[4,320,640]{2,1,0:T(8,128)(2,1)} all-to-all(bf16[4,320,640]{2,1,0:T(8,128)(2,1)} %bitcast.430), channel_id=1, replica_groups=mesh['si'=4,'sj'=2,'wt'=4] {'si'}, dimensions={0} | all-to-all | bytes 3276800 | tf_op jit(solution)/shard_map/all_to_all | solution.py:36
  112.0 14.8 %all-gather.36.cloned.1.call-done = bf16[1280,640]{1,0:T(8,128)(2,1)} async-done(((bf16[320,640]{1,0:T(8,128)(2,1)}), bf16[1280,640]{1,0:T(8,128)(2,1)}) %all-gather.36.cloned.1.call-update) | async-done | bytes 1638416 | tf_op jit(solution)/shard_map/all_gather | solution.py:35
  131.2 29.3 %all-gather.2 = s32[1,1024]{1,0:T(1,128)S(1)} all-gather(s32[1,128]{1,0:T(1,128)S(1)} %copy-done.34), channel_id=4, replica_groups=mesh['si'=4,'sj'=2,'wt'=4] {'si','sj'}, dimensions={1}, use_global_device_ids=true | all-gather | bytes 4608 | tf_op jit(solution)/shard_map/all_gather | solution.py:216
  166.3 12.7 all-gather.20.cloned.1.call-done
  179.0 14.0 %all-gather.30.cloned.1.call-done = bf16[4,640,640]{2,1,0:T(8,128)(2,1)} async-done(((bf16[4,320,640]{2,1,0:T(8,128)(2,1)}), bf16[4,640,640]{2,1,0:T(8,128)(2,1)}) %all-gather.30.cloned.1.call-update) | async-done | bytes 3276816 | tf_op jit(solution)/shard_map/all_gather | solution.py:37
  215.1 14.9 %shard_map.288 = (f32[512,640]{1,0:T(8,128)}, f32[512,640]{1,0:T(8,128)}, f32[512,640]{1,0:T(8,128)}, f32[512,640]{1,0:T(8,128)}) custom-call(s32[1]{0:T(128)} %bitcast.1.odd, bf16[512,768]{1,0:T(8,128)(2,1)} %maximum_select_fusion.1.c_ref.c_own, bf16[512,768]{1,0:T(8,128)(2,1)} %maximum_select_fusion.1.c_ref.c_own, ...), custom_call_target="tpu_custom_call" | custom-call | tf_op jit(solution)/shard_map/pallas_call | solution.py:153
  242.1 40.5 %reduce-scatter.23.cloned.1.call-done = bf16[128,2560]{1,0:T(8,128)(2,1)} async-done(((bf16[512,2560]{1,0:T(8,128)(2,1)}), bf16[128,2560]{1,0:T(8,128)(2,1)}) %reduce-scatter.23.cloned.1.call-update) | async-done | bytes 655376 | tf_op jit(solution)/shard_map/reduce_scatter | solution.py:294
  287.8 50.6 %all-gather.22.cloned.1.call-done = bf16[512,2560]{1,0:T(8,128)(2,1)} async-done(((bf16[128,2560]{1,0:T(8,128)(2,1)}), bf16[512,2560]{1,0:T(8,128)(2,1)}) %all-gather.22.cloned.1.call-update) | async-done | bytes 2621456 | tf_op jit(solution)/shard_map/all_gather | solution.py:297
  338.4 11.4 fusion.162
  349.8 10.3 fusion.163
  360.1 33.9 %all-gather.24.cloned.1.call-done = bf16[512,2560]{1,0:T(8,128)(2,1)} async-done(((bf16[128,2560]{1,0:T(8,128)(2,1)}), bf16[512,2560]{1,0:T(8,128)(2,1)}) %all-gather.24.cloned.1.call-update) | async-done | bytes 2621456 | tf_op jit(solution)/shard_map/all_gather | solution.py:242
  394.1 14.7 %multiply_convert_fusion = (bf16[512,1920]{1,0:T(8,128)(2,1)S(1)}, bf16[512,1920]{1,0:T(8,128)(2,1)S(1)}, bf16[512,1920]{1,0:T(8,128)(2,1)}) fusion(f32[512,1920]{1,0:T(8,128)} %fusion.162, f32[512,1920]{1,0:T(8,128)} %fusion.163, bf16[512,2560]{1,0:T(8,128)(2,1)} %all-gather.24.cloned.1.call-done, bf16[2560,1920]{1,0:T(8,128)(2,1)} %param.32), kind=kOutput, calls=%fused_computation.20 | convolution fusion | flops 5057740800 | bytes 26214400 | tf_op jit(solution)/shard_map/dot_general | solution.py:15
  425.6 52.0 %reduce-scatter.27.cloned.1.call-done = bf16[128,2560]{1,0:T(8,128)(2,1)} async-done(((bf16[512,2560]{1,0:T(8,128)(2,1)}), bf16[128,2560]{1,0:T(8,128)(2,1)}) %reduce-scatter.27.cloned.1.call-update) | async-done | bytes 655376 | tf_op jit(solution)/shard_map/reduce_scatter | solution.py:310
  480.8 10.3 all-reduce.11.cloned.1.call-start
  495.5 25.6 %all-gather.26.cloned.1.call-done = bf16[512,2560]{1,0:T(8,128)(2,1)} async-done(((bf16[128,2560]{1,0:T(8,128)(2,1)}), bf16[512,2560]{1,0:T(8,128)(2,1)}) %all-gather.26.cloned.1.call-update) | async-done | bytes 2621456 | tf_op jit(solution)/shard_map/all_gather | solution.py:324
  528.3 11.6 shard_map.289
  576.4 10.1 convolution_convert_fusion.2
  600.3 10.0 convolution_convert_fusion.1
  619.9 9.9 fusion
  629.7 14.4 %copy.160 = bf16[2560,1920]{1,0:T(8,128)(2,1)} copy(bf16[2560,1920]{0,1:T(8,128)(2,1)} %fusion) | data formatting | bytes 19660800
  644.2 10.1 convolution_convert_fusion.6
  655.5 124.2 %all-reduce.11.cloned.1.call-done = (bf16[8,4,80,640]{3,2,0,1:T(8,128)(2,1)}, bf16[8,4,80,640]{3,2,0,1:T(8,128)(2,1)}, bf16[8,4,80,640]{3,2,0,1:T(8,128)(2,1)}) async-done(((bf16[8,4,80,640]{3,2,0,1:T(8,128)(2,1)}, bf16[8,4,80,640]{3,2,0,1:T(8,128)(2,1)}, bf16[8,4,80,640]{3,2,0,1:T(8,128)(2,1)}), (bf16[8,4,80,640]{3,2,0,1:T(8,128)(2,1)}, bf16[8,4,80,640]{3,2,0,1:T(8,128)(2,1)}, ...) | async-done | bytes 9830416
  811.0 50.9 %reduce-scatter.33.cloned.1.call-done = bf16[320,1920]{1,0:T(8,128)(2,1)} async-done(((bf16[2560,1920]{1,0:T(8,128)(2,1)}), bf16[320,1920]{1,0:T(8,128)(2,1)}) %reduce-scatter.33.cloned.1.call-update) | async-done | bytes 1228816 | tf_op jit(solution)/shard_map/reduce_scatter | solution.py:313
  867.1 59.8 %reduce-scatter.31.cloned.1.call-done = f32[80,519]{1,0:T(8,128)} async-done(((f32[640,519]{1,0:T(8,128)}), f32[80,519]{1,0:T(8,128)}) %reduce-scatter.31.cloned.1.call-update) | async-done | bytes 166096 | tf_op jit(solution)/shard_map/reduce_scatter | solution.py:403
  928.4 79.9 %reduce-scatter.35.cloned.1.call-done = bf16[320,1920]{1,0:T(8,128)(2,1)} async-done(((bf16[2560,1920]{1,0:T(8,128)(2,1)}), bf16[320,1920]{1,0:T(8,128)(2,1)}) %reduce-scatter.35.cloned.1.call-update) | async-done | bytes 1228816 | tf_op jit(solution)/shard_map/reduce_scatter | solution.py:313
  1018.9 32.1 %reduce-scatter.29.cloned.1.call-done = bf16[128,2560]{1,0:T(8,128)(2,1)} async-done(((bf16[512,2560]{1,0:T(8,128)(2,1)}), bf16[128,2560]{1,0:T(8,128)(2,1)}) %reduce-scatter.29.cloned.1.call-update) | async-done | bytes 655376 | tf_op jit(solution)/shard_map/reduce_scatter | solution.py:384
  1054.1 79.0 %reduce-scatter.39.cloned.1.call-done = bf16[320,1920]{1,0:T(8,128)(2,1)} async-done(((bf16[2560,1920]{1,0:T(8,128)(2,1)}), bf16[320,1920]{1,0:T(8,128)(2,1)}) %reduce-scatter.39.cloned.1.call-update) | async-done | bytes 1228816 | tf_op jit(solution)/shard_map/reduce_scatter | solution.py:313
  1138.3 71.4 %reduce-scatter.25.cloned.1.call-done = bf16[128,2560]{1,0:T(8,128)(2,1)} async-done(((bf16[512,2560]{1,0:T(8,128)(2,1)}), bf16[128,2560]{1,0:T(8,128)(2,1)}) %reduce-scatter.25.cloned.1.call-update) | async-done | bytes 655376 | tf_op jit(solution)/shard_map/reduce_scatter | solution.py:304
  1213.3 121.5 %reduce-scatter.37.cloned.1.call-done = f32[80,2]{1,0:T(8,128)} async-done(((f32[2560,2]{1,0:T(8,128)}), f32[80,2]{1,0:T(8,128)}) %reduce-scatter.37.cloned.1.call-update) | async-done | bytes 656
  (315 shorter events, 221.2 us)
Async XLA Ops:
  7.2 41.2 %all-gather.28.cloned.1.call-start = ((), (), s32[]{:S(2)}) async-start(), calls=%async_computation.29 | async-start | bytes 2048000 | tf_op jit(solution)/shard_map/all_gather | solution.py:35
  9.9 77.7 %all-gather.32.cloned.1.call-start = ((), (), s32[]{:S(2)}) async-start(), calls=%async_computation.31 | async-start | bytes 2048000 | tf_op jit(solution)/shard_map/all_gather | solution.py:35
  11.9 115.0 %all-gather.36.cloned.1.call-start = ((), (), s32[]{:S(2)}) async-start(), calls=%async_computation.33 | async-start | bytes 2048000 | tf_op jit(solution)/shard_map/all_gather | solution.py:35
  13.7 165.3 %all-gather.20.cloned.1.call-start = ((), (), s32[]{:S(2)}) async-start(), calls=%async_computation.18 | async-start | bytes 3276800 | tf_op jit(solution)/shard_map/all_gather | solution.py:240
  15.1 177.9 %all-gather.30.cloned.1.call-start = ((), (), s32[]{:S(2)}) async-start(), calls=%async_computation.30 | async-start | bytes 4915200 | tf_op jit(solution)/shard_map/all_gather | solution.py:37
  72.8 135.1 %all-gather.34.cloned.1.call-start = ((), (), s32[]{:S(2)}) async-start(), calls=%async_computation.32 | async-start | bytes 4915200 | tf_op jit(solution)/shard_map/all_gather | solution.py:37
  126.8 37.5 %all-to-all-start.2 = ((bf16[4,320,640]{2,1,0:T(8,128)(2,1)}), bf16[4,320,640]{2,1,0:T(8,128)(2,1)S(1)}, u32[]{:S(2)}, u32[]{:S(2)}) async-start(bf16[4,320,640]{2,1,0:T(8,128)(2,1)} %bitcast.429), calls=%async_computation.2 | async-start | bytes 3276800 | tf_op jit(solution)/shard_map/all_to_all | solution.py:36
  131.2 104.5 %all-gather.38.cloned.1.call-start = ((), (), s32[]{:S(2)}) async-start(), calls=%async_computation.34 | async-start | bytes 4915200 | tf_op jit(solution)/shard_map/all_gather | solution.py:37
  165.5 117.1 %reduce-scatter.23.cloned.1.call-start = ((), (), s32[]{:S(2)}) async-start(), calls=%async_computation.19 | async-start | bytes 3276800 | tf_op jit(solution)/shard_map/reduce_scatter | solution.py:294
  198.0 3.9 collective-permute-start
  203.0 10.9 collective-permute-start.1
  242.1 96.4 %all-gather.22.cloned.1.call-start = ((), (), s32[]{:S(2)}) async-start(), calls=%async_computation.20 | async-start | bytes 3276800 | tf_op jit(solution)/shard_map/all_gather | solution.py:297
  285.2 108.8 %all-gather.24.cloned.1.call-start = ((), (), s32[]{:S(2)}) async-start(), calls=%async_computation.22 | async-start | bytes 3276800 | tf_op jit(solution)/shard_map/all_gather | solution.py:242
  287.5 190.1 %reduce-scatter.27.cloned.1.call-start = ((), (), s32[]{:S(2)}) async-start(), calls=%async_computation.23 | async-start | bytes 3276800 | tf_op jit(solution)/shard_map/reduce_scatter | solution.py:310
  425.6 95.6 %all-gather.26.cloned.1.call-start = ((), (), s32[]{:S(2)}) async-start(), calls=%async_computation.24 | async-start | bytes 3276800 | tf_op jit(solution)/shard_map/all_gather | solution.py:324
  480.8 298.9 %all-reduce.11.cloned.1.call-start = ((), (), s32[]{:S(2)}) async-start(), calls=%async_computation.37 | async-start | bytes 19660800
  549.1 8.4 collective-permute-start.2
  566.6 4.6 collective-permute-start.3
  576.1 285.8 %reduce-scatter.33.cloned.1.call-start = ((), (), s32[]{:S(2)}) async-start(), calls=%async_computation.27 | async-start | bytes 11059200 | tf_op jit(solution)/shard_map/reduce_scatter | solution.py:313
  586.5 340.3 %reduce-scatter.31.cloned.1.call-start = ((), (), s32[]{:S(2)}) async-start(), calls=%async_computation.26 | async-start | bytes 1843200 | tf_op jit(solution)/shard_map/reduce_scatter | solution.py:403
  600.2 408.0 %reduce-scatter.35.cloned.1.call-start = ((), (), s32[]{:S(2)}) async-start(), calls=%async_computation.28 | async-start | bytes 11059200 | tf_op jit(solution)/shard_map/reduce_scatter | solution.py:313
  610.3 440.7 %reduce-scatter.29.cloned.1.call-start = ((), (), s32[]{:S(2)}) async-start(), calls=%async_computation.25 | async-start | bytes 3276800 | tf_op jit(solution)/shard_map/reduce_scatter | solution.py:384
  619.6 513.5 %reduce-scatter.39.cloned.1.call-start = ((), (), s32[]{:S(2)}) async-start(), calls=%async_computation.36 | async-start | bytes 11059200 | tf_op jit(solution)/shard_map/reduce_scatter | solution.py:313
  644.1 565.5 %reduce-scatter.25.cloned.1.call-start = ((), (), s32[]{:S(2)}) async-start(), calls=%async_computation.21 | async-start | bytes 3276800 | tf_op jit(solution)/shard_map/reduce_scatter | solution.py:304
  782.2 10.3 all-to-all-start.3
  792.5 9.4 all-to-all-start.4
  861.9 146.3 %all-to-all-start.6 = ((bf16[4,80,1920]{2,1,0:T(8,128)(2,1)}), bf16[4,80,1920]{2,1,0:T(8,128)(2,1)S(1)}, u32[]{:S(2)}, u32[]{:S(2)}) async-start(bf16[4,80,1920]{2,1,0:T(8,128)(2,1)} %bitcast.434), calls=%async_computation.12 | async-start | bytes 2457600 | tf_op jit(solution)/shard_map/all_to_all | solution.py:314
  1008.3 124.9 %all-to-all-start.7 = ((bf16[4,80,1920]{2,1,0:T(8,128)(2,1)}), bf16[4,80,1920]{2,1,0:T(8,128)(2,1)}, u32[]{:S(2)}, u32[]{:S(2)}) async-start(bf16[4,80,1920]{2,1,0:T(8,128)(2,1)} %bitcast.435), calls=%async_computation.14 | async-start | bytes 2457600 | tf_op jit(solution)/shard_map/all_to_all | solution.py:314
  1013.4 321.4 %reduce-scatter.37.cloned.1.call-start = ((), (), s32[]{:S(2)}) async-start(), calls=%async_computation.35 | async-start | bytes 1351680
  1054.1 155.6 %copy-start.7 = (f32[1,128,2560]{2,1,0:T(8,128)S(1)}, f32[1,128,2560]{2,1,0:T(8,128)}, u32[]{:S(2)}) copy-start(f32[1,128,2560]{2,1,0:T(8,128)} %param.33) | copy-start | bytes 3932164
  1054.1 155.6 %copy-start.15 = (bf16[128,2560]{1,0:T(8,128)(2,1)S(1)}, bf16[128,2560]{1,0:T(8,128)(2,1)}, u32[]{:S(2)}) copy-start(bf16[128,2560]{1,0:T(8,128)(2,1)} %reduce-scatter.27.cloned.1.call-done) | copy-start | bytes 1966084
  1133.1 210.0 %all-to-all-start.8 = ((bf16[4,80,1920]{2,1,0:T(8,128)(2,1)}), bf16[4,80,1920]{2,1,0:T(8,128)(2,1)}, u32[]{:S(2)}, u32[]{:S(2)}) async-start(bf16[4,80,1920]{2,1,0:T(8,128)(2,1)} %bitcast.433), calls=%async_computation.15 | async-start | bytes 2457600 | tf_op jit(solution)/shard_map/all_to_all | solution.py:314
  (46 other events, 545.7 us)
Sparse Core Ops, SparseCore 0:
  10.2 38.2 all-gather.27
  50.6 37.0 all-gather.31
  89.8 37.0 all-gather.35
  129.1 49.8 all-gather.19
  180.4 12.5 all-gather.29
  194.4 13.4 all-gather.33
  210.1 13.5 all-gather.37
  242.2 40.4 reduce-scatter.22
  285.4 53.0 all-gather.21
  340.4 53.5 all-gather.23
  425.7 51.8 reduce-scatter.26
  481.0 40.1 all-gather.25
  576.3 203.4 all-reduce.10
  783.6 78.2 reduce-scatter.32
  864.8 62.0 reduce-scatter.30
  930.7 77.5 reduce-scatter.34
  1011.4 39.6 reduce-scatter.28
  1054.9 78.2 reduce-scatter.38
  1135.5 74.0 reduce-scatter.24
  1212.4 122.2 reduce-scatter.36

commit v2 on v1

v2 whole, which is shorter than its diff:
```python
import functools
import math

import jax
import jax.numpy as jnp
from jax import lax
from jax.experimental import pallas as pl
from jax.experimental.pallas import tpu as pltpu
from jax.sharding import PartitionSpec as P

EPSILON = 1e-06
LOW = jnp.bfloat16
FULL = jnp.float32


def dot(left, right, left_dim=1, right_dim=0):
    return lax.dot_general(
        left, right, (((left_dim,), (right_dim,)), ((), ())), preferred_element_type=FULL
    )


def gelu_both(values):
    slope = jnp.sqrt(2.0 / jnp.pi).astype(FULL)
    inner = jnp.tanh(slope * (values + 0.044715 * values * values * values))
    gelu = 0.5 * values * (1.0 + inner)
    grad = 0.5 * (1.0 + inner) + 0.5 * values * (1.0 - inner * inner) * slope * (
        1.0 + 3.0 * 0.044715 * values * values
    )
    return gelu, grad


def head_rows(gate_rows, shards):
    head = gate_rows.shape[1]
    width = gate_rows.shape[0] // shards
    heads = -(-width // head)
    first = (lax.axis_index("wt") * width) // head
    table = gate_rows.reshape(-1, head, head)
    return lax.dynamic_slice_in_dim(table, first, heads, 0)


def edge_swap(values, edge):
    me = lax.axis_index("wt")
    shards = lax.axis_size("wt")
    odd = me % 2 == 1
    mine = jnp.where(odd, values[:, :edge], values[:, -edge:])
    other = lax.ppermute(mine, "wt", [(i, i ^ 1) for i in range(shards)])
    return jnp.where(
        odd,
        jnp.concatenate([other, values], axis=1),
        jnp.concatenate([values, other], axis=1),
    )


def own_part(values, edge):
    odd = lax.axis_index("wt") % 2 == 1
    return jnp.where(odd, values[:, edge:], values[:, :-edge])


def heads_dot(values, table, transposed=False):
    heads, head, _ = table.shape
    return jnp.concatenate(
        [
            dot(values[:, n * head : (n + 1) * head], table[n], 1, 1 if transposed else 0)
            for n in range(heads)
        ],
        axis=1,
    )


def heads_grad(values, slopes, head):
    return jnp.concatenate(
        [
            dot(values[:, n * head : (n + 1) * head], slopes[:, n * head : (n + 1) * head], 0, 0)
            for n in range(values.shape[1] // head)
        ],
        axis=0,
    )


def scan_rows(coef, value, reverse):
    rows = coef.shape[0]
    place = lax.broadcasted_iota(jnp.int32, coef.shape, 0)
    step = 1
    while step < rows:
        if reverse:
            inside = place < rows - step
            by = rows - step
        else:
            inside = place >= step
            by = step
        far_coef = jnp.where(inside, pltpu.roll(coef, by, 0), 1.0)
        far_value = jnp.where(inside, pltpu.roll(value, by, 0), 0.0)
        value = coef * far_value + value
        coef = coef * far_coef
        step *= 2
    return coef, value


def gates_kernel(odd, c_ref, c_own, table_r, table_i, rows_ref, mask_ref, r_ref, ii_ref, a_ref, h_ref):
    c_head = c_ref[...]
    ra = jnp.dot(c_head, table_r[0], preferred_element_type=FULL)
    ia = jnp.dot(c_head, table_i[0], preferred_element_type=FULL)
    r = jax.nn.sigmoid(ra + rows_ref[0:1, :])
    ii = jax.nn.sigmoid(ia + rows_ref[1:2, :])
    keep = mask_ref[:, 0:1]
    log_a = rows_ref[2:3, :] * r
    decay = jnp.exp(2.0 * log_a)
    gap = jnp.where(2.0 * log_a > -0.01, -expm1_small(2.0 * log_a), 1.0 - decay)
    mult = jnp.where(keep == 0.0, 1.0, jnp.sqrt(gap))
    b = (mult * c_own[...].astype(FULL) * ii).astype(LOW).astype(FULL)
    a = jnp.exp(log_a.astype(LOW).astype(FULL)) * keep
    cum_a, h_loc = scan_rows(a, b, False)
    r_ref[...] = r
    ii_ref[...] = ii
    a_ref[...] = cum_a
    h_ref[...] = h_loc


def expm1_small(values):
    return values * (
        1.0 + values * (0.5 + values * (1.0 / 6.0 + values * (1.0 / 24.0 + values / 120.0)))
    )


def gates_scan(c_ext, table_r, table_i, rows8, mask, odd, part_len, width):
    rows = c_ext.shape[0]
    head = table_r.shape[1]
    half = 128
    per = head // half
    grid = (rows // part_len, width // half)
    spec = pltpu.PrefetchScalarGridSpec(
        num_scalar_prefetch=1,
        grid=grid,
        in_specs=[
            pl.BlockSpec((part_len, head), lambda m, n, s: (m, (n + s[0]) // per)),
            pl.BlockSpec((part_len, half), lambda m, n, s: (m, n + s[0])),
            pl.BlockSpec((1, head, half), lambda m, n, s: ((n + s[0]) // per, 0, (n + s[0]) % per)),
            pl.BlockSpec((1, head, half), lambda m, n, s: ((n + s[0]) // per, 0, (n + s[0]) % per)),
            pl.BlockSpec((8, half), lambda m, n, s: (0, n)),
            pl.BlockSpec((part_len, mask.shape[1]), lambda m, n, s: (m, 0)),
        ],
        out_specs=[pl.BlockSpec((part_len, half), lambda m, n, s: (m, n))] * 4,
    )
    return pl.pallas_call(
        gates_kernel,
        grid_spec=spec,
        out_shape=[jax.ShapeDtypeStruct((rows, width), FULL)] * 4,
    )(odd, c_ext, c_ext, table_r, table_i, rows8, mask)


def back_kernel(dh_ref, a_ref, rem_ref, e_ref):
    rows = dh_ref.shape[0]
    place = lax.broadcasted_iota(jnp.int32, dh_ref.shape, 0)
    a_next = jnp.where(place < rows - 1, pltpu.roll(a_ref[...], rows - 1, 0), 1.0)
    rem, e_loc = scan_rows(a_next, dh_ref[...].astype(FULL), True)
    rem_ref[...] = rem
    e_ref[...] = e_loc


def back_scan(dh, a, part_len):
    rows, width = a.shape
    half = 128
    block = pl.BlockSpec((part_len, half), lambda m, n: (m, n))
    return pl.pallas_call(
        back_kernel,
        grid=(rows // part_len, width // half),
        in_specs=[block, block],
        out_specs=[block, block],
        out_shape=[jax.ShapeDtypeStruct((rows, width), FULL)] * 2,
    )(dh, a)


MESH = pl.DeviceIdType.MESH


def remote(source, target, sent, landed, to):
    return pltpu.make_async_remote_copy(
        src_ref=source,
        dst_ref=target,
        send_sem=sent,
        recv_sem=landed,
        device_id={"wt": to},
        device_id_type=MESH,
    )


def greet(n, me, pair=False):
    barrier = pltpu.get_barrier_semaphore()

    @pl.when(me > 0)
    def _():
        pl.semaphore_signal(barrier, 1, device_id={"wt": me - 1}, device_id_type=MESH)

    @pl.when(me < n - 1)
    def _():
        pl.semaphore_signal(barrier, 1, device_id={"wt": me + 1}, device_id_type=MESH)

    peers = (me > 0).astype(jnp.int32) + (me < n - 1).astype(jnp.int32)
    if pair:
        place = lax.axis_index("seq")
        other = {"seq": place + 1 - 2 * lax.rem(place, 2)}
        pl.semaphore_signal(barrier, 1, device_id=other, device_id_type=MESH)
        peers = peers + 1
    pl.semaphore_wait(barrier, peers)


class LineGather:
    def __init__(self, n, me, blocks, sent, landed):
        self.n, self.me, self.blocks, self.sent, self.landed = n, me, blocks, sent, landed

    def rightward(self, d):
        block = self.blocks.at[self.me - d]
        return remote(block, block, self.sent.at[0, d], self.landed.at[0, d + 1], self.me + 1)

    def leftward(self, d):
        block = self.blocks.at[self.me + d]
        return remote(block, block, self.sent.at[1, d], self.landed.at[1, d + 1], self.me - 1)

    def start(self):
        @pl.when(self.me < self.n - 1)
        def _():
            self.rightward(0).start()

        @pl.when(self.me > 0)
        def _():
            self.leftward(0).start()

    def arrive(self, d):
        n, me = self.n, self.me

        @pl.when(me - d >= 0)
        def _():
            block = self.blocks.at[me - d]
            remote(block, block, self.sent.at[0, 0], self.landed.at[0, d], me).wait_recv()

            @pl.when(me < n - 1)
            def _():
                self.rightward(d).start()

        @pl.when(me + d < n)
        def _():
            block = self.blocks.at[me + d]
            remote(block, block, self.sent.at[1, 0], self.landed.at[1, d], me).wait_recv()

            @pl.when(me > 0)
            def _():
                self.leftward(d).start()

    def each(self, d, use):
        def side(k, carry):
            q = self.me + (2 * k - 1) * d

            @pl.when((q >= 0) & (q < self.n))
            def _():
                use(q)

            return carry

        lax.fori_loop(0, 2, side, 0)

    def finish(self):
        n, me = self.n, self.me
        for d in range(n - 1):

            @pl.when((me - d >= 0) & (me < n - 1))
            def _():
                self.rightward(d).wait_send()

            @pl.when((me + d < n) & (me > 0))
            def _():
                self.leftward(d).wait_send()


def line_gather(n, me, blocks, sent, landed, use, ready):
    line = LineGather(n, me, blocks, sent, landed)
    line.start()
    ready()
    use(me)

    def step(d, carry):
        line.arrive(d)
        line.each(d, use)
        return carry

    lax.fori_loop(1, n, step, 0)
    line.finish()


class LineReduce:
    def __init__(self, n, me, parts, slots, sent, landed):
        self.n, self.me, self.parts, self.slots = n, me, parts, slots
        self.sent, self.landed = sent, landed

    def rightward(self, k):
        source, target = self.parts.at[self.n - 1 - k], self.slots.at[0, k]
        return remote(source, target, self.sent.at[0, k], self.landed.at[0, k], self.me + 1)

    def leftward(self, k):
        source, target = self.parts.at[k], self.slots.at[1, k]
        return remote(source, target, self.sent.at[1, k], self.landed.at[1, k], self.me - 1)

    def arrived(self, side, k):
        slot = self.slots.at[side, k]
        remote(slot, slot, self.sent.at[side, k], self.landed.at[side, k], self.me).wait_recv()

    def add(self, q, side, k):
        total = self.parts[q].astype(FULL) + self.slots[side, k].astype(FULL)
        self.parts[q] = total.astype(LOW)

    def start(self, partial, early=True):
        n, me = self.n, self.me

        def first(k, carry):
            def side(which, inner):
                q = jnp.where(which == 0, n - 1 - k, k)

                @pl.when(jnp.where(which == 0, q > me, q < me))
                def _():
                    partial(q)

                return inner

            lax.fori_loop(0, 2, side, 0)

            @pl.when((k == 0) & (me == 0) & early)
            def _():
                self.rightward(0).start()

            @pl.when((k == 0) & (me == n - 1) & early)
            def _():
                self.leftward(0).start()

            return carry

        lax.fori_loop(0, n - 1, first, 0)
        partial(me)

    def relay(self, k):
        n, me = self.n, self.me

        @pl.when(n - 1 - k > me)
        def _():
            @pl.when(me > 0)
            def _():
                self.arrived(0, k)
                self.add(n - 1 - k, 0, k)

            if k > 0:
                self.rightward(k - 1).wait_send()

            @pl.when((me > 0) | (k > 0))
            def _():
                self.rightward(k).start()

        @pl.when(k < me)
        def _():
            @pl.when(me < n - 1)
            def _():
                self.arrived(1, k)
                self.add(k, 1, k)

            if k > 0:
                self.leftward(k - 1).wait_send()

            @pl.when((me < n - 1) | (k > 0))
            def _():
                self.leftward(k).start()

    def total(self):
        n, me = self.n, self.me

        @pl.when(me > 0)
        def _():
            self.arrived(0, n - 1 - me)

        @pl.when(me < n - 1)
        def _():
            self.arrived(1, me)

        total = self.parts[me].astype(FULL)
        other = self.slots[0, jnp.clip(n - 1 - me, 0, n - 2)].astype(FULL)
        total = total + jnp.where(me > 0, other, 0.0)
        other = self.slots[1, jnp.clip(me, 0, n - 2)].astype(FULL)
        return total + jnp.where(me < n - 1, other, 0.0)

    def finish(self):
        @pl.when(self.me < self.n - 1)
        def _():
            self.rightward(self.n - 2 - self.me).wait_send()

        @pl.when(self.me > 0)
        def _():
            self.leftward(self.me - 1).wait_send()


class LineBoth:
    def __init__(self, gather, back):
        self.gather, self.back = gather, back
        self.n, self.me = gather.n, gather.me

    def sends(self, side, t, act):
        n, me = self.n, self.me
        place = me if side == 0 else n - 1 - me
        spread = self.gather.rightward if side == 0 else self.gather.leftward
        pull = self.back.rightward if side == 0 else self.back.leftward

        @pl.when(place < n - 1)
        def _():
            @pl.when(t <= place)
            def _():
                act(spread(t))

            @pl.when(t > place)
            def _():
                act(pull(t - place - 1))

    def step(self, t):
        n, me = self.n, self.me
        for side in range(2):
            place = me if side == 0 else n - 1 - me
            if t > 0:

                @pl.when(t <= place)
                def _():
                    block = self.gather.blocks.at[me - t if side == 0 else me + t]
                    remote(
                        block, block, self.gather.sent.at[side, 0], self.gather.landed.at[side, t], me
                    ).wait_recv()

                @pl.when((t > place) & (place > 0))
                def _():
                    k = t - place - 1
                    self.back.arrived(side, k)
                    self.back.add(n - 1 - k if side == 0 else k, side, k)

                self.sends(side, t - 1, lambda copy: copy.wait_send())
            self.sends(side, t, lambda copy: copy.start())

    def finish(self):
        for side in range(2):
            self.sends(side, self.n - 1, lambda copy: copy.wait_send())


def line_reduce(n, me, parts, slots, sent, landed, partial, between, finish):
    line = LineReduce(n, me, parts, slots, sent, landed)
    line.start(partial)
    for k in range(n - 1):
        line.relay(k)
        between(k)
    finish(line.total())
    line.finish()


def tiles(count, size, body):
    def step(t, carry):
        body(pl.ds(pl.multiple_of(t * size, size), size))
        return carry

    lax.fori_loop(0, count // size, step, 0)


def tile_of(width, limit):
    size = limit
    while width % size:
        size -= 128
    return size


VMEM = pl.BlockSpec(memory_space=pltpu.VMEM)
ANY = pl.BlockSpec(memory_space=pl.ANY)


def gather_sems(n):
    return [pltpu.SemaphoreType.DMA((2, n)), pltpu.SemaphoreType.DMA((2, n + 1))]


def reduce_sems(n):
    return [pltpu.SemaphoreType.DMA((2, n)), pltpu.SemaphoreType.DMA((2, n))]


def lasting(micros):
    return pl.CostEstimate(
        flops=int(micros * 1.0e9), bytes_accessed=int(micros * 3.4e6), transcendentals=0
    )


def comm_params(number):
    return pltpu.CompilerParams(
        collective_id=number, has_side_effects=True, vmem_limit_bytes=64 * 1024 * 1024
    )


def enter_kernel(
    n, x_ref, gain_ref, doc_ref, win_hbm, wbr_hbm, xn_ref, u_ref, y_ref, docs_ref, win, wbr, docs, sent, landed, dsent, dlanded, local
):
    me = lax.axis_index("wt")
    loads = [
        pltpu.make_async_copy(win_hbm, win, local.at[0]),
        pltpu.make_async_copy(wbr_hbm, wbr, local.at[1]),
    ]
    for load in loads:
        load.start()
    docs[me] = jnp.broadcast_to(doc_ref[...], docs.shape[1:])
    flat = x_ref[...].astype(FULL)
    scale = lax.rsqrt(jnp.mean(flat * flat, axis=-1, keepdims=True) + EPSILON)
    xn_ref[me] = (flat * scale * gain_ref[...]).astype(LOW)
    greet(n, me)
    notes = LineGather(n, me, docs, dsent, dlanded)
    line = LineGather(n, me, xn_ref, sent, landed)
    notes.start()
    line.start()
    for load in loads:
        load.wait()

    def use(q):
        block = xn_ref[q]
        u_ref[q] = dot(block, win[...]).astype(LOW)
        y_ref[q] = dot(block, wbr[...])

    use(me)

    def step(d, carry):
        notes.arrive(d)
        line.arrive(d)
        line.each(d, use)
        return carry

    lax.fori_loop(1, n, step, 0)
    docs_ref[...] = docs[...]
    notes.finish()
    line.finish()


def enter(n, x, gain, doc, win, wbr):
    rows, model = x.shape
    width = win.shape[1]
    return pl.pallas_call(
        functools.partial(enter_kernel, n),
        out_shape=[
            jax.ShapeDtypeStruct((n, rows, model), LOW),
            jax.ShapeDtypeStruct((n, rows, width), LOW),
            jax.ShapeDtypeStruct((n, rows, width), FULL),
            jax.ShapeDtypeStruct((n, 8, rows), jnp.int32),
        ],
        in_specs=[VMEM, VMEM, VMEM, ANY, ANY],
        out_specs=[VMEM, VMEM, VMEM, VMEM],
        scratch_shapes=[
            pltpu.VMEM(win.shape, LOW),
            pltpu.VMEM(wbr.shape, LOW),
            pltpu.VMEM((n, 8, rows), jnp.int32),
        ]
        + gather_sems(n)
        + gather_sems(n)
        + [pltpu.SemaphoreType.DMA((2,))],
        compiler_params=comm_params(0),
        cost_estimate=lasting(50),
    )(x, gain, doc, win, wbr)


def close_kernel(
    n, o_ref, x_ref, gain_ref, w_ref, slope_ref, x1_ref, xn2_ref, dm_ref, parts, slots, sent, landed, gsent, glanded
):
    me = lax.axis_index("wt")
    dm_ref[me] = slope_ref[...].astype(LOW)
    greet(n, me)
    model = w_ref.shape[0]

    def partial(q):
        block = o_ref[q]

        def tile(at):
            parts[q, :, at] = dot(block, w_ref[at, :], 1, 1).astype(LOW)

        tiles(model, tile_of(model, 512), tile)

    def finish(total):
        x1 = x_ref[...].astype(FULL) + total
        x1_ref[...] = x1
        scale = lax.rsqrt(jnp.mean(x1 * x1, axis=-1, keepdims=True) + EPSILON)
        xn2_ref[...] = (x1 * scale * gain_ref[...]).astype(LOW)

    back = LineReduce(n, me, parts, slots, sent, landed)
    both = LineBoth(LineGather(n, me, dm_ref, gsent, glanded), back)
    both.step(0)
    back.start(partial, False)
    for t in range(1, n):
        both.step(t)
    finish(back.total())
    both.finish()


def close(n, o, x, gain, weight, slope):
    rows, model = x.shape
    return pl.pallas_call(
        functools.partial(close_kernel, n),
        out_shape=[
            jax.ShapeDtypeStruct((rows, model), FULL),
            jax.ShapeDtypeStruct((rows, model), LOW),
            jax.ShapeDtypeStruct((n, rows, model), LOW),
        ],
        in_specs=[VMEM] * 5,
        out_specs=[VMEM] * 3,
        scratch_shapes=[
            pltpu.VMEM((n, rows, model), LOW),
            pltpu.VMEM((2, n - 1, rows, model), LOW),
        ]
        + reduce_sems(n)
        + gather_sems(n),
        compiler_params=comm_params(1),
        cost_estimate=lasting(65),
    )(o, x, gain, weight, slope)


class PairSum:
    def __init__(self, part, halves, landing, sent, landed, free, flush, tag):
        self.me = lax.axis_index("seq")
        self.mine = lax.rem(self.me, 2)
        self.part, self.halves, self.landing = part, halves, landing
        self.sent, self.landed, self.free, self.flush = sent, landed, free, flush
        self.count = tag

    def other(self):
        return {"seq": self.me + 1 - 2 * self.mine}

    def send(self, slot):
        return pltpu.make_async_remote_copy(
            src_ref=self.halves.at[slot, 1 - self.mine],
            dst_ref=self.landing.at[slot],
            send_sem=self.sent.at[slot],
            recv_sem=self.landed.at[slot],
            device_id=self.other(),
            device_id_type=MESH,
        )

    def run(self, steps, compute, target):
        half = self.landing.shape[1]
        for t in range(steps):
            slot = self.count % 2

            def out(slot, t):
                return pltpu.make_async_copy(
                    self.halves.at[slot, self.mine],
                    target.at[pl.ds(t * half, half), :],
                    self.flush.at[slot],
                )

            if self.count >= 2:
                self.send(slot).wait_send()
                pltpu.make_async_copy(
                    self.halves.at[slot, self.mine], target.at[pl.ds(0, half), :], self.flush.at[slot]
                ).wait()
                pl.semaphore_wait(self.free, 1)
            compute(t, self.halves.at[slot])
            self.send(slot).start()
            self.send(slot).wait_recv()
            total = self.halves[slot, self.mine].astype(FULL) + self.landing[slot].astype(FULL)
            self.halves[slot, self.mine] = total.astype(LOW)
            pl.semaphore_signal(self.free, 1, device_id=self.other(), device_id_type=MESH)
            out(slot, t).start()
            self.count += 1

    def finish(self, target):
        half = self.landing.shape[1]
        for slot in range(2):
            self.send(slot).wait_send()
            pltpu.make_async_copy(
                self.halves.at[slot, self.mine], target.at[pl.ds(0, half), :], self.flush.at[slot]
            ).wait()
        pl.semaphore_wait(self.free, 2)


def pair_scratch(half, width):
    return [
        pltpu.VMEM((2, 2, half, width), LOW),
        pltpu.VMEM((2, half, width), LOW),
        pltpu.SemaphoreType.DMA((2,)),
        pltpu.SemaphoreType.DMA((2,)),
        pltpu.SemaphoreType.REGULAR,
        pltpu.SemaphoreType.DMA((2,)),
    ]


def pair_tile(model, places):
    size = 2 * model // places
    return size if size % 128 == 0 else size * 128 // math.gcd(size, 128)


def pair_dot(left, right, part, size):
    n, rows, _ = left.shape

    def compute(t, halves):
        lhs = left[:, :, pl.ds(t * size, size)].reshape(n * rows, size)
        width = right.shape[2]

        def tile(at):
            rhs = right[:, :, at].reshape(n * rows, -1)
            value = dot(lhs, rhs, 0, 0).astype(LOW)
            for k in range(size // (2 * part)):
                for side in range(2):
                    first = (2 * k + side) * part
                    halves[side, k * part : (k + 1) * part, at] = value[first : first + part]

        tiles(width, tile_of(width, 640), tile)

    return compute


def ffn_kernel(
    n,
    places,
    xn2_ref,
    dm_hbm,
    wg_hbm,
    wu_hbm,
    wd_hbm,
    dxn2_ref,
    hidden_hbm,
    gate_hbm,
    up_hbm,
    down_hbm,
    xall,
    dm,
    wg,
    wu,
    wd,
    hidden,
    dg,
    dv,
    parts,
    slots,
    halves,
    landing,
    psent,
    planded,
    free,
    pflush,
    gsent,
    glanded,
    rsent,
    rlanded,
    local,
    flush,
):
    me = lax.axis_index("wt")
    rows, model = xn2_ref.shape
    units = wg.shape[1]
    cut = tile_of(units, 640)
    span = tile_of(model, 512)
    loads = [
        pltpu.make_async_copy(source, target, local.at[k])
        for k, (source, target) in enumerate(
            [(wg_hbm, wg), (wu_hbm, wu), (wd_hbm, wd), (dm_hbm, dm)]
        )
    ]
    for load in loads:
        load.start()
    xall[me] = xn2_ref[...]
    greet(n, me, True)

    def ready():
        for load in loads:
            load.wait()

    def use(q):
        def tile(at):
            block = xall[q]
            g = dot(block, wg[:, at])
            v = dot(block, wu[:, at])
            back = dot(dm[q], wd[:, at])
            gelu, slope = gelu_both(g)
            hidden[q, :, at] = (gelu * v).astype(LOW)
            dg[q, :, at] = (back * v * slope).astype(LOW)
            dv[q, :, at] = (back * gelu).astype(LOW)

        tiles(units, cut, tile)

    line_gather(n, me, xall, gsent, glanded, use, ready)
    out = pltpu.make_async_copy(hidden, hidden_hbm, flush.at[0])
    out.start()

    def partial(q):
        def tile(at):
            total = dot(dg[q], wg[at, :], 1, 1) + dot(dv[q], wu[at, :], 1, 1)
            parts[q, :, at] = total.astype(LOW)

        tiles(model, span, tile)

    part = model // places
    size = pair_tile(model, places)
    pair = PairSum(part, halves, landing, psent, planded, free, pflush, 0)

    def between(k):
        if k == 0:
            pair.run(model // size, pair_dot(dm, hidden, part, size), down_hbm)
        if k == 1:
            pair.run(model // size, pair_dot(xall, dg, part, size), gate_hbm)
        if k == n - 2:
            pair.run(model // size, pair_dot(xall, dv, part, size), up_hbm)

    def finish(total):
        dxn2_ref[...] = total

    line_reduce(n, me, parts, slots, rsent, rlanded, partial, between, finish)
    pair.finish(up_hbm)
    out.wait()


def ffn(n, places, xn2, dm, wg, wu, wd):
    rows, model = xn2.shape
    units = wg.shape[1]
    grad = jax.ShapeDtypeStruct((model // 2, units), LOW)
    return pl.pallas_call(
        functools.partial(ffn_kernel, n, places),
        out_shape=[
            jax.ShapeDtypeStruct((rows, model), FULL),
            jax.ShapeDtypeStruct((n, rows, units), LOW),
            grad,
            grad,
            grad,
        ],
        in_specs=[VMEM, ANY, ANY, ANY, ANY],
        out_specs=[VMEM, ANY, ANY, ANY, ANY],
        scratch_shapes=[
            pltpu.VMEM((n, rows, model), LOW),
            pltpu.VMEM((n, rows, model), LOW),
            pltpu.VMEM((model, units), LOW),
            pltpu.VMEM((model, units), LOW),
            pltpu.VMEM((model, units), LOW),
            pltpu.VMEM((n, rows, units), LOW),
            pltpu.VMEM((n, rows, units), LOW),
            pltpu.VMEM((n, rows, units), LOW),
            pltpu.VMEM((n, rows, model), LOW),
            pltpu.VMEM((2, n - 1, rows, model), LOW),
        ]
        + pair_scratch(pair_tile(model, places) // 2, units)
        + gather_sems(n)
        + reduce_sems(n)
        + [pltpu.SemaphoreType.DMA((4,)), pltpu.SemaphoreType.DMA((1,))],
        compiler_params=comm_params(2),
        cost_estimate=lasting(125),
    )(xn2, dm, wg, wu, wd)


def back_in_kernel(
    n,
    dxn2_ref,
    x1_ref,
    slope_ref,
    gain_ref,
    w_hbm,
    hidden_hbm,
    wd_hbm,
    dx1_ref,
    dz_ref,
    do_ref,
    sum_ref,
    out_ref,
    w,
    hidden,
    wd,
    parts,
    slots,
    sent,
    landed,
    rsent,
    rlanded,
    local,
):
    me = lax.axis_index("wt")
    loads = [
        pltpu.make_async_copy(source, target, local.at[k])
        for k, (source, target) in enumerate([(w_hbm, w), (hidden_hbm, hidden), (wd_hbm, wd)])
    ]
    for load in loads:
        load.start()
    x1 = x1_ref[...]
    dxn2 = dxn2_ref[...]
    model = x1.shape[1]
    scale = lax.rsqrt(jnp.mean(x1 * x1, axis=-1, keepdims=True) + EPSILON)
    q2 = dxn2 * gain_ref[...]
    pull = jnp.mean(q2 * x1, axis=-1, keepdims=True)
    dx1 = slope_ref[...] + scale * (q2 - x1 * (scale * scale * pull))
    dx1_ref[...] = dx1
    dz_ref[me] = dx1.astype(LOW)
    greet(n, me)
    line = LineGather(n, me, dz_ref, sent, landed)
    back = LineReduce(n, me, parts, slots, rsent, rlanded)
    both = LineBoth(line, back)
    both.step(0)
    sum_ref[...] = jnp.sum(dxn2 * x1 * scale, axis=0, keepdims=True)
    for load in loads:
        load.wait()

    def use(q):
        do_ref[q] = dot(dz_ref[q], w[...])

    def partial(q):
        def tile(at):
            parts[q, :, at] = dot(hidden[q], wd[at, :], 1, 1).astype(LOW)

        tiles(model, tile_of(model, 512), tile)

    back.start(partial, False)
    use(me)
    for t in range(1, n):
        both.step(t)
        line.each(t, use)
    out_ref[...] = (x1_ref[...] + back.total()).astype(LOW)
    both.finish()


def back_in(n, dxn2, x1, slope, gain, weight, hidden, wd):
    rows, model = x1.shape
    return pl.pallas_call(
        functools.partial(back_in_kernel, n),
        out_shape=[
            jax.ShapeDtypeStruct((rows, model), FULL),
            jax.ShapeDtypeStruct((n, rows, model), LOW),
            jax.ShapeDtypeStruct((n, rows, weight.shape[1]), FULL),
            jax.ShapeDtypeStruct((1, model), FULL),
            jax.ShapeDtypeStruct((rows, model), LOW),
        ],
        in_specs=[VMEM] * 4 + [ANY] * 3,
        out_specs=[VMEM] * 5,
        scratch_shapes=[
            pltpu.VMEM(weight.shape, LOW),
            pltpu.VMEM(hidden.shape, LOW),
            pltpu.VMEM(wd.shape, LOW),
            pltpu.VMEM((n, rows, model), LOW),
            pltpu.VMEM((2, n - 1, rows, model), LOW),
        ]
        + gather_sems(n)
        + reduce_sems(n)
        + [pltpu.SemaphoreType.DMA((3,))],
        compiler_params=comm_params(3),
        cost_estimate=lasting(65),
    )(dxn2, x1, slope, gain, weight, hidden, wd)


def leave_kernel(
    n,
    places,
    du_ref,
    dy_ref,
    o_ref,
    x_ref,
    dx1_ref,
    gain_ref,
    xn_hbm,
    dz_hbm,
    win_hbm,
    wbr_hbm,
    grad_ref,
    sum_ref,
    mix_hbm,
    xn,
    dz,
    win,
    wbr,
    parts,
    slots,
    halves,
    landing,
    psent,
    planded,
    free,
    pflush,
    sent,
    landed,
    local,
):
    me = lax.axis_index("wt")
    loads = [
        pltpu.make_async_copy(source, target, local.at[k])
        for k, (source, target) in enumerate(
            [(win_hbm, win), (wbr_hbm, wbr), (xn_hbm, xn), (dz_hbm, dz)]
        )
    ]
    for load in loads:
        load.start()
    greet(n, me, True)
    for load in loads:
        load.wait()
    model = win.shape[0]

    def partial(q):
        def tile(at):
            total = dot(du_ref[q], win[at, :], 1, 1) + dot(dy_ref[q], wbr[at, :], 1, 1)
            parts[q, :, at] = total.astype(LOW)

        tiles(model, tile_of(model, 512), tile)

    part = model // places
    size = pair_tile(model, places)
    width = du_ref.shape[2]
    pair = PairSum(part, halves, landing, psent, planded, free, pflush, 0)

    def compute(t, target):
        for k, (left, right) in enumerate([(dz, o_ref), (xn, dy_ref), (xn, du_ref)]):
            columns = pl.ds(k * width, width)
            pair_dot(left, right, part, size)(t, target.at[:, :, columns])

    def between(k):
        if k == 0:
            pair.run(model // size, compute, mix_hbm)

    def finish(total):
        flat = x_ref[...].astype(FULL)
        scale = lax.rsqrt(jnp.mean(flat * flat, axis=-1, keepdims=True) + EPSILON)
        q1 = total * gain_ref[...]
        pull = jnp.mean(q1 * flat, axis=-1, keepdims=True)
        grad_ref[...] = dx1_ref[...] + scale * (q1 - flat * (scale * scale * pull))
        sum_ref[...] = jnp.sum(total * flat * scale, axis=0, keepdims=True)

    line_reduce(n, me, parts, slots, sent, landed, partial, between, finish)
    pair.finish(mix_hbm)


def leave(n, places, du, dy, o, x, dx1, gain, xn, dz, win, wbr):
    rows, model = x.shape
    width = win.shape[1]
    return pl.pallas_call(
        functools.partial(leave_kernel, n, places),
        out_shape=[
            jax.ShapeDtypeStruct((rows, model), FULL),
            jax.ShapeDtypeStruct((1, model), FULL),
            jax.ShapeDtypeStruct((model // 2, 3 * width), LOW),
        ],
        in_specs=[VMEM] * 6 + [ANY] * 4,
        out_specs=[VMEM, VMEM, ANY],
        scratch_shapes=[
            pltpu.VMEM((n, rows, model), LOW),
            pltpu.VMEM((n, rows, model), LOW),
            pltpu.VMEM(win.shape, LOW),
            pltpu.VMEM(wbr.shape, LOW),
            pltpu.VMEM((n, rows, model), LOW),
            pltpu.VMEM((2, n - 1, rows, model), LOW),
        ]
        + pair_scratch(pair_tile(model, places) // 2, 3 * width)
        + reduce_sems(n)
        + [pltpu.SemaphoreType.DMA((4,))],
        compiler_params=comm_params(4),
        cost_estimate=lasting(60),
    )(du, dy, o, x, dx1, gain, xn, dz, win, wbr)


def on_device(
    inputs,
    segment,
    mixer_gain,
    input_weight,
    branch_weight,
    conv_weight,
    recur_gate,
    input_gate,
    recur_bias,
    input_bias,
    decay_rate,
    output_weight,
    second_gain,
    gate_weight,
    up_weight,
    down_weight,
    cotangent,
):
    shards = lax.axis_size("wt")
    places = lax.axis_size("seq")
    me_w = lax.axis_index("wt")
    me_s = lax.axis_index("seq")
    part_len, model = inputs.shape[1:]
    lru = conv_weight.shape[0]
    taps = conv_weight.shape[1]
    width = lru // shards
    head = recur_gate.shape[1]
    edge = width % head
    rows = shards * part_len
    onward = [(s, s + 1) for s in range(places - 1)]
    backward = [(s + 1, s) for s in range(places - 1)]

    def mine(vector):
        return lax.dynamic_slice_in_dim(vector, me_w * width, width, 0)

    x = inputs[0]
    xn, u3, y, docs = enter(shards, x, mixer_gain[None], segment, input_weight, branch_weight)
    docs = docs[:, 0]
    reach = taps - 1
    lead = lax.ppermute(docs[:, -reach:], "seq", onward)
    trail = lax.ppermute(docs[:, :reach], "seq", backward)
    lead = jnp.where(me_s == 0, -1, lead)
    trail = jnp.where(me_s == places - 1, -1, trail)
    window = jnp.concatenate([lead, docs, trail], axis=1)
    same_wide = jnp.stack(
        [
            window[:, taps - 1 :] == window[:, taps - 1 - k : window.shape[1] - k]
            for k in range(taps)
        ],
        axis=-1,
    ).astype(FULL)
    same = same_wide[:, :part_len]
    keep = same[:, :, 1].reshape(rows, 1)
    reset = keep == 0.0

    y = y.reshape(rows, width)
    slope = cotangent[0]

    tail = u3[:, part_len - (taps - 1) :, :]
    before = lax.ppermute(tail, "seq", onward)
    extended = jnp.concatenate([before, u3], axis=1).astype(FULL)
    conv_mine = mine(conv_weight)
    windows = [
        extended[:, taps - 1 - k : taps - 1 - k + part_len, :] * same[:, :, k : k + 1]
        for k in range(taps)
    ]
    conv = sum(windows[k] * conv_mine[:, k] for k in range(taps))
    c_low = conv.reshape(rows, width).astype(LOW)
    c_ext = edge_swap(c_low, edge)
    recur_table = head_rows(recur_gate, shards)
    input_table = head_rows(input_gate, shards)
    c = c_low.astype(FULL)
    rate = mine(decay_rate)
    soft = -8.0 * jax.nn.softplus(rate)
    odd = (me_w % 2).astype(jnp.int32).reshape(1) * (edge // 128)
    rows8 = jnp.concatenate(
        [jnp.stack([mine(recur_bias), mine(input_bias), soft]), jnp.zeros((5, width), FULL)]
    )
    r, ii, cum_a, h_loc = gates_scan(
        c_ext, recur_table, input_table, rows8, keep, odd, part_len, width
    )
    log_a = soft * r
    mult = jnp.where(reset, 1.0, jnp.sqrt(-jnp.expm1(2.0 * log_a)))
    a = jnp.exp(log_a.astype(LOW).astype(FULL)) * keep
    a3 = a.reshape(shards, part_len, width)
    cum_a = cum_a.reshape(a3.shape)
    h_loc = h_loc.reshape(a3.shape)
    ends = lax.all_gather(jnp.stack([cum_a[:, -1], h_loc[:, -1]]), "seq", axis=0)
    carry = jnp.zeros((shards, width), FULL)
    h_in = carry
    for n in range(places):
        h_in = jnp.where(me_s == n, carry, h_in)
        carry = ends[n, 0] * carry + ends[n, 1]
    h_in = h_in[:, None]
    h = h_loc + cum_a * h_in
    h_prev = jnp.concatenate([h_in, h[:, :-1]], axis=1).reshape(rows, width)
    hr = h.reshape(rows, width).astype(LOW).astype(FULL)
    gelu_y, grad_y = gelu_both(y)
    o = (hr * gelu_y).astype(LOW)
    x1, xn2, dm = close(shards, o.reshape(u3.shape), x, second_gain[None], output_weight, slope)
    dxn2, hidden, gate_term, up_term, down_term = ffn(
        shards, places, xn2, dm, gate_weight, up_weight, down_weight
    )
    groups = [list(range(k, places, 2)) for k in range(2)]

    def reduce_pair(term):
        kept = lax.psum_scatter(
            term, "seq", scatter_dimension=0, tiled=True, axis_index_groups=groups
        )
        wide = lax.all_to_all(kept, "wt", split_axis=0, concat_axis=1, tiled=True)
        return wide.astype(FULL)

    def reduce(term):
        kept = lax.psum_scatter(term.astype(LOW), "seq", scatter_dimension=0, tiled=True)
        wide = lax.all_to_all(kept, "wt", split_axis=0, concat_axis=1, tiled=True)
        return wide.astype(FULL)

    gate_grad = reduce_pair(gate_term)
    up_grad = reduce_pair(up_term)
    down_grad = reduce_pair(down_term)

    dx1, dz, do, second_gain_grad, block_out = back_in(
        shards, dxn2, x1, slope, second_gain[None], output_weight, hidden, down_weight
    )
    do = do.reshape(rows, width)

    dh = (do * gelu_y).astype(LOW)
    dy = (do * hr * grad_y).astype(LOW)

    rem, e_loc = back_scan(dh, a, part_len)
    rem = rem.reshape(a3.shape)
    e_loc = e_loc.reshape(a3.shape)
    heads_out = jnp.stack([cum_a[:, -1], a3[:, 0] * e_loc[:, 0]])
    firsts = lax.all_gather(heads_out, "seq", axis=0)
    carry = jnp.zeros((shards, width), FULL)
    e_in = carry
    for n in reversed(range(places)):
        e_in = jnp.where(me_s == n, carry, e_in)
        carry = firsts[n, 0] * carry + firsts[n, 1]
    e_in = e_in[:, None]
    e = (e_loc + rem * e_in).reshape(rows, width)
    dla = (e * h_prev * a).astype(LOW).astype(FULL)
    dbr = e.astype(LOW).astype(FULL)
    dmult = jnp.where(reset, 0.0, -jnp.exp(2.0 * log_a) / mult)
    dlog_a = dla + dbr * c * ii * dmult
    dra_f = soft * dlog_a * r * (1.0 - r)
    dia_f = dbr * mult * c * ii * (1.0 - ii)
    recur_bias_grad = jnp.sum(dra_f, axis=0)
    input_bias_grad = jnp.sum(dia_f, axis=0)
    decay_grad = jnp.sum(-8.0 * dlog_a * r, axis=0) * jax.nn.sigmoid(rate)
    slopes = jnp.concatenate([dra_f.astype(LOW), dia_f.astype(LOW)], axis=0)
    slopes = edge_swap(slopes, edge)
    dra, dia = slopes[:rows], slopes[rows:]
    recur_gate_grad = heads_grad(c_ext, dra, head)
    input_gate_grad = heads_grad(c_ext, dia, head)
    mixed = heads_dot(dra, recur_table, True) + heads_dot(dia, input_table, True)
    dc = (dbr * mult * ii + own_part(mixed, edge)).reshape(shards, part_len, width)
    conv_grad = jnp.stack([jnp.sum(windows[k] * dc, axis=(0, 1)) for k in range(taps)], axis=-1)
    lead = lax.ppermute(dc[:, : taps - 1], "seq", backward)
    dc_ext = jnp.concatenate([dc, lead], axis=1)
    du = sum(
        (dc_ext * same_wide[:, :, k : k + 1])[:, k : k + part_len] * conv_mine[:, k]
        for k in range(taps)
    )
    du = du.reshape(rows, width).astype(LOW)
    input_grad, mixer_gain_grad, mix_term = leave(
        shards,
        places,
        du.reshape(u3.shape),
        dy.reshape(u3.shape),
        o.reshape(u3.shape),
        x,
        dx1,
        mixer_gain[None],
        xn,
        dz,
        input_weight,
        branch_weight,
    )
    mixed = reduce_pair(mix_term).reshape(-1, shards, 3, width)
    out_grad, branch_grad, input_weight_grad = [
        mixed[:, :, k].reshape(-1, lru) for k in range(3)
    ]

    small = jnp.concatenate(
        [
            own_part(recur_gate_grad.T, edge).T,
            own_part(input_gate_grad.T, edge).T,
            conv_grad,
            recur_bias_grad[:, None],
            input_bias_grad[:, None],
            decay_grad[:, None],
        ],
        axis=1,
    )
    small = lax.psum_scatter(small.astype(LOW), "seq", scatter_dimension=0, tiled=True)
    moves = [
        (s * shards + w, w * places + s) for s in range(places) for w in range(shards)
    ]
    small = lax.ppermute(small, ("seq", "wt"), moves).astype(FULL)
    share = model // (places * shards)
    gains = jnp.concatenate(
        [mixer_gain_grad.reshape(-1, share), second_gain_grad.reshape(-1, share)], axis=1
    )
    gains = lax.psum_scatter(gains, ("seq", "wt"), scatter_dimension=0, tiled=True)[0]
    at = 2 * head + taps
    return (
        block_out[None],
        input_grad[None],
        gains[:share],
        input_weight_grad,
        branch_grad,
        small[:, 2 * head : at],
        small[:, :head],
        small[:, head : 2 * head],
        small[:, at],
        small[:, at + 1],
        small[:, at + 2],
        out_grad,
        gains[share:],
        gate_grad,
        up_grad,
        down_grad,
    )


def solution(mesh):
    tokens = P("wt", "seq", None)
    columns = P(None, "wt")
    row = P(("seq", "wt"))
    flat_rows = P(("seq", "wt"), None)
    return jax.shard_map(
        on_device,
        mesh=mesh,
        in_specs=(
            tokens,
            P("wt", "seq"),
            P(),
            columns,
            columns,
            P(),
            P(),
            P(),
            P(),
            P(),
            P(),
            columns,
            P(),
            columns,
            columns,
            columns,
            tokens,
        ),
        out_specs=(
            tokens,
            tokens,
            row,
            flat_rows,
            flat_rows,
            flat_rows,
            flat_rows,
            flat_rows,
            row,
            row,
            row,
            flat_rows,
            row,
            flat_rows,
            flat_rows,
            flat_rows,
        ),
        check_vma=False,
    )
```

time: 1380 us -> 776 us (0.56)
  waiting for transfers between devices: 925 us -> 82 us
  Pallas kernels: 26.4 us -> 473 us
  matrix products: 147 us -> 8.61 us
  local copies, waits for them, and re-layouts: 70.1 us -> 42.7 us
  blocking collectives: 90.8 us -> 67.2 us
    reduce_scatter x8 -> x5, waiting for transfers between devices: 466 us -> 0.03 us  [the longest x4 0.03 us: reduce_pair(): lax.psum_scatter(term, 'seq', scatter_dimension=0, tiled=True, axis_index...]
    pallas_call x0 -> x5, Pallas kernels: none -> 447 us  [the longest x1 166 us: ffn(): pl.pallas_call(functools.partial(ffn_kernel, n, places), out_shape=[jax.S...]
    unnamed x22 -> x5, waiting for transfers between devices: 246 us -> 0.76 us
    all_gather x10 -> x0, waiting for transfers between devices: 204 us -> none  [the longest x3 62.8 us: shard_weight(): every = lax.all_gather(mine, 'wt', axis=0)]
    dot_general x30 -> x12, matrix products: 147 us -> 8.61 us  [dot(): lax.dot_general(left, right, (((left_dim,), (right_dim,)), ((), ())), pre...]
    all_to_all x6 -> x4, waiting for transfers between devices: 7.31 us -> 70 us  [reduce_pair(): wide = lax.all_to_all(kept, 'wt', split_axis=0, concat_axis=1, tiled=True)]
    all_to_all x3 -> x0, blocking collectives: 57.8 us -> none  [the longest x2 48.7 us: shard_weight(): here = lax.all_to_all(every, 'si', split_axis=0, concat_axis=0, tiled=True)]
    unnamed x0 -> x1, blocking collectives: none -> 47.2 us
  transfers between devices with their start and end apart: 30 -> 16, of which waited for: 22 -> 5; matrix products, arithmetic and copies ran while one was open for 13% -> 7% of each run, Pallas kernels for 1% -> 23%
where the time goes in v2:
time: 776 us; the launch traced here: 763 us
  Pallas kernels  473 us (61%)
  waiting for transfers between devices  82 us (11%)
  blocking collectives  67.2 us (9%)
  starting transfers between devices  44.9 us (6%)
  local copies, waits for them, and re-layouts  42.7 us (6%)
  other arithmetic  28.9 us (4%)
  between operations  15.2 us (2%)
  matrix products  8.61 us (1%)
    pallas_call x1, Pallas kernels, ffn(): pl.pallas_call(functools.partial(ffn_kernel, n, places), out_shape=[jax.S...  166 us
    pallas_call x1, Pallas kernels, leave(): pl.pallas_call(functools.partial(leave_kernel, n, places), out_shape=[jax...  92.1 us
    pallas_call x1, Pallas kernels, back_in(): pl.pallas_call(functools.partial(back_in_kernel, n), out_shape=[jax.Shape...  72.3 us
    all_to_all x4, waiting for transfers between devices, reduce_pair(): wide = lax.all_to_all(kept, 'wt', split_axis=0, concat_axis=1, tiled=True)  70 us
    pallas_call x1, Pallas kernels, close(): pl.pallas_call(functools.partial(close_kernel, n), out_shape=[jax.ShapeDt...  67.4 us
    pallas_call x1, Pallas kernels, enter(): pl.pallas_call(functools.partial(enter_kernel, n), out_shape=[jax.ShapeDt...  49.1 us
    unnamed x1, blocking collectives  47.2 us
    all_to_all x4, starting transfers between devices, reduce_pair(): wide = lax.all_to_all(kept, 'wt', split_axis=0, concat_axis=1, tiled=True)  27.2 us
  transfers between devices with their start and end apart: 16, of which 5 were waited for; matrix products, arithmetic and copies ran while one was open for 7% of the time, Pallas kernels for 23%

profile of v2, /device:TPU:10, one launch (start us, length us, event | category | flops | bytes accessed | tf_op | source)
XLA Modules:
  0.0 762.7 jit_solution(15249869698097727586)
XLA Ops:
  8.5 49.1 %shard_map.288 = (bf16[4,128,2560]{2,1,0:T(8,128)(2,1)}, bf16[4,128,640]{2,1,0:T(8,128)(2,1)}, f32[4,128,640]{2,1,0:T(8,128)}, s32[4,8,128]{2,1,0:T(8,128)}) custom-call(bf16[128,2560]{1,0:T(8,128)(2,1)} %bitcast.232, f32[1,2560]{1,0:T(1,128)} %broadcast_in_dim.54.gain_ref, s32[1,128]{1,0:T(1,128)} %doc_ref.1, bf16[2560,640]{1,0:T(8,128)(2,1)} %win_hbm.3, ...), custom_call_target="tpu_custom_call" | custom-call | flops 49999998976 | bytes 170000000 | tf_op jit(solution)/shard_map/pallas_call | solution.py:537
  58.4 1.9 collective-permute-start.2
  60.3 3.6 collective-permute-start.1
  64.8 1.9 collective-permute-start
  74.8 3.8 collective-permute-start.3
  84.7 14.8 %shard_map.289 = (f32[512,640]{1,0:T(8,128)}, f32[512,640]{1,0:T(8,128)}, f32[512,640]{1,0:T(8,128)}, f32[512,640]{1,0:T(8,128)}) custom-call(s32[1]{0:T(128)} %bitcast.odd, bf16[512,768]{1,0:T(8,128)(2,1)} %maximum_select_fusion.1.c_ref.c_own, bf16[512,768]{1,0:T(8,128)(2,1)} %maximum_select_fusion.1.c_ref.c_own, ...), custom_call_target="tpu_custom_call" | custom-call | tf_op jit(solution)/shard_map/pallas_call | solution.py:144
  101.3 9.9 %all-gather = f32[16,4,640]{2,1,0:T(4,128)S(1)} all-gather(f32[2,4,640]{2,1,0:T(4,128)S(1)} %pad_maximum_fusion.5), channel_id=2, replica_groups=mesh['seq'=8,'wt'=4] {'seq'}, dimensions={0}, use_global_device_ids=true | all-gather | bytes 184320 | tf_op jit(solution)/shard_map/all_gather | solution.py:1135
  112.0 3.4 fusion
  115.4 67.4 %shard_map.290 = (f32[128,2560]{1,0:T(8,128)}, bf16[128,2560]{1,0:T(8,128)(2,1)}, bf16[4,128,2560]{2,1,0:T(8,128)(2,1)}) custom-call(bf16[4,128,640]{2,1,0:T(8,128)(2,1)} %bitcast.209, bf16[128,2560]{1,0:T(8,128)(2,1)} %bitcast.233, f32[1,2560]{1,0:T(1,128)} %broadcast_in_dim.57.gain_ref, bf16[2560,640]{1,0:T(8,128)(2,1)} %w_hbm.1, f32[128,2560]{1,0:T(8,128)} %bitcast.230), custom_call_target="tpu_custom_call" | custom-call | flops 65000001536 | bytes 221000000 | tf_op jit(solution)/shard_map/pallas_call | solution.py:594
  182.8 165.7 %shard_map.291 = (f32[128,2560]{1,0:T(8,128)}, bf16[4,128,1920]{2,1,0:T(8,128)(2,1)}, bf16[1280,1920]{1,0:T(8,128)(2,1)}, bf16[1280,1920]{1,0:T(8,128)(2,1)}, bf16[1280,1920]{1,0:T(8,128)(2,1)}) custom-call(bf16[128,2560]{1,0:T(8,128)(2,1)} %get-tuple-element.47.xn2_ref, bf16[4,128,2560]{2,1,0:T(8,128)(2,1)} %get-tuple-element.48.dm_hbm, ...), custom_call_target="tpu_custom_call" | custom-call | flops 124999999488 | bytes 425000000 | tf_op jit(solution)/shard_map/pallas_call | solution.py:812
  350.7 72.3 %shard_map.292 = (f32[128,2560]{1,0:T(8,128)}, bf16[4,128,2560]{2,1,0:T(8,128)(2,1)}, f32[4,128,640]{2,1,0:T(8,128)}, f32[1,2560]{1,0:T(1,128)}, bf16[128,2560]{1,0:T(8,128)(2,1)}) custom-call(f32[128,2560]{1,0:T(8,128)} %get-tuple-element.49.dxn2_ref, f32[128,2560]{1,0:T(8,128)} %get-tuple-element.50.x1_ref, f32[128,2560]{1,0:T(8,128)} %bitcast.231, ...), custom_call_target="tpu_custom_call" | custom-call | flops 65000001536 | bytes 221000000 | tf_op jit(solution)/shard_map/pallas_call | solution.py:914
  426.8 3.7 fusion.2
  430.5 11.8 %shard_map.293 = (f32[512,640]{1,0:T(8,128)}, f32[512,640]{1,0:T(8,128)}) custom-call(bf16[512,640]{1,0:T(8,128)(2,1)} %get-tuple-element.157.dh_ref, f32[512,640]{1,0:T(8,128)} %copy-done.9), custom_call_target="tpu_custom_call" | custom-call | tf_op jit(solution)/shard_map/pallas_call | solution.py:164
  443.2 10.1 %all-gather.1 = f32[16,4,640]{2,1,0:T(4,128)S(1)} all-gather(f32[2,4,640]{2,1,0:T(4,128)S(1)} %pad_maximum_fusion.4), channel_id=3, replica_groups=mesh['seq'=8,'wt'=4] {'seq'}, dimensions={0}, use_global_device_ids=true | all-gather | bytes 184320 | tf_op jit(solution)/shard_map/all_gather | solution.py:1181
  456.1 2.8 multiply_reduce_fusion
  462.0 6.2 collective-permute-done.4
  478.2 1.9 collective-permute-start.5
  482.6 3.3 concatenate.94
  485.9 1.8 fusion.18.du_ref
  487.8 92.1 %shard_map.294 = (f32[128,2560]{1,0:T(8,128)}, f32[1,2560]{1,0:T(1,128)}, bf16[1280,1920]{1,0:T(8,128)(2,1)}) custom-call(bf16[4,128,640]{2,1,0:T(8,128)(2,1)} %fusion.18.du_ref, bf16[4,128,640]{2,1,0:T(8,128)(2,1)} %bitcast.211, bf16[4,128,640]{2,1,0:T(8,128)(2,1)} %bitcast.210, bf16[128,2560]{1,0:T(8,128)(2,1)} %bitcast.234, ...), custom_call_target="tpu_custom_call" | custom-call | flops 60000002048 | bytes 204000000 | tf_op jit(solution)/shard_map/pallas_call | solution.py:1022
  579.9 6.4 all-to-all-start.3
  586.4 24.7 %all-to-all-done.3 = bf16[4,80,1920]{2,1,0:T(8,128)(2,1)S(1)} async-done(((bf16[4,80,1920]{2,1,0:T(8,128)(2,1)}), bf16[4,80,1920]{2,1,0:T(8,128)(2,1)S(1)}, u32[]{:S(2)}, u32[]{:S(2)}) %all-to-all-start.3) | async-done | bytes 1228832 | tf_op jit(solution)/shard_map/all_to_all | solution.py:1157
  611.1 6.8 all-to-all-start.2
  617.9 25.8 %all-to-all-done.2 = bf16[4,80,1920]{2,1,0:T(8,128)(2,1)S(1)} async-done(((bf16[4,80,1920]{2,1,0:T(8,128)(2,1)}), bf16[4,80,1920]{2,1,0:T(8,128)(2,1)S(1)}, u32[]{:S(2)}, u32[]{:S(2)}) %all-to-all-start.2) | async-done | bytes 1228832 | tf_op jit(solution)/shard_map/all_to_all | solution.py:1157
  643.7 7.5 all-to-all-start.1
  651.5 47.2 %all-reduce = f32[32,160]{1,0:T(8,128)S(1)} all-reduce(f32[32,160]{1,0:T(8,128)S(1)} %pad_maximum_fusion.3), channel_id=4, replica_groups=mesh['seq'=8,'wt'=4] {'seq','wt'}, use_global_device_ids=true, to_apply=%region_0.1.clone | all-reduce | flops 5120 | bytes 40960
  698.7 3.3 collective-permute-start.6
  702.6 4.9 collective-permute-done.6
  709.0 6.5 all-to-all-start
  722.9 19.5 %all-to-all-done = bf16[4,80,1920]{2,1,0:T(8,128)(2,1)} async-done(((bf16[4,80,1920]{2,1,0:T(8,128)(2,1)}), bf16[4,80,1920]{2,1,0:T(8,128)(2,1)}, u32[]{:S(2)}, u32[]{:S(2)}) %all-to-all-start) | async-done | bytes 1228832 | tf_op jit(solution)/shard_map/all_to_all | solution.py:1157
  742.4 2.9 convert_bitcast_fusion.3
  745.3 3.0 reshape.482
  (226 shorter events, 61.3 us)
Async XLA Ops:
  7.2 572.7 %reduce-scatter.14.cloned.1.call-start = ((), (), s32[]{:S(2)}) async-start(), calls=%async_computation.13 | async-start | bytes 6144000 | tf_op jit(solution)/shard_map/reduce_scatter | solution.py:1154
  58.4 13.0 %collective-permute-start.2 = (s32[4,3]{1,0:T(4,128)S(1)}, s32[4,3]{1,0:T(4,128)S(1)}, u32[]{:S(2)}, u32[]{:S(2)}) collective-permute-start(s32[4,3]{1,0:T(4,128)S(1)} %get-tuple-element.174), channel_id=1, source_target_pairs={{0,4},{4,8},{8,12},{12,16},{16,20},{20,24},{24,28},{1,5},{5,9},{9,... | collective-permute-start | bytes 152 | tf_op jit(solution)/shard_map/ppermute | solution.py:1087
  60.3 11.1 %collective-permute-start.1 = (s32[4,3]{1,0:T(4,128)S(1)}, s32[4,3]{1,0:T(4,128)S(1)}, u32[]{:S(2)}, u32[]{:S(2)}) collective-permute-start(s32[4,3]{1,0:T(4,128)S(1)} %get-tuple-element.175), channel_id=1, source_target_pairs={{4,0},{8,4},{12,8},{16,12},{20,16},{24,20},{28,24},{5,1},{9,5},{13... | collective-permute-start | bytes 152 | tf_op jit(solution)/shard_map/ppermute | solution.py:1088
  64.8 7.7 %collective-permute-start = (bf16[4,3,640]{2,1,0:T(4,128)(2,1)S(1)}, bf16[4,3,640]{2,1,0:T(4,128)(2,1)S(1)}, u32[]{:S(2)}, u32[]{:S(2)}) collective-permute-start(bf16[4,3,640]{2,1,0:T(4,128)(2,1)S(1)} %slice.330), channel_id=1, source_target_pairs={{0,4},{4,8},{8,12},{12,16},{16,20},{20,24},{24,28},{1,5},{5,9},{9,... | collective-permute-start | bytes 46088 | tf_op jit(solution)/shard_map/ppermute | solution.py:1107
  71.4 3.2 copy-start.26
  71.4 3.2 copy-start.28
  73.7 6.7 copy-start.43
  74.8 9.9 %copy-start.2 = (bf16[4,128,640]{2,1,0:T(8,128)(2,1)}, bf16[4,128,640]{2,1,0:T(8,128)(2,1)S(1)}, u32[]{:S(2)}) copy-start(bf16[4,128,640]{2,1,0:T(8,128)(2,1)S(1)} %add_convert_fusion) | copy-start | bytes 1966084
  74.8 8.8 %collective-permute-start.3 = (bf16[512,128]{1,0:T(8,128)(2,1)S(1)}, bf16[512,128]{1,0:T(8,128)(2,1)S(1)}, u32[]{:S(2)}, u32[]{:S(2)}) collective-permute-start(bf16[512,128]{1,0:T(8,128)(2,1)S(1)} %slice_select_fusion.3), channel_id=1, source_target_pairs={{0,1},{1,0},{2,3},{3,2},{4,5},{5,4},{6,7},{7,6},{8,9},{9,8},{10,11... | collective-permute-start | bytes 393224 | tf_op jit(solution)/shard_map/ppermute | solution.py:46
  84.7 27.3 %copy-start.10 = (f32[4,128,640]{2,1,0:T(8,128)S(1)}, f32[4,128,640]{2,1,0:T(8,128)}, u32[]{:S(2)}) copy-start(f32[4,128,640]{2,1,0:T(8,128)} %get-tuple-element.46) | copy-start | bytes 3932164
  112.0 3.4 copy-start.22
  348.6 237.8 %reduce-scatter.12.cloned.1.call-start = ((), (), s32[]{:S(2)}) async-start(), calls=%async_computation.12 | async-start | bytes 6144000 | tf_op jit(solution)/shard_map/reduce_scatter | solution.py:1154
  349.4 268.5 %reduce-scatter.10.cloned.1.call-start = ((), (), s32[]{:S(2)}) async-start(), calls=%async_computation.11 | async-start | bytes 6144000 | tf_op jit(solution)/shard_map/reduce_scatter | solution.py:1154
  350.6 348.1 %reduce-scatter.8.cloned.1.call-start = ((), (), s32[]{:S(2)}) async-start(), calls=%async_computation.10 | async-start | bytes 921600 | tf_op jit(solution)/shard_map/reduce_scatter | solution.py:1243
  426.8 26.5 %copy-start.8 = (f32[512,640]{1,0:T(8,128)S(1)}, f32[512,640]{1,0:T(8,128)}, u32[]{:S(2)}) copy-start(f32[512,640]{1,0:T(8,128)} %get-tuple-element.44) | copy-start | bytes 3932164
  430.5 12.7 %copy-start.25 = (f32[4,1,640]{2,0,1:T(4,128)S(1)}, f32[4,1,640]{2,0,1:T(4,128)}, u32[]{:S(2)}) copy-start(f32[4,1,640]{2,0,1:T(4,128)} %copy-done.24) | copy-start | bytes 30724
  430.5 22.8 %copy-start.7 = (f32[512,640]{1,0:T(8,128)S(1)}, f32[512,640]{1,0:T(8,128)}, u32[]{:S(2)}) copy-start(f32[512,640]{1,0:T(8,128)} %get-tuple-element.45) | copy-start | bytes 3932164
  430.5 22.8 %copy-start.23 = (f32[4,640]{1,0:T(4,128)S(1)}, f32[4,640]{1,0:T(4,128)}, u32[]{:S(2)}) copy-start(f32[4,640]{1,0:T(4,128)} %copy-done.22) | copy-start | bytes 30724
  459.6 8.6 %collective-permute-start.4 = (bf16[1024,128]{1,0:T(8,128)(2,1)S(1)}, bf16[1024,128]{1,0:T(8,128)(2,1)S(1)}, u32[]{:S(2)}, u32[]{:S(2)}) collective-permute-start(bf16[1024,128]{1,0:T(8,128)(2,1)S(1)} %fusion.43), channel_id=1, source_target_pairs={{0,1},{1,0},{2,3},{3,2},{4,5},{5,4},{6,7},{7,6},{8,9},{9,8},{10,11... | collective-permute-start | bytes 786440 | tf_op jit(solution)/shard_map/ppermute | solution.py:46
  478.2 7.7 %collective-permute-start.5 = (f32[4,3,640]{2,1,0:T(4,128)S(1)}, f32[4,3,640]{2,1,0:T(4,128)S(1)}, u32[]{:S(2)}, u32[]{:S(2)}) collective-permute-start(f32[4,3,640]{2,1,0:T(4,128)S(1)} %slice.482), channel_id=1, source_target_pairs={{4,0},{8,4},{12,8},{16,12},{20,16},{24,20},{28,24},{5,1},{9,5},{13... | collective-permute-start | bytes 92168 | tf_op jit(solution)/shard_map/ppermute | solution.py:1206
  482.5 3.4 copy-start.27
  482.5 3.4 copy-start.29
  482.5 3.4 copy-start.31
  482.5 3.4 copy-start.33
  485.8 223.1 %reduce-scatter.6.cloned.1.call-start = ((), (), s32[]{:S(2)}) async-start(), calls=%async_computation.9 | async-start | bytes 6144000 | tf_op jit(solution)/shard_map/reduce_scatter | solution.py:1154
  579.9 31.2 %all-to-all-start.3 = ((bf16[4,80,1920]{2,1,0:T(8,128)(2,1)}), bf16[4,80,1920]{2,1,0:T(8,128)(2,1)S(1)}, u32[]{:S(2)}, u32[]{:S(2)}) async-start(bf16[4,80,1920]{2,1,0:T(8,128)(2,1)} %bitcast.204), calls=%async_computation.8 | async-start | bytes 2457600 | tf_op jit(solution)/shard_map/all_to_all | solution.py:1157
  611.1 32.6 %all-to-all-start.2 = ((bf16[4,80,1920]{2,1,0:T(8,128)(2,1)}), bf16[4,80,1920]{2,1,0:T(8,128)(2,1)S(1)}, u32[]{:S(2)}, u32[]{:S(2)}) async-start(bf16[4,80,1920]{2,1,0:T(8,128)(2,1)} %bitcast.203), calls=%async_computation.6 | async-start | bytes 2457600 | tf_op jit(solution)/shard_map/all_to_all | solution.py:1157
  617.9 33.3 %copy-start.44 = (f32[1,2560]{1,0:T(1,128)S(1)}, f32[1,2560]{1,0:T(1,128)}, u32[]{:S(2)}) copy-start(f32[1,2560]{1,0:T(1,128)} %get-tuple-element.63) | copy-start | bytes 30724
  617.9 33.4 %copy-start.45 = (f32[1,2560]{1,0:T(1,128)S(1)}, f32[1,2560]{1,0:T(1,128)}, u32[]{:S(2)}) copy-start(f32[1,2560]{1,0:T(1,128)} %get-tuple-element.62) | copy-start | bytes 30724
  643.7 65.3 %all-to-all-start.1 = ((bf16[4,80,1920]{2,1,0:T(8,128)(2,1)}), bf16[4,80,1920]{2,1,0:T(8,128)(2,1)}, u32[]{:S(2)}, u32[]{:S(2)}) async-start(bf16[4,80,1920]{2,1,0:T(8,128)(2,1)} %bitcast.202), calls=%async_computation.4 | async-start | bytes 2457600 | tf_op jit(solution)/shard_map/all_to_all | solution.py:1157
  698.7 8.8 %collective-permute-start.6 = (bf16[80,519]{1,0:T(8,128)(2,1)}, bf16[80,519]{1,0:T(8,128)(2,1)S(1)}, u32[]{:S(2)}, u32[]{:S(2)}) collective-permute-start(bf16[80,519]{1,0:T(8,128)(2,1)} %reduce-scatter.8.cloned.1.call-done), channel_id=1, source_target_pairs={{0,0},{1,8},{2,16},{3,24},{4,1},{5,9},{6,17},{7,25},{8,2},{9,10},{... | collective-permute-start | bytes 249128 | tf_op jit(solution)/shard_map/ppermute | solution.py:1247
  709.0 33.5 %all-to-all-start = ((bf16[4,80,1920]{2,1,0:T(8,128)(2,1)}), bf16[4,80,1920]{2,1,0:T(8,128)(2,1)}, u32[]{:S(2)}, u32[]{:S(2)}) async-start(bf16[4,80,1920]{2,1,0:T(8,128)(2,1)} %bitcast.205), calls=%async_computation.1 | async-start | bytes 2457600 | tf_op jit(solution)/shard_map/all_to_all | solution.py:1157
  (31 other events, 57.8 us)
Sparse Core Ops, SparseCore 0:
  348.7 58.6 reduce-scatter.13
  410.5 58.7 reduce-scatter.11
  472.3 59.0 reduce-scatter.9
  535.1 35.7 reduce-scatter.7
  580.0 59.9 reduce-scatter.5

commit v3 on v2

--- a/solution.py
+++ b/solution.py
@@ -184,7 +184,7 @@
     )
 
 
-def greet(n, me, pair=False):
+def greet(n, me, pair=False, bits=0, places=0):
     barrier = pltpu.get_barrier_semaphore()
 
     @pl.when(me > 0)
@@ -196,11 +196,20 @@
         pl.semaphore_signal(barrier, 1, device_id={"wt": me + 1}, device_id_type=MESH)
 
     peers = (me > 0).astype(jnp.int32) + (me < n - 1).astype(jnp.int32)
+    place = lax.axis_index("seq")
+    if places:
+        peers = peers + places - 1
+        for by in range(1, places):
+            other = {"seq": lax.rem(place + by, places)}
+            pl.semaphore_signal(barrier, 1, device_id=other, device_id_type=MESH)
     if pair:
-        place = lax.axis_index("seq")
         other = {"seq": place + 1 - 2 * lax.rem(place, 2)}
         pl.semaphore_signal(barrier, 1, device_id=other, device_id_type=MESH)
-        peers = peers + 1
+        peers = peers + 1 + bits
+        for k in range(1, bits + 1):
+            step = 1 << k
+            other = {"seq": place + step * (1 - 2 * lax.rem(place // step, 2))}
+            pl.semaphore_signal(barrier, 1, device_id=other, device_id_type=MESH)
     pl.semaphore_wait(barrier, peers)
 
 
@@ -307,64 +316,37 @@
         total = self.parts[q].astype(FULL) + self.slots[side, k].astype(FULL)
         self.parts[q] = total.astype(LOW)
 
-    def start(self, partial, early=True):
-        n, me = self.n, self.me
-
-        def first(k, carry):
-            def side(which, inner):
-                q = jnp.where(which == 0, n - 1 - k, k)
-
-                @pl.when(jnp.where(which == 0, q > me, q < me))
+    def prepare(self, k, partial):
+        def side(which, carry):
+            q = jnp.where(which == 0, self.n - 1 - k, k)
+
+            @pl.when(jnp.where(which == 0, q > self.me, q < self.me))
+            def _():
+                partial(q)
+
+            return carry
+
+        lax.fori_loop(0, 2, side, 0)
+
+    def step(self, t):
+        n = self.n
+        for side in range(2):
+            place = self.me if side == 0 else n - 1 - self.me
+            k = t - place
+            pull = self.rightward if side == 0 else self.leftward
+
+            @pl.when((k >= 0) & (t <= n - 2))
+            def _():
+                @pl.when(place > 0)
                 def _():
-                    partial(q)
-
-                return inner
-
-            lax.fori_loop(0, 2, side, 0)
-
-            @pl.when((k == 0) & (me == 0) & early)
-            def _():
-                self.rightward(0).start()
-
-            @pl.when((k == 0) & (me == n - 1) & early)
-            def _():
-                self.leftward(0).start()
-
-            return carry
-
-        lax.fori_loop(0, n - 1, first, 0)
-        partial(me)
-
-    def relay(self, k):
-        n, me = self.n, self.me
-
-        @pl.when(n - 1 - k > me)
-        def _():
-            @pl.when(me > 0)
-            def _():
-                self.arrived(0, k)
-                self.add(n - 1 - k, 0, k)
-
-            if k > 0:
-                self.rightward(k - 1).wait_send()
-
-            @pl.when((me > 0) | (k > 0))
-            def _():
-                self.rightward(k).start()
-
-        @pl.when(k < me)
-        def _():
-            @pl.when(me < n - 1)
-            def _():
-                self.arrived(1, k)
-                self.add(k, 1, k)
-
-            if k > 0:
-                self.leftward(k - 1).wait_send()
-
-            @pl.when((me < n - 1) | (k > 0))
-            def _():
-                self.leftward(k).start()
+                    self.arrived(side, k)
+                    self.add(n - 1 - k if side == 0 else k, side, k)
+
+                @pl.when(k > 0)
+                def _():
+                    pull(k - 1).wait_send()
+
+                pull(k).start()
 
     def total(self):
         n, me = self.n, self.me
@@ -441,12 +423,20 @@
             self.sends(side, self.n - 1, lambda copy: copy.wait_send())
 
 
-def line_reduce(n, me, parts, slots, sent, landed, partial, between, finish):
+def line_reduce(n, me, parts, slots, sent, landed, partial, work, finish):
     line = LineReduce(n, me, parts, slots, sent, landed)
-    line.start(partial)
-    for k in range(n - 1):
-        line.relay(k)
-        between(k)
+    line.prepare(0, partial)
+    line.step(0)
+    for k in range(1, n - 1):
+        line.prepare(k, partial)
+    line.step(1)
+    partial(me)
+    share = -(-len(work) // (n - 2))
+    for t in range(2, n):
+        for task in work[(t - 2) * share : (t - 1) * share]:
+            task()
+        if t < n - 1:
+            line.step(t)
     finish(line.total())
     line.finish()
 
@@ -582,9 +572,12 @@
     back = LineReduce(n, me, parts, slots, sent, landed)
     both = LineBoth(LineGather(n, me, dm_ref, gsent, glanded), back)
     both.step(0)
-    back.start(partial, False)
+    for k in range(n - 1):
+        back.prepare(k, partial)
     for t in range(1, n):
         both.step(t)
+        if t == 1:
+            partial(me)
     finish(back.total())
     both.finish()
 
@@ -612,12 +605,13 @@
 
 
 class PairSum:
-    def __init__(self, part, halves, landing, sent, landed, free, flush, tag):
+    def __init__(self, part, halves, landing, sent, landed, free, flush):
         self.me = lax.axis_index("seq")
         self.mine = lax.rem(self.me, 2)
         self.part, self.halves, self.landing = part, halves, landing
         self.sent, self.landed, self.free, self.flush = sent, landed, free, flush
-        self.count = tag
+        self.count = 0
+        self.pending = None
 
     def other(self):
         return {"seq": self.me + 1 - 2 * self.mine}
@@ -632,40 +626,45 @@
             device_id_type=MESH,
         )
 
-    def run(self, steps, compute, target):
+    def out(self, slot, t, target):
         half = self.landing.shape[1]
-        for t in range(steps):
-            slot = self.count % 2
-
-            def out(slot, t):
-                return pltpu.make_async_copy(
-                    self.halves.at[slot, self.mine],
-                    target.at[pl.ds(t * half, half), :],
-                    self.flush.at[slot],
-                )
-
-            if self.count >= 2:
-                self.send(slot).wait_send()
-                pltpu.make_async_copy(
-                    self.halves.at[slot, self.mine], target.at[pl.ds(0, half), :], self.flush.at[slot]
-                ).wait()
-                pl.semaphore_wait(self.free, 1)
-            compute(t, self.halves.at[slot])
-            self.send(slot).start()
-            self.send(slot).wait_recv()
-            total = self.halves[slot, self.mine].astype(FULL) + self.landing[slot].astype(FULL)
-            self.halves[slot, self.mine] = total.astype(LOW)
-            pl.semaphore_signal(self.free, 1, device_id=self.other(), device_id_type=MESH)
-            out(slot, t).start()
-            self.count += 1
+        return pltpu.make_async_copy(
+            self.halves.at[slot, self.mine],
+            target.at[pl.ds(t * half, half), :],
+            self.flush.at[slot],
+        )
+
+    def tasks(self, steps, compute, target):
+        return [functools.partial(self.run, t, compute, target) for t in range(steps)]
+
+    def run(self, t, compute, target):
+        slot = self.count % 2
+        if self.count >= 2:
+            self.send(slot).wait_send()
+            self.out(slot, 0, target).wait()
+            pl.semaphore_wait(self.free, 1)
+        compute(t, self.halves.at[slot])
+        self.send(slot).start()
+        self.settle()
+        self.pending = (slot, t, target)
+        self.count += 1
+
+    def settle(self):
+        if self.pending is None:
+            return
+        slot, t, target = self.pending
+        self.send(slot).wait_recv()
+        total = self.halves[slot, self.mine].astype(FULL) + self.landing[slot].astype(FULL)
+        self.halves[slot, self.mine] = total.astype(LOW)
+        pl.semaphore_signal(self.free, 1, device_id=self.other(), device_id_type=MESH)
+        self.out(slot, t, target).start()
+        self.pending = None
 
     def finish(self, target):
-        half = self.landing.shape[1]
+        self.settle()
         for slot in range(2):
             self.send(slot).wait_send()
-            pltpu.make_async_copy(
-                self.halves.at[slot, self.mine], target.at[pl.ds(0, half), :], self.flush.at[slot]
-            ).wait()
+            self.out(slot, 0, target).wait()
         pl.semaphore_wait(self.free, 2)
 
 
@@ -703,6 +702,82 @@
         tiles(width, tile_of(width, 640), tile)
 
     return compute
+
+
+def column_halves(width):
+    first = -(-width // 256) * 128
+    return [(0, first), (first, width - first)]
+
+
+class PlaneReduce:
+    def __init__(self, blocks, landings, sent, landed):
+        self.blocks, self.landings, self.sent, self.landed = blocks, landings, sent, landed
+        self.bits = len(blocks.shape) - 3
+        self.me = lax.axis_index("seq")
+        self.columns = column_halves(blocks.shape[-1])
+
+    def bit(self, dim):
+        return 1 << (self.bits - dim)
+
+    def mine(self, dim):
+        return lax.rem(self.me // self.bit(dim), 2)
+
+    def order(self, side):
+        dims = list(range(self.bits))
+        return dims[::-1] if side == 0 else dims
+
+    def peer(self, dim):
+        return {"seq": self.me + self.bit(dim) * (1 - 2 * self.mine(dim))}
+
+    def index(self, side, step, own):
+        order = self.order(side)
+        place = [slice(None)] * self.bits
+        for dim in order[:step]:
+            place[dim] = self.mine(dim)
+        now = order[step]
+        place[now] = self.mine(now) if own else 1 - self.mine(now)
+        return tuple(place) + (slice(None), slice(None), pl.ds(*self.columns[side]))
+
+    def send(self, side, step):
+        return pltpu.make_async_remote_copy(
+            src_ref=self.blocks.at[self.index(side, step, False)],
+            dst_ref=self.landings[2 * step + side],
+            send_sem=self.sent.at[side, step],
+            recv_sem=self.landed.at[side, step],
+            device_id=self.peer(self.order(side)[step]),
+            device_id_type=MESH,
+        )
+
+    def begin(self):
+        for side in range(2):
+            self.send(side, 0).start()
+
+    def advance(self, step):
+        for side in range(2):
+            self.send(side, step).wait_recv()
+            at = self.index(side, step, True)
+            total = self.blocks[at].astype(FULL) + self.landings[2 * step + side][...].astype(FULL)
+            self.blocks[at] = total.astype(LOW)
+            if step + 1 < self.bits:
+                self.send(side, step + 1).start()
+
+    def kept(self):
+        return self.blocks.at[tuple(self.mine(dim) for dim in range(self.bits))]
+
+    def finish(self):
+        for step in range(self.bits):
+            for side in range(2):
+                self.send(side, step).wait_send()
+
+
+def plane_scratch(shape):
+    bits = len(shape) - 3
+    landings = []
+    for step in range(bits):
+        for _, width in column_halves(shape[-1]):
+            rest = [2] * (bits - 1 - step) + [shape[-3], shape[-2], width]
+            landings.append(pltpu.VMEM(tuple(rest), LOW))
+    return landings
 
 
 def ffn_kernel(
@@ -715,8 +790,9 @@
     wd_hbm,
     dxn2_ref,
     hidden_hbm,
-    gate_hbm,
-    up_hbm,
+    dg_hbm,
+    dv_hbm,
+    xall_hbm,
     down_hbm,
     xall,
     dm,
@@ -775,8 +851,14 @@
         tiles(units, cut, tile)
 
     line_gather(n, me, xall, gsent, glanded, use, ready)
-    out = pltpu.make_async_copy(hidden, hidden_hbm, flush.at[0])
-    out.start()
+    outs = [
+        pltpu.make_async_copy(source, target, flush.at[k])
+        for k, (source, target) in enumerate(
+            [(hidden, hidden_hbm), (dg, dg_hbm), (dv, dv_hbm), (xall, xall_hbm)]
+        )
+    ]
+    for out in outs:
+        out.start()
 
     def partial(q):
         def tile(at):
@@ -787,22 +869,17 @@
 
     part = model // places
     size = pair_tile(model, places)
-    pair = PairSum(part, halves, landing, psent, planded, free, pflush, 0)
-
-    def between(k):
-        if k == 0:
-            pair.run(model // size, pair_dot(dm, hidden, part, size), down_hbm)
-        if k == 1:
-            pair.run(model // size, pair_dot(xall, dg, part, size), gate_hbm)
-        if k == n - 2:
-            pair.run(model // size, pair_dot(xall, dv, part, size), up_hbm)
+    pair = PairSum(part, halves, landing, psent, planded, free, pflush)
+
+    work = pair.tasks(model // size, pair_dot(dm, hidden, part, size), down_hbm)
 
     def finish(total):
         dxn2_ref[...] = total
 
-    line_reduce(n, me, parts, slots, rsent, rlanded, partial, between, finish)
-    pair.finish(up_hbm)
-    out.wait()
+    line_reduce(n, me, parts, slots, rsent, rlanded, partial, work, finish)
+    pair.finish(down_hbm)
+    for out in outs:
+        out.wait()
 
 
 def ffn(n, places, xn2, dm, wg, wu, wd):
@@ -814,12 +891,13 @@
         out_shape=[
             jax.ShapeDtypeStruct((rows, model), FULL),
             jax.ShapeDtypeStruct((n, rows, units), LOW),
-            grad,
-            grad,
+            jax.ShapeDtypeStruct((n, rows, units), LOW),
+            jax.ShapeDtypeStruct((n, rows, units), LOW),
+            jax.ShapeDtypeStruct((n, rows, model), LOW),
             grad,
         ],
         in_specs=[VMEM, ANY, ANY, ANY, ANY],
-        out_specs=[VMEM, ANY, ANY, ANY, ANY],
+        out_specs=[VMEM, ANY, ANY, ANY, ANY, ANY],
         scratch_shapes=[
             pltpu.VMEM((n, rows, model), LOW),
             pltpu.VMEM((n, rows, model), LOW),
@@ -835,41 +913,25 @@
         + pair_scratch(pair_tile(model, places) // 2, units)
         + gather_sems(n)
         + reduce_sems(n)
-        + [pltpu.SemaphoreType.DMA((4,)), pltpu.SemaphoreType.DMA((1,))],
+        + [pltpu.SemaphoreType.DMA((4,)), pltpu.SemaphoreType.DMA((4,))],
         compiler_params=comm_params(2),
         cost_estimate=lasting(125),
     )(xn2, dm, wg, wu, wd)
 
 
-def back_in_kernel(
-    n,
-    dxn2_ref,
-    x1_ref,
-    slope_ref,
-    gain_ref,
-    w_hbm,
-    hidden_hbm,
-    wd_hbm,
-    dx1_ref,
-    dz_ref,
-    do_ref,
-    sum_ref,
-    out_ref,
-    w,
-    hidden,
-    wd,
-    parts,
-    slots,
-    sent,
-    landed,
-    rsent,
-    rlanded,
-    local,
-):
+def back_in_kernel(n, places, bits, *refs):
+    dxn2_ref, x1_ref, slope_ref, gain_ref, *sources = refs[:11]
+    dx1_ref, dz_ref, do_ref, sum_ref, out_ref, kept_ref, gate_hbm, up_hbm = refs[11:19]
+    w, hidden, wd, xall, dg, dv, blocks = refs[19:26]
+    landings = refs[26 : 26 + 2 * bits]
+    parts, slots, *sems = refs[26 + 2 * bits :]
+    halves, landing, psent, planded, free, pflush, sent, landed, rsent, rlanded, bsent, blanded, local = sems
     me = lax.axis_index("wt")
     loads = [
         pltpu.make_async_copy(source, target, local.at[k])
-        for k, (source, target) in enumerate([(w_hbm, w), (hidden_hbm, hidden), (wd_hbm, wd)])
+        for k, (source, target) in enumerate(
+            zip(sources, [blocks, w, wd, hidden, xall, dg, dv])
+        )
     ]
     for load in loads:
         load.start()
@@ -882,13 +944,16 @@
     dx1 = slope_ref[...] + scale * (q2 - x1 * (scale * scale * pull))
     dx1_ref[...] = dx1
     dz_ref[me] = dx1.astype(LOW)
-    greet(n, me)
+    greet(n, me, True, bits)
     line = LineGather(n, me, dz_ref, sent, landed)
     back = LineReduce(n, me, parts, slots, rsent, rlanded)
     both = LineBoth(line, back)
     both.step(0)
+    loads[0].wait()
+    plane = PlaneReduce(blocks, landings, bsent, blanded)
+    plane.begin()
     sum_ref[...] = jnp.sum(dxn2 * x1 * scale, axis=0, keepdims=True)
-    for load in loads:
+    for load in loads[1:]:
         load.wait()
 
     def use(q):
@@ -900,41 +965,105 @@
 
         tiles(model, tile_of(model, 512), tile)
 
-    back.start(partial, False)
+    part = model // places
+    size = pair_tile(model, places)
+    pair = PairSum(part, halves, landing, psent, planded, free, pflush)
+    for k in range(n - 1):
+        back.prepare(k, partial)
+    partial(me)
     use(me)
+    work = pair.tasks(model // size, pair_dot(xall, dg, part, size), gate_hbm)
+    work += pair.tasks(model // size, pair_dot(xall, dv, part, size), up_hbm)
+    share = -(-len(work) // (n - 1))
     for t in range(1, n):
         both.step(t)
+        if t >= 2 and t - 2 < bits:
+            plane.advance(t - 2)
         line.each(t, use)
+        for task in work[(t - 1) * share : t * share]:
+            task()
+    for step in range(max(n - 2, 0), bits):
+        plane.advance(step)
     out_ref[...] = (x1_ref[...] + back.total()).astype(LOW)
+    kept_ref[...] = plane.kept()[...]
+    pair.finish(up_hbm)
     both.finish()
-
-
-def back_in(n, dxn2, x1, slope, gain, weight, hidden, wd):
+    plane.finish()
+
+
+def back_in(n, places, dxn2, x1, slope, gain, down, weight, wd, hidden, xall, dg, dv):
     rows, model = x1.shape
+    bits = len(down.shape) - 3
+    grad = jax.ShapeDtypeStruct((model // 2, wd.shape[1]), LOW)
     return pl.pallas_call(
-        functools.partial(back_in_kernel, n),
+        functools.partial(back_in_kernel, n, places, bits),
         out_shape=[
             jax.ShapeDtypeStruct((rows, model), FULL),
             jax.ShapeDtypeStruct((n, rows, model), LOW),
             jax.ShapeDtypeStruct((n, rows, weight.shape[1]), FULL),
             jax.ShapeDtypeStruct((1, model), FULL),
             jax.ShapeDtypeStruct((rows, model), LOW),
+            jax.ShapeDtypeStruct(down.shape[bits:], LOW),
+            grad,
+            grad,
         ],
-        in_specs=[VMEM] * 4 + [ANY] * 3,
-        out_specs=[VMEM] * 5,
+        in_specs=[VMEM] * 4 + [ANY] * 7,
+        out_specs=[VMEM] * 6 + [ANY] * 2,
         scratch_shapes=[
             pltpu.VMEM(weight.shape, LOW),
             pltpu.VMEM(hidden.shape, LOW),
             pltpu.VMEM(wd.shape, LOW),
+            pltpu.VMEM(xall.shape, LOW),
+            pltpu.VMEM(dg.shape, LOW),
+            pltpu.VMEM(dv.shape, LOW),
+            pltpu.VMEM(down.shape, LOW),
+        ]
+        + plane_scratch(down.shape)
+        + [
             pltpu.VMEM((n, rows, model), LOW),
             pltpu.VMEM((2, n - 1, rows, model), LOW),
         ]
+        + pair_scratch(pair_tile(model, places) // 2, wd.shape[1])
         + gather_sems(n)
         + reduce_sems(n)
-        + [pltpu.SemaphoreType.DMA((3,))],
+        + [
+            pltpu.SemaphoreType.DMA((2, bits)),
+            pltpu.SemaphoreType.DMA((2, bits)),
+            pltpu.SemaphoreType.DMA((7,)),
+        ],
         compiler_params=comm_params(3),
-        cost_estimate=lasting(65),
-    )(dxn2, x1, slope, gain, weight, hidden, wd)
+        cost_estimate=lasting(75),
+    )(dxn2, x1, slope, gain, down, weight, wd, hidden, xall, dg, dv)
+
+
+class PlaneShare:
+    def __init__(self, places, source, lands, sent, landed):
+        self.places, self.source, self.lands = places, source, lands
+        self.sent, self.landed = sent, landed
+        self.me = lax.axis_index("seq")
+
+    def send(self, by):
+        to = lax.rem(self.me + by, self.places)
+        return pltpu.make_async_remote_copy(
+            src_ref=self.source.at[to],
+            dst_ref=self.lands.at[by],
+            send_sem=self.sent.at[by],
+            recv_sem=self.landed.at[by],
+            device_id={"seq": to},
+            device_id_type=MESH,
+        )
+
+    def start(self):
+        self.lands[0] = self.source[self.me]
+        for by in range(1, self.places):
+            self.send(by).start()
+
+    def finish(self, target):
+        for by in range(1, self.places):
+            self.send(by).wait_recv()
+        target[...] = jnp.sum(self.lands[...].astype(FULL), axis=0)
+        for by in range(1, self.places):
+            self.send(by).wait_send()
 
 
 def leave_kernel(
@@ -950,9 +1079,12 @@
     dz_hbm,
     win_hbm,
     wbr_hbm,
+    after_hbm,
+    small_ref,
     grad_ref,
     sum_ref,
     mix_hbm,
+    passed_ref,
     xn,
     dz,
     win,
@@ -967,6 +1099,9 @@
     pflush,
     sent,
     landed,
+    lands,
+    ssent,
+    slanded,
     local,
 ):
     me = lax.axis_index("wt")
@@ -978,7 +1113,9 @@
     ]
     for load in loads:
         load.start()
-    greet(n, me, True)
+    greet(n, me, False, 0, places)
+    small = PlaneShare(places, small_ref, lands, ssent, slanded)
+    small.start()
     for load in loads:
         load.wait()
     model = win.shape[0]
@@ -993,16 +1130,14 @@
     part = model // places
     size = pair_tile(model, places)
     width = du_ref.shape[2]
-    pair = PairSum(part, halves, landing, psent, planded, free, pflush, 0)
+    pair = PairSum(part, halves, landing, psent, planded, free, pflush)
 
     def compute(t, target):
         for k, (left, right) in enumerate([(dz, o_ref), (xn, dy_ref), (xn, du_ref)]):
             columns = pl.ds(k * width, width)
             pair_dot(left, right, part, size)(t, target.at[:, :, columns])
 
-    def between(k):
-        if k == 0:
-            pair.run(model // size, compute, mix_hbm)
+    work = pair.tasks(model // size, compute, mix_hbm)
 
     def finish(total):
         flat = x_ref[...].astype(FULL)
@@ -1012,11 +1147,12 @@
         grad_ref[...] = dx1_ref[...] + scale * (q1 - flat * (scale * scale * pull))
         sum_ref[...] = jnp.sum(total * flat * scale, axis=0, keepdims=True)
 
-    line_reduce(n, me, parts, slots, sent, landed, partial, between, finish)
+    line_reduce(n, me, parts, slots, sent, landed, partial, work, finish)
     pair.finish(mix_hbm)
-
-
-def leave(n, places, du, dy, o, x, dx1, gain, xn, dz, win, wbr):
+    small.finish(passed_ref)
+
+
+def leave(n, places, du, dy, o, x, dx1, gain, xn, dz, win, wbr, after, small):
     rows, model = x.shape
     width = win.shape[1]
     return pl.pallas_call(
@@ -1025,9 +1161,10 @@
             jax.ShapeDtypeStruct((rows, model), FULL),
             jax.ShapeDtypeStruct((1, model), FULL),
             jax.ShapeDtypeStruct((model // 2, 3 * width), LOW),
+            jax.ShapeDtypeStruct(small.shape[1:], FULL),
         ],
-        in_specs=[VMEM] * 6 + [ANY] * 4,
-        out_specs=[VMEM, VMEM, ANY],
+        in_specs=[VMEM] * 6 + [ANY] * 5 + [VMEM],
+        out_specs=[VMEM, VMEM, ANY, VMEM],
         scratch_shapes=[
             pltpu.VMEM((n, rows, model), LOW),
             pltpu.VMEM((n, rows, model), LOW),
@@ -1038,10 +1175,171 @@
         ]
         + pair_scratch(pair_tile(model, places) // 2, 3 * width)
         + reduce_sems(n)
-        + [pltpu.SemaphoreType.DMA((4,))],
+        + [
+            pltpu.VMEM(small.shape, LOW),
+            pltpu.SemaphoreType.DMA((places,)),
+            pltpu.SemaphoreType.DMA((places,)),
+            pltpu.SemaphoreType.DMA((4,)),
+        ],
         compiler_params=comm_params(4),
         cost_estimate=lasting(60),
-    )(du, dy, o, x, dx1, gain, xn, dz, win, wbr)
+    )(du, dy, o, x, dx1, gain, xn, dz, win, wbr, after, small)
+
+
+class LineSpread:
+    def __init__(self, n, me, source, lands, sent, landed):
+        self.n, self.me, self.source, self.lands = n, me, source, lands
+        self.sent, self.landed = sent, landed
+
+    def send(self, by):
+        to = lax.rem(self.me + by, self.n)
+        return remote(
+            self.source.at[to], self.lands.at[self.me], self.sent.at[by], self.landed.at[by], to
+        )
+
+    def start(self):
+        for by in range(1, self.n):
+            self.send(by).start()
+
+    def take(self, put, own):
+        put(self.me, own[...])
+        for by in range(1, self.n):
+            slot = lax.rem(self.me + self.n - by, self.n)
+            land = self.lands.at[slot]
+            remote(land, land, self.sent.at[by], self.landed.at[by], self.me).wait_recv()
+            put(slot, land[...])
+
+    def finish(self):
+        for by in range(1, self.n):
+            self.send(by).wait_send()
+
+
+def settle_kernel(n, places, bits, gate_hbm, up_hbm, mix_hbm, gains_ref, gate_ref, up_ref, out_ref, branch_ref, in_ref, total_ref, *scratch):
+    blocks, landings, scratch = scratch[0], scratch[1 : 1 + 2 * bits], scratch[1 + 2 * bits :]
+    lands, own, notes, around, psent, planded, ssent, slanded, gsent, glanded, local = scratch
+    me = lax.axis_index("wt")
+    seat = lax.axis_index("seq")
+    loads = [
+        pltpu.make_async_copy(mix_hbm, blocks, local.at[0]),
+        pltpu.make_async_copy(gate_hbm.at[me], own.at[0], local.at[1]),
+        pltpu.make_async_copy(up_hbm.at[me], own.at[1], local.at[2]),
+    ]
+    for load in loads:
+        load.start()
+    notes[me] = gains_ref[...]
+    barrier = pltpu.get_barrier_semaphore()
+    for by in range(1, n):
+        pl.semaphore_signal(
+            barrier, 1, device_id={"wt": lax.rem(me + by, n)}, device_id_type=MESH
+        )
+    for by in range(1, places):
+        pl.semaphore_signal(
+            barrier, 1, device_id={"seq": lax.rem(seat + by, places)}, device_id_type=MESH
+        )
+    pl.semaphore_wait(barrier, n + places - 2)
+    loads[0].wait()
+    plane = PlaneReduce(blocks, landings, psent, planded)
+    plane.begin()
+    spreads = [
+        LineSpread(n, me, source, lands.at[k], ssent.at[k], slanded.at[k])
+        for k, source in enumerate([gate_hbm, up_hbm])
+    ]
+
+    def note(by):
+        to = lax.rem(me + by, n)
+        return remote(notes.at[me], notes.at[me], gsent.at[0, by], glanded.at[0, by], to)
+
+    for by in range(1, n):
+        note(by).start()
+    for spread in spreads:
+        spread.start()
+    for by in range(1, n):
+        slot = notes.at[lax.rem(me + n - by, n)]
+        remote(slot, slot, gsent.at[0, by], glanded.at[0, by], me).wait_recv()
+    around[seat] = jnp.sum(notes[...], axis=0)
+
+    def share(by):
+        to = lax.rem(seat + by, places)
+        return pltpu.make_async_remote_copy(
+            src_ref=around.at[seat],
+            dst_ref=around.at[seat],
+            send_sem=gsent.at[1, by],
+            recv_sem=glanded.at[1, by],
+            device_id={"seq": to},
+            device_id_type=MESH,
+        )
+
+    for by in range(1, places):
+        share(by).start()
+    for step in range(bits):
+        plane.advance(step)
+    kept = plane.kept()
+    last = LineSpread(n, me, kept, lands.at[2], ssent.at[2], slanded.at[2])
+    last.start()
+    for by in range(1, places):
+        slot = around.at[lax.rem(seat + places - by, places)]
+        pltpu.make_async_remote_copy(
+            src_ref=slot,
+            dst_ref=slot,
+            send_sem=gsent.at[1, by],
+            recv_sem=glanded.at[1, by],
+            device_id={"seq": seat},
+            device_id_type=MESH,
+        ).wait_recv()
+    total_ref[...] = jnp.sum(around[...], axis=0)
+    units = gate_hbm.shape[-1]
+    for k, (spread, target) in enumerate(zip(spreads, [gate_ref, up_ref])):
+        loads[1 + k].wait()
+
+        def put(q, value, target=target):
+            target[:, pl.ds(pl.multiple_of(q * units, 128), units)] = value.astype(FULL)
+
+        spread.take(put, own.at[k])
+    width = units // 3
+
+    def put_mix(q, value):
+        columns = pl.ds(pl.multiple_of(q * width, 128), width)
+        for k, target in enumerate([out_ref, branch_ref, in_ref]):
+            target[:, columns] = value[:, k * width : (k + 1) * width].astype(FULL)
+
+    last.take(put_mix, kept.at[me])
+    plane.finish()
+    for spread in spreads + [last]:
+        spread.finish()
+    for by in range(1, n):
+        note(by).wait_send()
+    for by in range(1, places):
+        share(by).wait_send()
+
+
+def settle(n, places, gate, up, mix, gains):
+    _, part, units = gate.shape
+    bits = len(mix.shape) - 3
+    wide = jax.ShapeDtypeStruct((part, n * units), FULL)
+    thin = jax.ShapeDtypeStruct((part, n * units // 3), FULL)
+    return pl.pallas_call(
+        functools.partial(settle_kernel, n, places, bits),
+        out_shape=[wide, wide, thin, thin, thin, jax.ShapeDtypeStruct(gains.shape, FULL)],
+        in_specs=[ANY, ANY, ANY, VMEM],
+        out_specs=[VMEM] * 6,
+        scratch_shapes=[pltpu.VMEM(mix.shape, LOW)]
+        + plane_scratch(mix.shape)
+        + [
+            pltpu.VMEM((3, n, part, units), LOW),
+            pltpu.VMEM((2, part, units), LOW),
+            pltpu.VMEM((n,) + gains.shape, FULL),
+            pltpu.VMEM((places,) + gains.shape, FULL),
+            pltpu.SemaphoreType.DMA((2, bits)),
+            pltpu.SemaphoreType.DMA((2, bits)),
+            pltpu.SemaphoreType.DMA((3, n)),
+            pltpu.SemaphoreType.DMA((3, n)),
+            pltpu.SemaphoreType.DMA((2, max(n, places))),
+            pltpu.SemaphoreType.DMA((2, max(n, places))),
+            pltpu.SemaphoreType.DMA((3,)),
+        ],
+        compiler_params=comm_params(5),
+        cost_estimate=lasting(100),
+    )(gate, up, mix, gains)
 
 
 def on_device(
@@ -1145,30 +1443,40 @@
     gelu_y, grad_y = gelu_both(y)
     o = (hr * gelu_y).astype(LOW)
     x1, xn2, dm = close(shards, o.reshape(u3.shape), x, second_gain[None], output_weight, slope)
-    dxn2, hidden, gate_term, up_term, down_term = ffn(
+    dxn2, hidden, dg, dv, xn2, down_term = ffn(
         shards, places, xn2, dm, gate_weight, up_weight, down_weight
     )
     groups = [list(range(k, places, 2)) for k in range(2)]
 
-    def reduce_pair(term):
-        kept = lax.psum_scatter(
+    def summed(term):
+        return lax.psum_scatter(
             term, "seq", scatter_dimension=0, tiled=True, axis_index_groups=groups
         )
-        wide = lax.all_to_all(kept, "wt", split_axis=0, concat_axis=1, tiled=True)
-        return wide.astype(FULL)
-
-    def reduce(term):
-        kept = lax.psum_scatter(term.astype(LOW), "seq", scatter_dimension=0, tiled=True)
-        wide = lax.all_to_all(kept, "wt", split_axis=0, concat_axis=1, tiled=True)
-        return wide.astype(FULL)
-
-    gate_grad = reduce_pair(gate_term)
-    up_grad = reduce_pair(up_term)
-    down_grad = reduce_pair(down_term)
-
-    dx1, dz, do, second_gain_grad, block_out = back_in(
-        shards, dxn2, x1, slope, second_gain[None], output_weight, hidden, down_weight
-    )
+
+    def spread(kept):
+        return lax.all_to_all(kept, "wt", split_axis=0, concat_axis=1, tiled=True)
+
+    part = model // (places * shards)
+    bits = (places // 2 - 1).bit_length()
+    dx1, dz, do, second_gain_grad, block_out, down_kept, gate_term, up_term = back_in(
+        shards,
+        places,
+        dxn2,
+        x1,
+        slope,
+        second_gain[None],
+        down_term.reshape((2,) * bits + (shards, part, -1)),
+        output_weight,
+        down_weight,
+        hidden,
+        xn2,
+        dg,
+        dv,
+    )
+    down_wide = spread(down_kept.reshape(shards * part, -1))
+    down_grad = down_wide.astype(FULL)
+    gate_kept = summed(gate_term)
+    up_kept = summed(up_term)
     do = do.reshape(rows, width)
 
     dh = (do * gelu_y).astype(LOW)
@@ -1210,7 +1518,18 @@
         for k in range(taps)
     )
     du = du.reshape(rows, width).astype(LOW)
-    input_grad, mixer_gain_grad, mix_term = leave(
+    small = jnp.concatenate(
+        [
+            own_part(recur_gate_grad.T, edge).T,
+            own_part(input_gate_grad.T, edge).T,
+            conv_grad,
+            recur_bias_grad[:, None],
+            input_bias_grad[:, None],
+            decay_grad[:, None],
+        ],
+        axis=1,
+    )
+    input_grad, mixer_gain_grad, mix_term, small = leave(
         shards,
         places,
         du.reshape(u3.shape),
@@ -1223,38 +1542,31 @@
         dz,
         input_weight,
         branch_weight,
-    )
-    mixed = reduce_pair(mix_term).reshape(-1, shards, 3, width)
-    out_grad, branch_grad, input_weight_grad = [
-        mixed[:, :, k].reshape(-1, lru) for k in range(3)
-    ]
-
-    small = jnp.concatenate(
-        [
-            own_part(recur_gate_grad.T, edge).T,
-            own_part(input_gate_grad.T, edge).T,
-            conv_grad,
-            recur_bias_grad[:, None],
-            input_bias_grad[:, None],
-            decay_grad[:, None],
-        ],
-        axis=1,
-    )
-    small = lax.psum_scatter(small.astype(LOW), "seq", scatter_dimension=0, tiled=True)
+        down_wide,
+        jnp.pad(small, ((0, 0), (0, -small.shape[1] % 128))).astype(LOW).reshape(places, -1, -(-small.shape[1] // 128) * 128),
+    )
+    gains = jnp.concatenate(
+        [mixer_gain_grad, second_gain_grad, jnp.zeros((6, model), FULL)], axis=0
+    )
+    gate_grad, up_grad, out_grad, branch_grad, input_weight_grad, gains = settle(
+        shards,
+        places,
+        gate_kept.reshape(shards, part, -1),
+        up_kept.reshape(shards, part, -1),
+        mix_term.reshape((2,) * bits + (shards, part, -1)),
+        gains,
+    )
+    gains = lax.dynamic_slice_in_dim(gains, (me_s * shards + me_w) * part, part, 1)
+
     moves = [
         (s * shards + w, w * places + s) for s in range(places) for w in range(shards)
     ]
-    small = lax.ppermute(small, ("seq", "wt"), moves).astype(FULL)
-    share = model // (places * shards)
-    gains = jnp.concatenate(
-        [mixer_gain_grad.reshape(-1, share), second_gain_grad.reshape(-1, share)], axis=1
-    )
-    gains = lax.psum_scatter(gains, ("seq", "wt"), scatter_dimension=0, tiled=True)[0]
+    small = lax.ppermute(small, ("seq", "wt"), moves)
     at = 2 * head + taps
     return (
         block_out[None],
         input_grad[None],
-        gains[:share],
+        gains[0],
         input_weight_grad,
         branch_grad,
         small[:, 2 * head : at],
@@ -1264,7 +1576,7 @@
         small[:, at + 1],
         small[:, at + 2],
         out_grad,
-        gains[share:],
+        gains[1],
         gate_grad,
         up_grad,
         down_grad,

time: 776 us -> 638 us (0.82)
  waiting for transfers between devices: 82 us -> 5.37 us
  blocking collectives: 67.2 us -> 20.2 us
  starting transfers between devices: 44.9 us -> 23.3 us
  Pallas kernels: 473 us -> 482 us
    pallas_call x1 -> x2, Pallas kernels: 72.3 us -> 173 us  [the longest x1 96.1 us: settle(): pl.pallas_call(functools.partial(settle_kernel, n, places, bits), out_sha...]
    all_to_all x4 -> x1, waiting for transfers between devices: 70 us -> 1.3 us  [spread(): return lax.all_to_all(kept, 'wt', split_axis=0, concat_axis=1, tiled=True)]
    pallas_call x1, Pallas kernels: 166 us -> 106 us  [ffn(): pl.pallas_call(functools.partial(ffn_kernel, n, places), out_shape=[jax.S...]
    unnamed x1 -> x0, blocking collectives: 47.2 us -> none
    pallas_call x1, Pallas kernels: 92.1 us -> 60.2 us  [leave(): pl.pallas_call(functools.partial(leave_kernel, n, places), out_shape=[jax...]
    all_to_all x4 -> x1, starting transfers between devices: 27.2 us -> 5.45 us  [spread(): return lax.all_to_all(kept, 'wt', split_axis=0, concat_axis=1, tiled=True)]
    unnamed x102 -> x114, local copies, waits for them, and re-layouts: 11.5 us -> 19.8 us
    convert_element_type x4 -> x0, local copies, waits for them, and re-layouts: 7.98 us -> none  [reduce_pair(): return wide.astype(FULL)]
  transfers between devices with their start and end apart: 16 -> 10, of which waited for: 5 -> 2; matrix products, arithmetic and copies ran while one was open for 7% -> 8% of each run, Pallas kernels for 23% -> 11%
where the time goes in v3:
time: 638 us; the launch traced here: 627 us
  Pallas kernels  482 us (76%)
  local copies, waits for them, and re-layouts  48.1 us (8%)
  other arithmetic  24.8 us (4%)
  starting transfers between devices  23.3 us (4%)
  blocking collectives  20.2 us (3%)
  between operations  15.4 us (2%)
  matrix products  8.63 us (1%)
    pallas_call x1, Pallas kernels, ffn(): pl.pallas_call(functools.partial(ffn_kernel, n, places), out_shape=[jax.S...  106 us
    pallas_call x1, Pallas kernels, settle(): pl.pallas_call(functools.partial(settle_kernel, n, places, bits), out_sha...  96.1 us
    pallas_call x1, Pallas kernels, back_in(): pl.pallas_call(functools.partial(back_in_kernel, n, places, bits), out_sh...  76.5 us
    pallas_call x1, Pallas kernels, close(): pl.pallas_call(functools.partial(close_kernel, n), out_shape=[jax.ShapeDt...  67.4 us
    pallas_call x1, Pallas kernels, leave(): pl.pallas_call(functools.partial(leave_kernel, n, places), out_shape=[jax...  60.2 us
    pallas_call x1, Pallas kernels, enter(): pl.pallas_call(functools.partial(enter_kernel, n), out_shape=[jax.ShapeDt...  49.1 us
    unnamed x114, local copies, waits for them, and re-layouts  19.8 us
    pallas_call x1, Pallas kernels, gates_scan(): pl.pallas_call(gates_kernel, grid_spec=spec, out_shape=[jax.ShapeDtypeStr...  14.8 us
  transfers between devices with their start and end apart: 10, of which 2 were waited for; matrix products, arithmetic and copies ran while one was open for 8% of the time, Pallas kernels for 11%

profile of v3, /device:TPU:10, one launch (start us, length us, event | category | flops | bytes accessed | tf_op | source)
XLA Modules:
  0.0 627.5 jit_solution(10875828989794160176)
XLA Ops:
  8.5 49.1 %shard_map.288 = (bf16[4,128,2560]{2,1,0:T(8,128)(2,1)}, bf16[4,128,640]{2,1,0:T(8,128)(2,1)}, f32[4,128,640]{2,1,0:T(8,128)}, s32[4,8,128]{2,1,0:T(8,128)}) custom-call(bf16[128,2560]{1,0:T(8,128)(2,1)} %bitcast.200, f32[1,2560]{1,0:T(1,128)} %broadcast_in_dim.57.gain_ref, s32[1,128]{1,0:T(1,128)} %doc_ref.1, bf16[2560,640]{1,0:T(8,128)(2,1)} %win_hbm.3, ...), custom_call_target="tpu_custom_call" | custom-call | flops 49999998976 | bytes 170000000 | tf_op jit(solution)/shard_map/pallas_call | solution.py:527
  58.5 1.9 collective-permute-start.2
  60.4 3.6 collective-permute-start.1
  64.8 1.9 collective-permute-start
  74.8 3.8 collective-permute-start.3
  78.6 1.8 constant_dynamic-slice_fusion.2.table_r
  81.0 1.8 constant_dynamic-slice_fusion.1.table_i
  84.7 14.8 %shard_map.289 = (f32[512,640]{1,0:T(8,128)}, f32[512,640]{1,0:T(8,128)}, f32[512,640]{1,0:T(8,128)}, f32[512,640]{1,0:T(8,128)}) custom-call(s32[1]{0:T(128)} %bitcast.odd, bf16[512,768]{1,0:T(8,128)(2,1)} %maximum_select_fusion.1.c_ref.c_own, bf16[512,768]{1,0:T(8,128)(2,1)} %maximum_select_fusion.1.c_ref.c_own, ...), custom_call_target="tpu_custom_call" | custom-call | tf_op jit(solution)/shard_map/pallas_call | solution.py:144
  101.4 9.9 %all-gather = f32[16,4,640]{2,1,0:T(4,128)S(1)} all-gather(f32[2,4,640]{2,1,0:T(4,128)S(1)} %pad_maximum_fusion.4), channel_id=2, replica_groups=mesh['seq'=8,'wt'=4] {'seq'}, dimensions={0}, use_global_device_ids=true | all-gather | bytes 184320 | tf_op jit(solution)/shard_map/all_gather | solution.py:1433
  112.0 3.4 fusion
  115.4 67.4 %shard_map.290 = (f32[128,2560]{1,0:T(8,128)}, bf16[128,2560]{1,0:T(8,128)(2,1)}, bf16[4,128,2560]{2,1,0:T(8,128)(2,1)}) custom-call(bf16[4,128,640]{2,1,0:T(8,128)(2,1)} %bitcast.175, bf16[128,2560]{1,0:T(8,128)(2,1)} %bitcast.201, f32[1,2560]{1,0:T(1,128)} %broadcast_in_dim.60.gain_ref.refs_3_, bf16[2560,640]{1,0:T(8,128)(2,1)} %refs_5_.1, ...), custom_call_target="tpu_custom_call" | custom-call | flops 65000001536 | bytes 221000000 | tf_op jit(solution)/shard_map/pallas_call | solution.py:587
  182.8 105.6 %shard_map.291 = (f32[128,2560]{1,0:T(8,128)}, bf16[4,128,1920]{2,1,0:T(8,128)(2,1)}, bf16[4,128,1920]{2,1,0:T(8,128)(2,1)}, bf16[4,128,1920]{2,1,0:T(8,128)(2,1...) custom-call(bf16[128,2560]{1,0:T(8,128)(2,1)} %get-tuple-element.58.xn2_ref, ...), custom_call_target="tpu_custom_call" | custom-call | flops 124999999488 | bytes 425000000 | tf_op jit(solution)/shard_map/pallas_call | solution.py:889
  288.5 76.5 %shard_map.292 = (f32[128,2560]{1,0:T(8,128)}, bf16[4,128,2560]{2,1,0:T(8,128)(2,1)}, f32[4,128,640]{2,1,0:T(8,128)}, f32[1,2560]{1,0:T(1,128)}, bf16[128,2560]{...) custom-call(f32[128,2560]{1,0:T(8,128)} %get-tuple-element.60.refs_0_, ...), custom_call_target="tpu_custom_call" | custom-call | flops 74999996416 | bytes 255000000 | tf_op jit(solution)/shard_map/pallas_call | solution.py:998
  368.5 2.1 fusion.2
  370.6 11.8 %shard_map.293 = (f32[512,640]{1,0:T(8,128)}, f32[512,640]{1,0:T(8,128)}) custom-call(bf16[512,640]{1,0:T(8,128)(2,1)} %get-tuple-element.160.dh_ref, f32[512,640]{1,0:T(8,128)} %copy-done.10), custom_call_target="tpu_custom_call" | custom-call | tf_op jit(solution)/shard_map/pallas_call | solution.py:164
  383.4 10.3 %all-gather.1 = f32[16,4,640]{2,1,0:T(4,128)S(1)} all-gather(f32[2,4,640]{2,1,0:T(4,128)S(1)} %pad_maximum_fusion.3), channel_id=3, replica_groups=mesh['seq'=8,'wt'=4] {'seq'}, dimensions={0}, use_global_device_ids=true | all-gather | bytes 184320 | tf_op jit(solution)/shard_map/all_gather | solution.py:1489
  393.7 1.6 slice_add_fusion
  397.0 2.8 multiply_reduce_fusion
  402.4 5.4 all-to-all-start
  422.0 2.1 collective-permute-start.5
  427.4 3.2 concatenate.93
  431.6 1.8 fusion.18.du_ref
  434.7 2.5 copy.93
  437.2 60.2 %shard_map.294 = (f32[128,2560]{1,0:T(8,128)}, f32[1,2560]{1,0:T(1,128)}, bf16[1280,1920]{1,0:T(8,128)(2,1)}, f32[80,640]{1,0:T(8,128)}) custom-call(bf16[4,128,640]{2,1,0:T(8,128)(2,1)} %fusion.18.du_ref, bf16[4,128,640]{2,1,0:T(8,128)(2,1)} %bitcast.177, bf16[4,128,640]{2,1,0:T(8,128)(2,1)} %bitcast.176, bf16[128,2560]{1,0:T(8,128)(2,1)} %bitcast.202, ...), custom_call_target="tpu_custom_call" | custom-call | flops 60000002048 | bytes 204000000 | tf_op jit(solution)/shard_map/pallas_call | solution.py:1158
  497.4 3.4 collective-permute-start.6
  500.8 1.4 maximum_maximum_fusion.gains_ref
  502.2 2.9 convert_element_type.83
  505.2 4.0 collective-permute-done.6
  511.3 96.1 %shard_map.295 = (f32[80,7680]{1,0:T(8,128)}, f32[80,7680]{1,0:T(8,128)}, f32[80,2560]{1,0:T(8,128)}, f32[80,2560]{1,0:T(8,128)}, f32[80,2560]{1,0:T(8,128)}, /*index=5*/f32[8,2560]{1,0:T(8,128)}) custom-call(bf16[4,80,1920]{2,1,0:T(8,128)(2,1)} %bitcast.198, bf16[4,80,1920]{2,1,0:T(8,128)(2,1)} %bitcast.199, bf16[2,2,4,80,1920]{4,3,2,1,0:T(8,128)(2,1)} %bitcast.203, ...), custom_call_target="tpu_custom_call" | custom-call | flops 99999997952 | bytes 340000000 | tf_op jit(solution)/shard_map/pallas_call | solution.py:1320
  608.8 2.0 copy.109
  616.2 1.4 copy.114
  618.7 1.4 copy.115
  (212 shorter events, 53.8 us)
Async XLA Ops:
  7.2 504.1 %reduce-scatter.3.cloned.1.call-start = ((), (), s32[]{:S(2)}) async-start(), calls=%async_computation.3 | async-start | bytes 6144000 | tf_op jit(solution)/shard_map/reduce_scatter | solution.py:1452
  58.5 13.0 %collective-permute-start.2 = (s32[4,3]{1,0:T(4,128)S(1)}, s32[4,3]{1,0:T(4,128)S(1)}, u32[]{:S(2)}, u32[]{:S(2)}) collective-permute-start(s32[4,3]{1,0:T(4,128)S(1)} %get-tuple-element.177), channel_id=1, source_target_pairs={{0,4},{4,8},{8,12},{12,16},{16,20},{20,24},{24,28},{1,5},{5,9},{9,... | collective-permute-start | bytes 152 | tf_op jit(solution)/shard_map/ppermute | solution.py:1385
  60.4 11.1 %collective-permute-start.1 = (s32[4,3]{1,0:T(4,128)S(1)}, s32[4,3]{1,0:T(4,128)S(1)}, u32[]{:S(2)}, u32[]{:S(2)}) collective-permute-start(s32[4,3]{1,0:T(4,128)S(1)} %get-tuple-element.178), channel_id=1, source_target_pairs={{4,0},{8,4},{12,8},{16,12},{20,16},{24,20},{28,24},{5,1},{9,5},{13... | collective-permute-start | bytes 152 | tf_op jit(solution)/shard_map/ppermute | solution.py:1386
  64.8 7.7 %collective-permute-start = (bf16[4,3,640]{2,1,0:T(4,128)(2,1)S(1)}, bf16[4,3,640]{2,1,0:T(4,128)(2,1)S(1)}, u32[]{:S(2)}, u32[]{:S(2)}) collective-permute-start(bf16[4,3,640]{2,1,0:T(4,128)(2,1)S(1)} %slice.315), channel_id=1, source_target_pairs={{0,4},{4,8},{8,12},{12,16},{16,20},{20,24},{24,28},{1,5},{5,9},{9,... | collective-permute-start | bytes 46088 | tf_op jit(solution)/shard_map/ppermute | solution.py:1405
  71.4 3.2 copy-start.34
  71.5 3.2 copy-start.36
  71.5 3.2 copy-start.38
  71.5 3.2 copy-start.40
  72.5 2.2 copy-start.42
  72.5 2.2 copy-start.44
  72.5 2.3 copy-start.46
  72.5 2.3 copy-start.48
  73.7 6.7 %copy-start.51 = (f32[2560]{0:T(1024)S(1)}, f32[2560]{0:T(1024)}, u32[]{:S(2)}) copy-start(f32[2560]{0:T(1024)} %param.29) | copy-start | bytes 30724
  74.8 9.9 %copy-start.2 = (bf16[4,128,640]{2,1,0:T(8,128)(2,1)}, bf16[4,128,640]{2,1,0:T(8,128)(2,1)S(1)}, u32[]{:S(2)}) copy-start(bf16[4,128,640]{2,1,0:T(8,128)(2,1)S(1)} %add_convert_fusion) | copy-start | bytes 1966084
  74.8 8.8 %collective-permute-start.3 = (bf16[512,128]{1,0:T(8,128)(2,1)S(1)}, bf16[512,128]{1,0:T(8,128)(2,1)S(1)}, u32[]{:S(2)}, u32[]{:S(2)}) collective-permute-start(bf16[512,128]{1,0:T(8,128)(2,1)S(1)} %slice_select_fusion.3), channel_id=1, source_target_pairs={{0,1},{1,0},{2,3},{3,2},{4,5},{5,4},{6,7},{7,6},{8,9},{9,8},{10,11... | collective-permute-start | bytes 393224 | tf_op jit(solution)/shard_map/ppermute | solution.py:46
  84.7 27.3 %copy-start.11 = (f32[4,128,640]{2,1,0:T(8,128)S(1)}, f32[4,128,640]{2,1,0:T(8,128)}, u32[]{:S(2)}) copy-start(f32[4,128,640]{2,1,0:T(8,128)} %get-tuple-element.57) | copy-start | bytes 3932164
  112.0 3.4 copy-start.30
  365.1 2.7 copy-start.18
  366.4 2.1 copy-start.13
  370.6 12.8 %copy-start.33 = (f32[4,1,640]{2,0,1:T(4,128)S(1)}, f32[4,1,640]{2,0,1:T(4,128)}, u32[]{:S(2)}) copy-start(f32[4,1,640]{2,0,1:T(4,128)} %copy-done.32) | copy-start | bytes 30724
  370.6 23.1 %copy-start.9 = (f32[512,640]{1,0:T(8,128)S(1)}, f32[512,640]{1,0:T(8,128)}, u32[]{:S(2)}) copy-start(f32[512,640]{1,0:T(8,128)} %get-tuple-element.56) | copy-start | bytes 3932164
  370.6 23.1 %copy-start.31 = (f32[4,640]{1,0:T(4,128)S(1)}, f32[4,640]{1,0:T(4,128)}, u32[]{:S(2)}) copy-start(f32[4,640]{1,0:T(4,128)} %copy-done.30) | copy-start | bytes 30724
  393.7 2.1 copy-start.19
  401.3 9.9 %collective-permute-start.4 = (bf16[1024,128]{1,0:T(8,128)(2,1)S(1)}, bf16[1024,128]{1,0:T(8,128)(2,1)S(1)}, u32[]{:S(2)}, u32[]{:S(2)}) collective-permute-start(bf16[1024,128]{1,0:T(8,128)(2,1)S(1)} %fusion.43), channel_id=1, source_target_pairs={{0,1},{1,0},{2,3},{3,2},{4,5},{5,4},{6,7},{7,6},{8,9},{9,8},{10,11... | collective-permute-start | bytes 786440 | tf_op jit(solution)/shard_map/ppermute | solution.py:46
  402.4 32.3 %all-to-all-start = ((bf16[4,80,1920]{2,1,0:T(8,128)(2,1)}), bf16[4,80,1920]{2,1,0:T(8,128)(2,1)}, u32[]{:S(2)}, u32[]{:S(2)}) async-start(bf16[4,80,1920]{2,1,0:T(8,128)(2,1)} %get-tuple-element.76), calls=%async_computation | async-start | bytes 2457600 | tf_op jit(solution)/shard_map/all_to_all | solution.py:1457
  407.9 103.4 %reduce-scatter.5.cloned.1.call-start = ((), (), s32[]{:S(2)}) async-start(), calls=%async_computation.4 | async-start | bytes 6144000 | tf_op jit(solution)/shard_map/reduce_scatter | solution.py:1452
  422.0 9.5 %collective-permute-start.5 = (f32[4,3,640]{2,1,0:T(4,128)S(1)}, f32[4,3,640]{2,1,0:T(4,128)S(1)}, u32[]{:S(2)}, u32[]{:S(2)}) collective-permute-start(f32[4,3,640]{2,1,0:T(4,128)S(1)} %slice.462), channel_id=1, source_target_pairs={{4,0},{8,4},{12,8},{16,12},{20,16},{24,20},{28,24},{5,1},{9,5},{13... | collective-permute-start | bytes 92168 | tf_op jit(solution)/shard_map/ppermute | solution.py:1514
  497.4 11.8 %collective-permute-start.6 = (f32[80,640]{1,0:T(8,128)}, f32[80,640]{1,0:T(8,128)S(1)}, u32[]{:S(2)}, u32[]{:S(2)}) collective-permute-start(f32[80,640]{1,0:T(8,128)} %get-tuple-element.86), channel_id=1, source_target_pairs={{0,0},{1,8},{2,16},{3,24},{4,1},{5,9},{6,17},{7,25},{8,2},{9,10},{... | collective-permute-start | bytes 614408 | tf_op jit(solution)/shard_map/ppermute | solution.py:1564
  607.4 3.4 copy-start.17
  612.4 2.3 copy-start.22
  613.8 2.3 copy-start.15
  616.2 2.6 copy-start.14
  (30 other events, 39.9 us)
Sparse Core Ops, SparseCore 0:
  365.2 59.0 reduce-scatter.2
  427.4 67.4 reduce-scatter.4

commit v4 on v3

--- a/solution.py
+++ b/solution.py
@@ -27,54 +27,6 @@
         1.0 + 3.0 * 0.044715 * values * values
     )
     return gelu, grad
-
-
-def head_rows(gate_rows, shards):
-    head = gate_rows.shape[1]
-    width = gate_rows.shape[0] // shards
-    heads = -(-width // head)
-    first = (lax.axis_index("wt") * width) // head
-    table = gate_rows.reshape(-1, head, head)
-    return lax.dynamic_slice_in_dim(table, first, heads, 0)
-
-
-def edge_swap(values, edge):
-    me = lax.axis_index("wt")
-    shards = lax.axis_size("wt")
-    odd = me % 2 == 1
-    mine = jnp.where(odd, values[:, :edge], values[:, -edge:])
-    other = lax.ppermute(mine, "wt", [(i, i ^ 1) for i in range(shards)])
-    return jnp.where(
-        odd,
-        jnp.concatenate([other, values], axis=1),
-        jnp.concatenate([values, other], axis=1),
-    )
-
-
-def own_part(values, edge):
-    odd = lax.axis_index("wt") % 2 == 1
-    return jnp.where(odd, values[:, edge:], values[:, :-edge])
-
-
-def heads_dot(values, table, transposed=False):
-    heads, head, _ = table.shape
-    return jnp.concatenate(
-        [
-            dot(values[:, n * head : (n + 1) * head], table[n], 1, 1 if transposed else 0)
-            for n in range(heads)
-        ],
-        axis=1,
-    )
-
-
-def heads_grad(values, slopes, head):
-    return jnp.concatenate(
-        [
-            dot(values[:, n * head : (n + 1) * head], slopes[:, n * head : (n + 1) * head], 0, 0)
-            for n in range(values.shape[1] // head)
-        ],
-        axis=0,
-    )
 
 
 def scan_rows(coef, value, reverse):
@@ -96,78 +48,10 @@
     return coef, value
 
 
-def gates_kernel(odd, c_ref, c_own, table_r, table_i, rows_ref, mask_ref, r_ref, ii_ref, a_ref, h_ref):
-    c_head = c_ref[...]
-    ra = jnp.dot(c_head, table_r[0], preferred_element_type=FULL)
-    ia = jnp.dot(c_head, table_i[0], preferred_element_type=FULL)
-    r = jax.nn.sigmoid(ra + rows_ref[0:1, :])
-    ii = jax.nn.sigmoid(ia + rows_ref[1:2, :])
-    keep = mask_ref[:, 0:1]
-    log_a = rows_ref[2:3, :] * r
-    decay = jnp.exp(2.0 * log_a)
-    gap = jnp.where(2.0 * log_a > -0.01, -expm1_small(2.0 * log_a), 1.0 - decay)
-    mult = jnp.where(keep == 0.0, 1.0, jnp.sqrt(gap))
-    b = (mult * c_own[...].astype(FULL) * ii).astype(LOW).astype(FULL)
-    a = jnp.exp(log_a.astype(LOW).astype(FULL)) * keep
-    cum_a, h_loc = scan_rows(a, b, False)
-    r_ref[...] = r
-    ii_ref[...] = ii
-    a_ref[...] = cum_a
-    h_ref[...] = h_loc
-
-
 def expm1_small(values):
     return values * (
         1.0 + values * (0.5 + values * (1.0 / 6.0 + values * (1.0 / 24.0 + values / 120.0)))
     )
-
-
-def gates_scan(c_ext, table_r, table_i, rows8, mask, odd, part_len, width):
-    rows = c_ext.shape[0]
-    head = table_r.shape[1]
-    half = 128
-    per = head // half
-    grid = (rows // part_len, width // half)
-    spec = pltpu.PrefetchScalarGridSpec(
-        num_scalar_prefetch=1,
-        grid=grid,
-        in_specs=[
-            pl.BlockSpec((part_len, head), lambda m, n, s: (m, (n + s[0]) // per)),
-            pl.BlockSpec((part_len, half), lambda m, n, s: (m, n + s[0])),
-            pl.BlockSpec((1, head, half), lambda m, n, s: ((n + s[0]) // per, 0, (n + s[0]) % per)),
-            pl.BlockSpec((1, head, half), lambda m, n, s: ((n + s[0]) // per, 0, (n + s[0]) % per)),
-            pl.BlockSpec((8, half), lambda m, n, s: (0, n)),
-            pl.BlockSpec((part_len, mask.shape[1]), lambda m, n, s: (m, 0)),
-        ],
-        out_specs=[pl.BlockSpec((part_len, half), lambda m, n, s: (m, n))] * 4,
-    )
-    return pl.pallas_call(
-        gates_kernel,
-        grid_spec=spec,
-        out_shape=[jax.ShapeDtypeStruct((rows, width), FULL)] * 4,
-    )(odd, c_ext, c_ext, table_r, table_i, rows8, mask)
-
-
-def back_kernel(dh_ref, a_ref, rem_ref, e_ref):
-    rows = dh_ref.shape[0]
-    place = lax.broadcasted_iota(jnp.int32, dh_ref.shape, 0)
-    a_next = jnp.where(place < rows - 1, pltpu.roll(a_ref[...], rows - 1, 0), 1.0)
-    rem, e_loc = scan_rows(a_next, dh_ref[...].astype(FULL), True)
-    rem_ref[...] = rem
-    e_ref[...] = e_loc
-
-
-def back_scan(dh, a, part_len):
-    rows, width = a.shape
-    half = 128
-    block = pl.BlockSpec((part_len, half), lambda m, n: (m, n))
-    return pl.pallas_call(
-        back_kernel,
-        grid=(rows // part_len, width // half),
-        in_specs=[block, block],
-        out_specs=[block, block],
-        out_shape=[jax.ShapeDtypeStruct((rows, width), FULL)] * 2,
-    )(dh, a)
 
 
 MESH = pl.DeviceIdType.MESH
@@ -376,8 +260,8 @@
 
 
 class LineBoth:
-    def __init__(self, gather, back):
-        self.gather, self.back = gather, back
+    def __init__(self, gather, back, skip=0):
+        self.gather, self.back, self.skip = gather, back, skip
         self.n, self.me = gather.n, gather.me
 
     def sends(self, side, t, act):
@@ -385,33 +269,35 @@
         place = me if side == 0 else n - 1 - me
         spread = self.gather.rightward if side == 0 else self.gather.leftward
         pull = self.back.rightward if side == 0 else self.back.leftward
+        d = t + self.skip
 
         @pl.when(place < n - 1)
         def _():
-            @pl.when(t <= place)
+            @pl.when(d <= place)
             def _():
-                act(spread(t))
-
-            @pl.when(t > place)
+                act(spread(d))
+
+            @pl.when(d > place)
             def _():
-                act(pull(t - place - 1))
+                act(pull(d - place - 1))
 
     def step(self, t):
         n, me = self.n, self.me
+        d = t + self.skip
         for side in range(2):
             place = me if side == 0 else n - 1 - me
             if t > 0:
 
-                @pl.when(t <= place)
+                @pl.when(d <= place)
                 def _():
-                    block = self.gather.blocks.at[me - t if side == 0 else me + t]
+                    block = self.gather.blocks.at[me - d if side == 0 else me + d]
                     remote(
-                        block, block, self.gather.sent.at[side, 0], self.gather.landed.at[side, t], me
+                        block, block, self.gather.sent.at[side, 0], self.gather.landed.at[side, d], me
                     ).wait_recv()
 
-                @pl.when((t > place) & (place > 0))
+                @pl.when((d > place) & (place > 0))
                 def _():
-                    k = t - place - 1
+                    k = d - place - 1
                     self.back.arrived(side, k)
                     self.back.add(n - 1 - k if side == 0 else k, side, k)
 
@@ -420,13 +306,15 @@
 
     def finish(self):
         for side in range(2):
-            self.sends(side, self.n - 1, lambda copy: copy.wait_send())
-
-
-def line_reduce(n, me, parts, slots, sent, landed, partial, work, finish):
+            self.sends(side, self.n - 1 - self.skip, lambda copy: copy.wait_send())
+
+
+def line_reduce(n, me, parts, slots, sent, landed, partial, work, finish, early=None):
     line = LineReduce(n, me, parts, slots, sent, landed)
     line.prepare(0, partial)
     line.step(0)
+    if early is not None:
+        early()
     for k in range(1, n - 1):
         line.prepare(k, partial)
     line.step(1)
@@ -548,12 +436,21 @@
 
 
 def close_kernel(
-    n, o_ref, x_ref, gain_ref, w_ref, slope_ref, x1_ref, xn2_ref, dm_ref, parts, slots, sent, landed, gsent, glanded
+    n, o_ref, x_ref, gain_ref, w_ref, near_hbm, x1_ref, xn2_ref, dm_ref, parts, slots, sent, landed, gsent, glanded, local
 ):
     me = lax.axis_index("wt")
-    dm_ref[me] = slope_ref[...].astype(LOW)
+    model = w_ref.shape[0]
+
+    def near(k, act):
+        q = me + k - 1
+
+        @pl.when((q >= 0) & (q < n))
+        def _():
+            act(pltpu.make_async_copy(near_hbm.at[k], dm_ref.at[q], local.at[k]))
+
+    for k in range(3):
+        near(k, lambda copy: copy.start())
     greet(n, me)
-    model = w_ref.shape[0]
 
     def partial(q):
         block = o_ref[q]
@@ -570,19 +467,21 @@
         xn2_ref[...] = (x1 * scale * gain_ref[...]).astype(LOW)
 
     back = LineReduce(n, me, parts, slots, sent, landed)
-    both = LineBoth(LineGather(n, me, dm_ref, gsent, glanded), back)
+    both = LineBoth(LineGather(n, me, dm_ref, gsent, glanded), back, 1)
+    for k in range(3):
+        near(k, lambda copy: copy.wait())
+    back.prepare(0, partial)
     both.step(0)
-    for k in range(n - 1):
+    for k in range(1, n - 1):
         back.prepare(k, partial)
-    for t in range(1, n):
+    partial(me)
+    for t in range(1, n - 1):
         both.step(t)
-        if t == 1:
-            partial(me)
     finish(back.total())
     both.finish()
 
 
-def close(n, o, x, gain, weight, slope):
+def close(n, o, x, gain, weight, near):
     rows, model = x.shape
     return pl.pallas_call(
         functools.partial(close_kernel, n),
@@ -591,17 +490,18 @@
             jax.ShapeDtypeStruct((rows, model), LOW),
             jax.ShapeDtypeStruct((n, rows, model), LOW),
         ],
-        in_specs=[VMEM] * 5,
+        in_specs=[VMEM] * 4 + [ANY],
         out_specs=[VMEM] * 3,
         scratch_shapes=[
             pltpu.VMEM((n, rows, model), LOW),
             pltpu.VMEM((2, n - 1, rows, model), LOW),
         ]
         + reduce_sems(n)
-        + gather_sems(n),
+        + gather_sems(n)
+        + [pltpu.SemaphoreType.DMA((3,))],
         compiler_params=comm_params(1),
-        cost_estimate=lasting(65),
-    )(o, x, gain, weight, slope)
+        cost_estimate=lasting(55),
+    )(o, x, gain, weight, near)
 
 
 class PairSum:
@@ -738,23 +638,34 @@
         place[now] = self.mine(now) if own else 1 - self.mine(now)
         return tuple(place) + (slice(None), slice(None), pl.ds(*self.columns[side]))
 
-    def send(self, side, step):
+    def send(self, side, step, piece=0):
+        at, landing = self.index(side, step, False), self.landings[2 * step + side]
+        if step == 0:
+            count = self.blocks.shape[-3] // 2
+            rows = pl.ds(piece * count, count)
+            at = at[: self.bits] + (rows,) + at[self.bits + 1 :]
+            landing = landing.at[(slice(None),) * (self.bits - 1) + (rows,)]
         return pltpu.make_async_remote_copy(
-            src_ref=self.blocks.at[self.index(side, step, False)],
-            dst_ref=self.landings[2 * step + side],
-            send_sem=self.sent.at[side, step],
-            recv_sem=self.landed.at[side, step],
+            src_ref=self.blocks.at[at],
+            dst_ref=landing,
+            send_sem=self.sent.at[side, step + piece * self.bits],
+            recv_sem=self.landed.at[side, step + piece * self.bits],
             device_id=self.peer(self.order(side)[step]),
             device_id_type=MESH,
         )
 
-    def begin(self):
-        for side in range(2):
-            self.send(side, 0).start()
+    def pieces(self, step):
+        return (0, 1) if step == 0 else (0,)
+
+    def begin(self, pieces=(0, 1)):
+        for piece in pieces:
+            for side in range(2):
+                self.send(side, 0, piece).start()
 
     def advance(self, step):
         for side in range(2):
-            self.send(side, step).wait_recv()
+            for piece in self.pieces(step):
+                self.send(side, step, piece).wait_recv()
             at = self.index(side, step, True)
             total = self.blocks[at].astype(FULL) + self.landings[2 * step + side][...].astype(FULL)
             self.blocks[at] = total.astype(LOW)
@@ -767,7 +678,8 @@
     def finish(self):
         for step in range(self.bits):
             for side in range(2):
-                self.send(side, step).wait_send()
+                for piece in self.pieces(step):
+                    self.send(side, step, piece).wait_send()
 
 
 def plane_scratch(shape):
@@ -825,7 +737,7 @@
     loads = [
         pltpu.make_async_copy(source, target, local.at[k])
         for k, (source, target) in enumerate(
-            [(wg_hbm, wg), (wu_hbm, wu), (wd_hbm, wd), (dm_hbm, dm)]
+            [(dm_hbm, dm), (wd_hbm, wd), (wg_hbm, wg), (wu_hbm, wu)]
         )
     ]
     for load in loads:
@@ -834,7 +746,15 @@
     greet(n, me, True)
 
     def ready():
-        for load in loads:
+        for load in loads[:2]:
+            load.wait()
+
+        def tile(at):
+            value = dot(dm[...].reshape(n * rows, model), wd[:, at])
+            dg[:, :, at] = value.reshape(n, rows, -1).astype(LOW)
+
+        tiles(units, cut, tile)
+        for load in loads[2:]:
             load.wait()
 
     def use(q):
@@ -842,11 +762,11 @@
             block = xall[q]
             g = dot(block, wg[:, at])
             v = dot(block, wu[:, at])
-            back = dot(dm[q], wd[:, at])
+            slopes = dg[q, :, at].astype(FULL)
             gelu, slope = gelu_both(g)
             hidden[q, :, at] = (gelu * v).astype(LOW)
-            dg[q, :, at] = (back * v * slope).astype(LOW)
-            dv[q, :, at] = (back * gelu).astype(LOW)
+            dg[q, :, at] = (slopes * v * slope).astype(LOW)
+            dv[q, :, at] = (slopes * gelu).astype(LOW)
 
         tiles(units, cut, tile)
 
@@ -915,7 +835,7 @@
         + reduce_sems(n)
         + [pltpu.SemaphoreType.DMA((4,)), pltpu.SemaphoreType.DMA((4,))],
         compiler_params=comm_params(2),
-        cost_estimate=lasting(125),
+        cost_estimate=lasting(105),
     )(xn2, dm, wg, wu, wd)
 
 
@@ -953,8 +873,6 @@
     plane = PlaneReduce(blocks, landings, bsent, blanded)
     plane.begin()
     sum_ref[...] = jnp.sum(dxn2 * x1 * scale, axis=0, keepdims=True)
-    for load in loads[1:]:
-        load.wait()
 
     def use(q):
         do_ref[q] = dot(dz_ref[q], w[...])
@@ -968,18 +886,26 @@
     part = model // places
     size = pair_tile(model, places)
     pair = PairSum(part, halves, landing, psent, planded, free, pflush)
-    for k in range(n - 1):
-        back.prepare(k, partial)
-    partial(me)
+    loads[1].wait()
     use(me)
+    for load in loads[2:4]:
+        load.wait()
+    back.prepare(0, partial)
     work = pair.tasks(model // size, pair_dot(xall, dg, part, size), gate_hbm)
     work += pair.tasks(model // size, pair_dot(xall, dv, part, size), up_hbm)
     share = -(-len(work) // (n - 1))
     for t in range(1, n):
         both.step(t)
+        if t == 1:
+            for k in range(1, n - 1):
+                back.prepare(k, partial)
         if t >= 2 and t - 2 < bits:
             plane.advance(t - 2)
         line.each(t, use)
+        if t == 1:
+            partial(me)
+            for load in loads[4:]:
+                load.wait()
         for task in work[(t - 1) * share : t * share]:
             task()
     for step in range(max(n - 2, 0), bits):
@@ -1027,8 +953,8 @@
         + gather_sems(n)
         + reduce_sems(n)
         + [
-            pltpu.SemaphoreType.DMA((2, bits)),
-            pltpu.SemaphoreType.DMA((2, bits)),
+            pltpu.SemaphoreType.DMA((2, 2 * bits)),
+            pltpu.SemaphoreType.DMA((2, 2 * bits)),
             pltpu.SemaphoreType.DMA((7,)),
         ],
         compiler_params=comm_params(3),
@@ -1069,6 +995,7 @@
 def leave_kernel(
     n,
     places,
+    bits,
     du_ref,
     dy_ref,
     o_ref,
@@ -1079,12 +1006,13 @@
     dz_hbm,
     win_hbm,
     wbr_hbm,
-    after_hbm,
+    up_hbm,
     small_ref,
     grad_ref,
     sum_ref,
     mix_hbm,
     passed_ref,
+    kept_ref,
     xn,
     dz,
     win,
@@ -1103,12 +1031,16 @@
     ssent,
     slanded,
     local,
+    usent,
+    ulanded,
+    blocks,
+    *landings,
 ):
     me = lax.axis_index("wt")
     loads = [
         pltpu.make_async_copy(source, target, local.at[k])
         for k, (source, target) in enumerate(
-            [(win_hbm, win), (wbr_hbm, wbr), (xn_hbm, xn), (dz_hbm, dz)]
+            [(win_hbm, win), (wbr_hbm, wbr), (up_hbm, blocks), (xn_hbm, xn), (dz_hbm, dz)]
         )
     ]
     for load in loads:
@@ -1116,8 +1048,16 @@
     greet(n, me, False, 0, places)
     small = PlaneShare(places, small_ref, lands, ssent, slanded)
     small.start()
-    for load in loads:
+    plane = PlaneReduce(blocks, landings, usent, ulanded)
+    for load in loads[:2]:
         load.wait()
+
+    def early():
+        loads[2].wait()
+        plane.begin()
+        for load in loads[3:]:
+            load.wait()
+
     model = win.shape[0]
 
     def partial(q):
@@ -1147,24 +1087,31 @@
         grad_ref[...] = dx1_ref[...] + scale * (q1 - flat * (scale * scale * pull))
         sum_ref[...] = jnp.sum(total * flat * scale, axis=0, keepdims=True)
 
-    line_reduce(n, me, parts, slots, sent, landed, partial, work, finish)
+    tasks = work[:-1] + [lambda: (work[-1](), plane.advance(0))]
+    line_reduce(n, me, parts, slots, sent, landed, partial, tasks, finish, early)
     pair.finish(mix_hbm)
     small.finish(passed_ref)
-
-
-def leave(n, places, du, dy, o, x, dx1, gain, xn, dz, win, wbr, after, small):
+    for step in range(1, bits):
+        plane.advance(step)
+    kept_ref[...] = plane.kept()[...]
+    plane.finish()
+
+
+def leave(n, places, du, dy, o, x, dx1, gain, xn, dz, win, wbr, up, small):
+    bits = len(up.shape) - 3
     rows, model = x.shape
     width = win.shape[1]
     return pl.pallas_call(
-        functools.partial(leave_kernel, n, places),
+        functools.partial(leave_kernel, n, places, bits),
         out_shape=[
             jax.ShapeDtypeStruct((rows, model), FULL),
             jax.ShapeDtypeStruct((1, model), FULL),
             jax.ShapeDtypeStruct((model // 2, 3 * width), LOW),
             jax.ShapeDtypeStruct(small.shape[1:], FULL),
+            jax.ShapeDtypeStruct(up.shape[bits:], LOW),
         ],
         in_specs=[VMEM] * 6 + [ANY] * 5 + [VMEM],
-        out_specs=[VMEM, VMEM, ANY, VMEM],
+        out_specs=[VMEM, VMEM, ANY, VMEM, VMEM],
         scratch_shapes=[
             pltpu.VMEM((n, rows, model), LOW),
             pltpu.VMEM((n, rows, model), LOW),
@@ -1179,11 +1126,15 @@
             pltpu.VMEM(small.shape, LOW),
             pltpu.SemaphoreType.DMA((places,)),
             pltpu.SemaphoreType.DMA((places,)),
-            pltpu.SemaphoreType.DMA((4,)),
-        ],
+            pltpu.SemaphoreType.DMA((5,)),
+            pltpu.SemaphoreType.DMA((2, 2 * bits)),
+            pltpu.SemaphoreType.DMA((2, 2 * bits)),
+            pltpu.VMEM(up.shape, LOW),
+        ]
+        + plane_scratch(up.shape),
         compiler_params=comm_params(4),
         cost_estimate=lasting(60),
-    )(du, dy, o, x, dx1, gain, xn, dz, win, wbr, after, small)
+    )(du, dy, o, x, dx1, gain, xn, dz, win, wbr, up, small)
 
 
 class LineSpread:
@@ -1329,8 +1280,8 @@
             pltpu.VMEM((2, part, units), LOW),
             pltpu.VMEM((n,) + gains.shape, FULL),
             pltpu.VMEM((places,) + gains.shape, FULL),
-            pltpu.SemaphoreType.DMA((2, bits)),
-            pltpu.SemaphoreType.DMA((2, bits)),
+            pltpu.SemaphoreType.DMA((2, 2 * bits)),
+            pltpu.SemaphoreType.DMA((2, 2 * bits)),
             pltpu.SemaphoreType.DMA((3, n)),
             pltpu.SemaphoreType.DMA((3, n)),
             pltpu.SemaphoreType.DMA((2, max(n, places))),
@@ -1340,6 +1291,655 @@
         compiler_params=comm_params(5),
         cost_estimate=lasting(100),
     )(gate, up, mix, gains)
+
+
+def conv_masks(own, before, after, taps):
+    lane = lax.broadcasted_iota(jnp.int32, own.shape, 1)
+    lines = []
+    for here, back in ((own, before), (after, own)):
+        for k in range(taps):
+            shifted = jnp.where(lane >= k, pltpu.roll(here, k, 1), pltpu.roll(back, k, 1))
+            lines.append((shifted == here).astype(FULL)[:1] if k else jnp.ones_like(here)[:1])
+    lines.append(jnp.zeros((own.shape[1] - 2 * taps, own.shape[1]), FULL))
+    return jnp.concatenate(lines, axis=0).T
+
+
+def mid_kernel(
+    n,
+    places,
+    taps,
+    u_ref,
+    y_ref,
+    docs_ref,
+    rows_ref,
+    gr_hbm,
+    gi_hbm,
+    slope_ref,
+    o_ref,
+    c_ref,
+    r_ref,
+    ii_ref,
+    h_ref,
+    edge_ref,
+    halo_ref,
+    mask_ref,
+    near_ref,
+    tr,
+    ti,
+    cum,
+    carry,
+    before,
+    after,
+    hsent,
+    hlanded,
+    esent,
+    elanded,
+    csent,
+    clanded,
+    nsent,
+    nlanded,
+    local,
+):
+    me = lax.axis_index("wt")
+    seat = lax.axis_index("seq")
+    part_len, width = u_ref.shape[1:]
+    head = gr_hbm.shape[1]
+    ext = tr.shape[0]
+    edge = ext - width
+    odd = lax.rem(me, 2)
+    shift = odd * edge
+    block = 128
+    first = pl.multiple_of((me * width) // head * head, head)
+    loads = [
+        pltpu.make_async_copy(source.at[pl.ds(first, ext), :], target, local.at[k])
+        for k, (source, target) in enumerate([(gr_hbm, tr), (gi_hbm, ti)])
+    ]
+    for load in loads:
+        load.start()
+    partner = {"wt": me + 1 - 2 * odd}
+    near_ref[1] = slope_ref[...].astype(LOW)
+    greet(n, me, False, 0, places)
+
+    def neighbours(act, out):
+        for k, (to, there) in enumerate([(me + 1, 0), (me - 1, 2)]):
+            copy = remote(near_ref.at[1], near_ref.at[there], nsent.at[k], nlanded.at[k], to)
+            inside = (to >= 0) & (to < n)
+            gives = (me > 0) if k == 0 else (me < n - 1)
+
+            @pl.when(inside if out else gives)
+            def _():
+                act(copy)
+
+
+    def hop(source, target, k, to):
+        return pltpu.make_async_remote_copy(
+            src_ref=source,
+            dst_ref=target,
+            send_sem=hsent.at[k],
+            recv_sem=hlanded.at[k],
+            device_id={"seq": to},
+            device_id_type=MESH,
+        )
+
+    reach = halo_ref.shape[1]
+    tails = u_ref.at[:, pl.ds(part_len - reach, reach), :]
+    onward = [hop(tails, halo_ref, 0, seat + 1), hop(docs_ref, before, 1, seat + 1)]
+    backward = [hop(docs_ref, after, 2, seat - 1)]
+
+    @pl.when(seat < places - 1)
+    def _():
+        for copy in onward:
+            copy.start()
+
+    @pl.when(seat > 0)
+    def _():
+        for copy in backward:
+            copy.start()
+
+    @pl.when(seat == 0)
+    def _():
+        halo_ref[...] = jnp.zeros_like(halo_ref)
+        before[...] = jnp.full_like(before, -1)
+
+    @pl.when(seat == places - 1)
+    def _():
+        after[...] = jnp.full_like(after, -1)
+
+    @pl.when(seat > 0)
+    def _():
+        for copy in onward:
+            copy.wait_recv()
+
+    @pl.when(seat < places - 1)
+    def _():
+        for copy in backward:
+            copy.wait_recv()
+
+    def columns(b):
+        return pl.ds(pl.multiple_of(b * block, block), block)
+
+    def ext_columns(b):
+        return pl.ds(pl.multiple_of(b * block + shift, block), block)
+
+    def each(body):
+        def outer(q, carried):
+            def inner(b, deeper):
+                body(q, b)
+                return deeper
+
+            return lax.fori_loop(0, width // block, inner, carried)
+
+        lax.fori_loop(0, n, outer, 0)
+
+    def masks(q, carried):
+        mask_ref[q] = conv_masks(
+            docs_ref[q].astype(FULL), before[q].astype(FULL), after[q].astype(FULL), taps
+        )
+        return carried
+
+    lax.fori_loop(0, n, masks, 0)
+
+    def conv(q, b):
+        at = columns(b)
+        long = jnp.concatenate([halo_ref[q, :, at], u_ref[q, :, at]], axis=0).astype(FULL)
+        total = long[reach:] * rows_ref[0:1, at]
+        for k in range(1, taps):
+            window = pltpu.roll(long, k, 0)[reach:]
+            total = total + window * mask_ref[q, :, k : k + 1] * rows_ref[k : k + 1, at]
+        c_ref[q, :, ext_columns(b)] = total.astype(LOW)
+
+    each(conv)
+    source = pl.ds(pl.multiple_of(jnp.where(odd == 1, edge, width - edge), edge), edge)
+    target = pl.ds(pl.multiple_of(jnp.where(odd == 1, width, 0), edge), edge)
+    swap = pltpu.make_async_remote_copy(
+        src_ref=c_ref.at[:, :, source],
+        dst_ref=c_ref.at[:, :, target],
+        send_sem=esent.at[0],
+        recv_sem=elanded.at[0],
+        device_id=partner,
+        device_id_type=MESH,
+    )
+    swap.start()
+    for load in loads:
+        load.wait()
+    swap.wait_recv()
+    neighbours(lambda copy: copy.start(), True)
+    per = head // block
+
+    def gates(q, b):
+        at = columns(b)
+        j = b + shift // block
+        spot = j // per
+        within = pl.ds(pl.multiple_of(lax.rem(j, per) * block, block), block)
+        rows = pl.ds(pl.multiple_of(spot * head, head), head)
+        c_head = c_ref[q, :, rows]
+        c_own = c_ref[q, :, ext_columns(b)].astype(FULL)
+        r = jax.nn.sigmoid(dot(c_head, tr[rows, within]) + rows_ref[taps : taps + 1, at])
+        ii = jax.nn.sigmoid(dot(c_head, ti[rows, within]) + rows_ref[taps + 1 : taps + 2, at])
+        keep = mask_ref[q, :, 1:2]
+        log_a = rows_ref[taps + 2 : taps + 3, at] * r
+        mult = mult_of(log_a, keep)
+        b_low = (mult * c_own * ii).astype(LOW).astype(FULL)
+        a = jnp.exp(log_a.astype(LOW).astype(FULL)) * keep
+        cum_a, h_loc = scan_rows(a, b_low, False)
+        r_ref[q, :, at] = r
+        ii_ref[q, :, at] = ii
+        cum[q, :, at] = cum_a
+        h_ref[q, :, at] = h_loc
+
+    each(gates)
+    for q in range(n):
+        carry[seat, q : q + 1, :] = cum[q, part_len - 1 : part_len, :]
+        carry[seat, n + q : n + q + 1, :] = h_ref[q, part_len - 1 : part_len, :]
+
+    def share(by):
+        return pltpu.make_async_remote_copy(
+            src_ref=carry.at[seat],
+            dst_ref=carry.at[seat],
+            send_sem=csent.at[by],
+            recv_sem=clanded.at[by],
+            device_id={"seq": lax.rem(seat + by, places)},
+            device_id_type=MESH,
+        )
+
+    for by in range(1, places):
+        share(by).start()
+    for by in range(1, places):
+        share(by).wait_recv()
+    state = jnp.zeros((n, width), FULL)
+    start = state
+    for p in range(places):
+        start = jnp.where(seat == p, state, start)
+        state = carry[p, :n, :] * state + carry[p, n:, :]
+    edge_ref[:n, :] = start
+    edge_ref[n:, :] = carry[seat, :n, :]
+
+    def finish(q, b):
+        at = columns(b)
+        h = h_ref[q, :, at] + cum[q, :, at] * pick_row(edge_ref[:, at], q)
+        h_ref[q, :, at] = h
+        gelu, _ = gelu_both(y_ref[q, :, at])
+        o_ref[q, :, at] = (h.astype(LOW).astype(FULL) * gelu).astype(LOW)
+
+    each(finish)
+    neighbours(lambda copy: copy.wait_recv(), False)
+    neighbours(lambda copy: copy.wait_send(), True)
+    swap.wait_send()
+
+    @pl.when(seat < places - 1)
+    def _():
+        for copy in onward:
+            copy.wait_send()
+
+    @pl.when(seat > 0)
+    def _():
+        for copy in backward:
+            copy.wait_send()
+
+    for by in range(1, places):
+        share(by).wait_send()
+
+
+def pick_row(table, q):
+    place = lax.broadcasted_iota(jnp.int32, table.shape, 0)
+    return jnp.sum(jnp.where(place == q, table, 0.0), axis=0, keepdims=True)
+
+
+def mult_of(log_a, keep):
+    twice = 2.0 * log_a
+    gap = jnp.where(twice > -0.01, -expm1_small(twice), 1.0 - jnp.exp(twice))
+    return jnp.where(keep == 0.0, 1.0, jnp.sqrt(gap))
+
+
+def mid(n, places, taps, u, y, docs, rows8, gate_r, gate_i, slope):
+    _, rows, width = u.shape
+    head = gate_r.shape[1]
+    ext = -(-width // head) * head
+    full = jax.ShapeDtypeStruct(u.shape, FULL)
+    return pl.pallas_call(
+        functools.partial(mid_kernel, n, places, taps),
+        out_shape=[
+            jax.ShapeDtypeStruct(u.shape, LOW),
+            jax.ShapeDtypeStruct((n, rows, ext), LOW),
+            full,
+            full,
+            full,
+            jax.ShapeDtypeStruct((2 * n, width), FULL),
+            jax.ShapeDtypeStruct((n, 16, width), LOW),
+            jax.ShapeDtypeStruct((n, rows, rows), FULL),
+            jax.ShapeDtypeStruct((3,) + slope.shape, LOW),
+        ],
+        in_specs=[VMEM] * 4 + [ANY] * 2 + [VMEM],
+        out_specs=[VMEM] * 9,
+        scratch_shapes=[
+            pltpu.VMEM((ext, head), LOW),
+            pltpu.VMEM((ext, head), LOW),
+            pltpu.VMEM(u.shape, FULL),
+            pltpu.VMEM((places, 2 * n, width), FULL),
+            pltpu.VMEM(docs.shape, jnp.int32),
+            pltpu.VMEM(docs.shape, jnp.int32),
+            pltpu.SemaphoreType.DMA((3,)),
+            pltpu.SemaphoreType.DMA((3,)),
+            pltpu.SemaphoreType.DMA((1,)),
+            pltpu.SemaphoreType.DMA((1,)),
+            pltpu.SemaphoreType.DMA((places,)),
+            pltpu.SemaphoreType.DMA((places,)),
+            pltpu.SemaphoreType.DMA((2,)),
+            pltpu.SemaphoreType.DMA((2,)),
+            pltpu.SemaphoreType.DMA((2,)),
+        ],
+        compiler_params=comm_params(6),
+        cost_estimate=lasting(30),
+    )(u, y, docs, rows8, gate_r, gate_i, slope)
+
+
+def turn_kernel(
+    n,
+    places,
+    taps,
+    bits,
+    do_ref,
+    y_ref,
+    r_ref,
+    ii_ref,
+    h_ref,
+    edge_ref,
+    c_ref,
+    u_ref,
+    halo_ref,
+    mask_ref,
+    rows_ref,
+    gr_hbm,
+    gi_hbm,
+    down_hbm,
+    gate_hbm,
+    du_ref,
+    dy_ref,
+    small_ref,
+    down_ref,
+    kept_ref,
+    tr,
+    ti,
+    rem,
+    e_ref,
+    dra,
+    dia,
+    dc,
+    lead,
+    carry,
+    ein,
+    sums,
+    lands,
+    own,
+    hsent,
+    hlanded,
+    esent,
+    elanded,
+    csent,
+    clanded,
+    ssent,
+    slanded,
+    local,
+    psent,
+    planded,
+    blocks,
+    *landings,
+):
+    me = lax.axis_index("wt")
+    seat = lax.axis_index("seq")
+    part_len, width = u_ref.shape[1:]
+    head = gr_hbm.shape[1]
+    ext = tr.shape[0]
+    edge = ext - width
+    odd = lax.rem(me, 2)
+    shift = odd * edge
+    block = 128
+    per = head // block
+    reach = halo_ref.shape[1]
+    first = pl.multiple_of((me * width) // head * head, head)
+    loads = [
+        pltpu.make_async_copy(gr_hbm.at[pl.ds(first, ext), :], tr, local.at[0]),
+        pltpu.make_async_copy(gi_hbm.at[pl.ds(first, ext), :], ti, local.at[1]),
+        pltpu.make_async_copy(down_hbm.at[me], own, local.at[2]),
+        pltpu.make_async_copy(gate_hbm, blocks, local.at[3]),
+    ]
+    for load in loads:
+        load.start()
+    barrier = pltpu.get_barrier_semaphore()
+    for by in range(1, places):
+        other = {"seq": lax.rem(seat + by, places)}
+        pl.semaphore_signal(barrier, 1, device_id=other, device_id_type=MESH)
+    for by in range(1, n):
+        other = {"wt": lax.rem(me + by, n)}
+        pl.semaphore_signal(barrier, 1, device_id=other, device_id_type=MESH)
+    pl.semaphore_wait(barrier, places + n - 2)
+    spread = LineSpread(n, me, down_hbm, lands, ssent, slanded)
+    spread.start()
+    loads[3].wait()
+    plane = PlaneReduce(blocks, landings, psent, planded)
+    plane.begin((0,))
+
+    def columns(b):
+        return pl.ds(pl.multiple_of(b * block, block), block)
+
+    def ext_columns(b):
+        return pl.ds(pl.multiple_of(b * block + shift, block), block)
+
+    def head_columns(b):
+        spot = (b + shift // block) // per
+        return pl.ds(pl.multiple_of(spot * head, head), head)
+
+    def each(body):
+        def outer(q, carried):
+            def inner(b, deeper):
+                body(q, b)
+                return deeper
+
+            return lax.fori_loop(0, width // block, inner, carried)
+
+        lax.fori_loop(0, n, outer, 0)
+
+    def decay(q, at, rows=slice(None)):
+        log_a = rows_ref[taps + 2 : taps + 3, at] * r_ref[q, rows, at]
+        return jnp.exp(log_a.astype(LOW).astype(FULL)) * mask_ref[q, rows, 1:2]
+
+    place = lax.broadcasted_iota(jnp.int32, (part_len, block), 0)
+
+    def scans(q, b):
+        at = columns(b)
+        gelu, slope = gelu_both(y_ref[q, :, at])
+        back = do_ref[q, :, at]
+        hr = h_ref[q, :, at].astype(LOW).astype(FULL)
+        dy_ref[q, :, at] = (back * hr * slope).astype(LOW)
+        dh = (back * gelu).astype(LOW).astype(FULL)
+        a_next = jnp.where(
+            place < part_len - 1, pltpu.roll(decay(q, at), part_len - 1, 0), 1.0
+        )
+        far, e_loc = scan_rows(a_next, dh, True)
+        rem[q, :, at] = far
+        e_ref[q, :, at] = e_loc
+
+    each(scans)
+    carry[seat, :n, :] = edge_ref[n:, :]
+    for q in range(n):
+        top = decay(q, slice(None), slice(0, 1)) * e_ref[q, 0:1, :]
+        carry[seat, n + q : n + q + 1, :] = top
+
+    def share(by):
+        return pltpu.make_async_remote_copy(
+            src_ref=carry.at[seat],
+            dst_ref=carry.at[seat],
+            send_sem=csent.at[by],
+            recv_sem=clanded.at[by],
+            device_id={"seq": lax.rem(seat + by, places)},
+            device_id_type=MESH,
+        )
+
+    for by in range(1, places):
+        share(by).start()
+    sums[...] = jnp.zeros_like(sums)
+    for by in range(1, places):
+        share(by).wait_recv()
+    plane.begin((1,))
+    state = jnp.zeros((n, width), FULL)
+    start = state
+    for p in reversed(range(places)):
+        start = jnp.where(seat == p, state, start)
+        state = carry[p, :n, :] * state + carry[p, n:, :]
+    ein[:n, :] = start
+    ein[n:, :] = jnp.zeros_like(start)
+
+    def slopes(q, b):
+        at = columns(b)
+        e = e_ref[q, :, at] + rem[q, :, at] * pick_row(ein[:, at], q)
+        h_prev = jnp.where(
+            place == 0, pick_row(edge_ref[:, at], q), pltpu.roll(h_ref[q, :, at], 1, 0)
+        )
+        r = r_ref[q, :, at]
+        ii = ii_ref[q, :, at]
+        keep = mask_ref[q, :, 1:2]
+        soft = rows_ref[taps + 2 : taps + 3, at]
+        log_a = soft * r
+        mult = mult_of(log_a, keep)
+        c = c_ref[q, :, ext_columns(b)].astype(FULL)
+        dla = (e * h_prev * decay(q, at)).astype(LOW).astype(FULL)
+        dbr = e.astype(LOW).astype(FULL)
+        dmult = jnp.where(keep == 0.0, 0.0, -jnp.exp(2.0 * log_a) / mult)
+        dlog_a = dla + dbr * c * ii * dmult
+        dra_f = soft * dlog_a * r * (1.0 - r)
+        direct = dbr * mult * ii
+        dia_f = direct * c * (1.0 - ii)
+        dra[q, :, ext_columns(b)] = dra_f.astype(LOW)
+        dia[q, :, ext_columns(b)] = dia_f.astype(LOW)
+        dc[q, :, at] = direct
+        for k, value in enumerate([dra_f, dia_f, -8.0 * dlog_a * r]):
+            sums[taps + k : taps + k + 1, at] += jnp.sum(value, axis=0, keepdims=True)
+
+    each(slopes)
+    source = pl.ds(pl.multiple_of(jnp.where(odd == 1, edge, width - edge), edge), edge)
+    target = pl.ds(pl.multiple_of(jnp.where(odd == 1, width, 0), edge), edge)
+    swaps = [
+        pltpu.make_async_remote_copy(
+            src_ref=ref.at[:, :, source],
+            dst_ref=ref.at[:, :, target],
+            send_sem=esent.at[k],
+            recv_sem=elanded.at[k],
+            device_id={"wt": me + 1 - 2 * odd},
+            device_id_type=MESH,
+        )
+        for k, ref in enumerate([dra, dia])
+    ]
+    for swap in swaps:
+        swap.start()
+    for load in loads[:3]:
+        load.wait()
+    for swap in swaps:
+        swap.wait_recv()
+
+    def mix(q, b):
+        at = columns(b)
+        rows = head_columns(b)
+        table = ext_columns(b)
+        dc[q, :, at] += dot(dra[q, :, rows], tr[table, :], 1, 1) + dot(
+            dia[q, :, rows], ti[table, :], 1, 1
+        )
+
+    each(mix)
+    leads = pltpu.make_async_remote_copy(
+        src_ref=dc.at[:, pl.ds(0, lead.shape[1]), :],
+        dst_ref=lead,
+        send_sem=hsent.at[0],
+        recv_sem=hlanded.at[0],
+        device_id={"seq": seat - 1},
+        device_id_type=MESH,
+    )
+
+    @pl.when(seat > 0)
+    def _():
+        leads.start()
+
+    @pl.when(seat == places - 1)
+    def _():
+        lead[...] = jnp.zeros_like(lead)
+
+    def gate_grads(b, carried):
+        left = c_ref[:, :, ext_columns(b)].reshape(n * part_len, block)
+        rows = head_columns(b)
+        for k, ref in enumerate([dra, dia]):
+            right = ref[:, :, rows].reshape(n * part_len, head)
+            small_ref[columns(b), k * head : (k + 1) * head] = dot(left, right, 0, 0).astype(LOW)
+        return carried
+
+    lax.fori_loop(0, width // block, gate_grads, 0)
+
+    @pl.when(seat < places - 1)
+    def _():
+        leads.wait_recv()
+
+    plane.advance(0)
+
+    def conv(q, b):
+        at = columns(b)
+        slope = dc[q, :, at]
+        next_rows = lead[q, :, at]
+        long = jnp.concatenate([slope, next_rows], axis=0)
+        total = slope * rows_ref[0:1, at]
+        behind = jnp.concatenate([halo_ref[q, :, at], u_ref[q, :, at]], axis=0).astype(FULL)
+        sums[0:1, at] += jnp.sum(behind[reach:] * slope, axis=0, keepdims=True)
+        for k in range(1, taps):
+            same = mask_ref[q, :, k : k + 1]
+            same_next = mask_ref[q, : lead.shape[1], taps + k : taps + k + 1]
+            masked = long * jnp.concatenate([same, same_next], axis=0)
+            shifted = pltpu.roll(masked, long.shape[0] - k, 0)[:part_len]
+            total = total + shifted * rows_ref[k : k + 1, at]
+            window = pltpu.roll(behind, k, 0)[reach:] * same
+            sums[k : k + 1, at] += jnp.sum(window * slope, axis=0, keepdims=True)
+        du_ref[q, :, at] = total.astype(LOW)
+
+    each(conv)
+    row = taps + 2
+    sums[row : row + 1, :] = sums[row : row + 1, :] * jax.nn.sigmoid(rows_ref[taps + 3 : taps + 4, :])
+
+    def turn(b, carried):
+        wide = jnp.concatenate(
+            [sums[:, columns(b)], jnp.zeros((block - sums.shape[0], block), FULL)], axis=0
+        )
+        small_ref[columns(b), 2 * head : 2 * head + block] = wide.T.astype(LOW)
+        return carried
+
+    lax.fori_loop(0, width // block, turn, 0)
+    units = down_hbm.shape[-1]
+
+    def put(q, value):
+        down_ref[:, pl.ds(pl.multiple_of(q * units, 128), units)] = value.astype(FULL)
+
+    spread.take(put, own)
+    for step in range(1, bits):
+        plane.advance(step)
+    kept_ref[...] = plane.kept()[...]
+    plane.finish()
+    spread.finish()
+    for swap in swaps:
+        swap.wait_send()
+    for by in range(1, places):
+        share(by).wait_send()
+
+    @pl.when(seat > 0)
+    def _():
+        leads.wait_send()
+
+
+def turn_back(
+    n, places, taps, do, y, r, ii, h, edges, c, u, halo, mask, rows8, gate_r, gate_i, down, gate
+):
+    _, rows, width = u.shape
+    head = gate_r.shape[1]
+    ext = c.shape[2]
+    _, part, units = down.shape
+    bits = len(gate.shape) - 3
+    low = jax.ShapeDtypeStruct(u.shape, LOW)
+    return pl.pallas_call(
+        functools.partial(turn_kernel, n, places, taps, bits),
+        out_shape=[
+            low,
+            low,
+            jax.ShapeDtypeStruct((width, 2 * head + 128), LOW),
+            jax.ShapeDtypeStruct((part, n * units), FULL),
+            jax.ShapeDtypeStruct(gate.shape[bits:], LOW),
+        ],
+        in_specs=[VMEM] * 11 + [ANY] * 4,
+        out_specs=[VMEM] * 5,
+        scratch_shapes=[
+            pltpu.VMEM((ext, head), LOW),
+            pltpu.VMEM((ext, head), LOW),
+            pltpu.VMEM(u.shape, FULL),
+            pltpu.VMEM(u.shape, FULL),
+            pltpu.VMEM((n, rows, ext), LOW),
+            pltpu.VMEM((n, rows, ext), LOW),
+            pltpu.VMEM(u.shape, FULL),
+            pltpu.VMEM((n, 8, width), FULL),
+            pltpu.VMEM((places, 2 * n, width), FULL),
+            pltpu.VMEM((2 * n, width), FULL),
+            pltpu.VMEM((8, width), FULL),
+            pltpu.VMEM(down.shape, LOW),
+            pltpu.VMEM(down.shape[1:], LOW),
+            pltpu.SemaphoreType.DMA((1,)),
+            pltpu.SemaphoreType.DMA((1,)),
+            pltpu.SemaphoreType.DMA((2,)),
+            pltpu.SemaphoreType.DMA((2,)),
+            pltpu.SemaphoreType.DMA((places,)),
+            pltpu.SemaphoreType.DMA((places,)),
+            pltpu.SemaphoreType.DMA((n,)),
+            pltpu.SemaphoreType.DMA((n,)),
+            pltpu.SemaphoreType.DMA((4,)),
+            pltpu.SemaphoreType.DMA((2, 2 * bits)),
+            pltpu.SemaphoreType.DMA((2, 2 * bits)),
+            pltpu.VMEM(gate.shape, LOW),
+        ]
+        + plane_scratch(gate.shape),
+        compiler_params=comm_params(7),
+        cost_estimate=lasting(45),
+    )(do, y, r, ii, h, edges, c, u, halo, mask, rows8, gate_r, gate_i, down, gate)
 
 
 def on_device(
@@ -1372,92 +1972,30 @@
     head = recur_gate.shape[1]
     edge = width % head
     rows = shards * part_len
-    onward = [(s, s + 1) for s in range(places - 1)]
-    backward = [(s + 1, s) for s in range(places - 1)]
 
     def mine(vector):
         return lax.dynamic_slice_in_dim(vector, me_w * width, width, 0)
 
     x = inputs[0]
+    slope = cotangent[0]
     xn, u3, y, docs = enter(shards, x, mixer_gain[None], segment, input_weight, branch_weight)
-    docs = docs[:, 0]
-    reach = taps - 1
-    lead = lax.ppermute(docs[:, -reach:], "seq", onward)
-    trail = lax.ppermute(docs[:, :reach], "seq", backward)
-    lead = jnp.where(me_s == 0, -1, lead)
-    trail = jnp.where(me_s == places - 1, -1, trail)
-    window = jnp.concatenate([lead, docs, trail], axis=1)
-    same_wide = jnp.stack(
-        [
-            window[:, taps - 1 :] == window[:, taps - 1 - k : window.shape[1] - k]
-            for k in range(taps)
-        ],
-        axis=-1,
-    ).astype(FULL)
-    same = same_wide[:, :part_len]
-    keep = same[:, :, 1].reshape(rows, 1)
-    reset = keep == 0.0
-
-    y = y.reshape(rows, width)
-    slope = cotangent[0]
-
-    tail = u3[:, part_len - (taps - 1) :, :]
-    before = lax.ppermute(tail, "seq", onward)
-    extended = jnp.concatenate([before, u3], axis=1).astype(FULL)
-    conv_mine = mine(conv_weight)
-    windows = [
-        extended[:, taps - 1 - k : taps - 1 - k + part_len, :] * same[:, :, k : k + 1]
-        for k in range(taps)
-    ]
-    conv = sum(windows[k] * conv_mine[:, k] for k in range(taps))
-    c_low = conv.reshape(rows, width).astype(LOW)
-    c_ext = edge_swap(c_low, edge)
-    recur_table = head_rows(recur_gate, shards)
-    input_table = head_rows(input_gate, shards)
-    c = c_low.astype(FULL)
     rate = mine(decay_rate)
     soft = -8.0 * jax.nn.softplus(rate)
-    odd = (me_w % 2).astype(jnp.int32).reshape(1) * (edge // 128)
+    conv_mine = mine(conv_weight)
     rows8 = jnp.concatenate(
-        [jnp.stack([mine(recur_bias), mine(input_bias), soft]), jnp.zeros((5, width), FULL)]
+        [conv_mine.T, jnp.stack([mine(recur_bias), mine(input_bias), soft, rate])], axis=0
     )
-    r, ii, cum_a, h_loc = gates_scan(
-        c_ext, recur_table, input_table, rows8, keep, odd, part_len, width
+    y = y.reshape(u3.shape)
+    o, c_ext, r, ii, h, ends, halo, mask, near = mid(
+        shards, places, taps, u3, y, docs, rows8, recur_gate, input_gate, slope
     )
-    log_a = soft * r
-    mult = jnp.where(reset, 1.0, jnp.sqrt(-jnp.expm1(2.0 * log_a)))
-    a = jnp.exp(log_a.astype(LOW).astype(FULL)) * keep
-    a3 = a.reshape(shards, part_len, width)
-    cum_a = cum_a.reshape(a3.shape)
-    h_loc = h_loc.reshape(a3.shape)
-    ends = lax.all_gather(jnp.stack([cum_a[:, -1], h_loc[:, -1]]), "seq", axis=0)
-    carry = jnp.zeros((shards, width), FULL)
-    h_in = carry
-    for n in range(places):
-        h_in = jnp.where(me_s == n, carry, h_in)
-        carry = ends[n, 0] * carry + ends[n, 1]
-    h_in = h_in[:, None]
-    h = h_loc + cum_a * h_in
-    h_prev = jnp.concatenate([h_in, h[:, :-1]], axis=1).reshape(rows, width)
-    hr = h.reshape(rows, width).astype(LOW).astype(FULL)
-    gelu_y, grad_y = gelu_both(y)
-    o = (hr * gelu_y).astype(LOW)
-    x1, xn2, dm = close(shards, o.reshape(u3.shape), x, second_gain[None], output_weight, slope)
+    x1, xn2, dm = close(shards, o, x, second_gain[None], output_weight, near)
     dxn2, hidden, dg, dv, xn2, down_term = ffn(
         shards, places, xn2, dm, gate_weight, up_weight, down_weight
     )
-    groups = [list(range(k, places, 2)) for k in range(2)]
-
-    def summed(term):
-        return lax.psum_scatter(
-            term, "seq", scatter_dimension=0, tiled=True, axis_index_groups=groups
-        )
-
-    def spread(kept):
-        return lax.all_to_all(kept, "wt", split_axis=0, concat_axis=1, tiled=True)
-
     part = model // (places * shards)
     bits = (places // 2 - 1).bit_length()
+    cut = (2,) * bits + (shards, part, -1)
     dx1, dz, do, second_gain_grad, block_out, down_kept, gate_term, up_term = back_in(
         shards,
         places,
@@ -1465,7 +2003,7 @@
         x1,
         slope,
         second_gain[None],
-        down_term.reshape((2,) * bits + (shards, part, -1)),
+        down_term.reshape(cut),
         output_weight,
         down_weight,
         hidden,
@@ -1473,68 +2011,32 @@
         dg,
         dv,
     )
-    down_wide = spread(down_kept.reshape(shards * part, -1))
-    down_grad = down_wide.astype(FULL)
-    gate_kept = summed(gate_term)
-    up_kept = summed(up_term)
-    do = do.reshape(rows, width)
-
-    dh = (do * gelu_y).astype(LOW)
-    dy = (do * hr * grad_y).astype(LOW)
-
-    rem, e_loc = back_scan(dh, a, part_len)
-    rem = rem.reshape(a3.shape)
-    e_loc = e_loc.reshape(a3.shape)
-    heads_out = jnp.stack([cum_a[:, -1], a3[:, 0] * e_loc[:, 0]])
-    firsts = lax.all_gather(heads_out, "seq", axis=0)
-    carry = jnp.zeros((shards, width), FULL)
-    e_in = carry
-    for n in reversed(range(places)):
-        e_in = jnp.where(me_s == n, carry, e_in)
-        carry = firsts[n, 0] * carry + firsts[n, 1]
-    e_in = e_in[:, None]
-    e = (e_loc + rem * e_in).reshape(rows, width)
-    dla = (e * h_prev * a).astype(LOW).astype(FULL)
-    dbr = e.astype(LOW).astype(FULL)
-    dmult = jnp.where(reset, 0.0, -jnp.exp(2.0 * log_a) / mult)
-    dlog_a = dla + dbr * c * ii * dmult
-    dra_f = soft * dlog_a * r * (1.0 - r)
-    dia_f = dbr * mult * c * ii * (1.0 - ii)
-    recur_bias_grad = jnp.sum(dra_f, axis=0)
-    input_bias_grad = jnp.sum(dia_f, axis=0)
-    decay_grad = jnp.sum(-8.0 * dlog_a * r, axis=0) * jax.nn.sigmoid(rate)
-    slopes = jnp.concatenate([dra_f.astype(LOW), dia_f.astype(LOW)], axis=0)
-    slopes = edge_swap(slopes, edge)
-    dra, dia = slopes[:rows], slopes[rows:]
-    recur_gate_grad = heads_grad(c_ext, dra, head)
-    input_gate_grad = heads_grad(c_ext, dia, head)
-    mixed = heads_dot(dra, recur_table, True) + heads_dot(dia, input_table, True)
-    dc = (dbr * mult * ii + own_part(mixed, edge)).reshape(shards, part_len, width)
-    conv_grad = jnp.stack([jnp.sum(windows[k] * dc, axis=(0, 1)) for k in range(taps)], axis=-1)
-    lead = lax.ppermute(dc[:, : taps - 1], "seq", backward)
-    dc_ext = jnp.concatenate([dc, lead], axis=1)
-    du = sum(
-        (dc_ext * same_wide[:, :, k : k + 1])[:, k : k + part_len] * conv_mine[:, k]
-        for k in range(taps)
-    )
-    du = du.reshape(rows, width).astype(LOW)
-    small = jnp.concatenate(
-        [
-            own_part(recur_gate_grad.T, edge).T,
-            own_part(input_gate_grad.T, edge).T,
-            conv_grad,
-            recur_bias_grad[:, None],
-            input_bias_grad[:, None],
-            decay_grad[:, None],
-        ],
-        axis=1,
-    )
-    input_grad, mixer_gain_grad, mix_term, small = leave(
+    du, dy, small, down_grad, gate_kept = turn_back(
         shards,
         places,
-        du.reshape(u3.shape),
-        dy.reshape(u3.shape),
-        o.reshape(u3.shape),
+        taps,
+        do,
+        y,
+        r,
+        ii,
+        h,
+        ends,
+        c_ext,
+        u3,
+        halo,
+        mask,
+        rows8,
+        recur_gate,
+        input_gate,
+        down_kept,
+        gate_term.reshape(cut),
+    )
+    input_grad, mixer_gain_grad, mix_term, small, up_kept = leave(
+        shards,
+        places,
+        du,
+        dy,
+        o,
         x,
         dx1,
         mixer_gain[None],
@@ -1542,8 +2044,8 @@
         dz,
         input_weight,
         branch_weight,
-        down_wide,
-        jnp.pad(small, ((0, 0), (0, -small.shape[1] % 128))).astype(LOW).reshape(places, -1, -(-small.shape[1] // 128) * 128),
+        up_term.reshape(cut),
+        small.reshape(places, -1, small.shape[1]),
     )
     gains = jnp.concatenate(
         [mixer_gain_grad, second_gain_grad, jnp.zeros((6, model), FULL)], axis=0
@@ -1551,9 +2053,9 @@
     gate_grad, up_grad, out_grad, branch_grad, input_weight_grad, gains = settle(
         shards,
         places,
-        gate_kept.reshape(shards, part, -1),
-        up_kept.reshape(shards, part, -1),
-        mix_term.reshape((2,) * bits + (shards, part, -1)),
+        gate_kept,
+        up_kept,
+        mix_term.reshape(cut),
         gains,
     )
     gains = lax.dynamic_slice_in_dim(gains, (me_s * shards + me_w) * part, part, 1)

time: 638 us -> 590 us (0.925)
  Pallas kernels: 482 us -> 551 us
  local copies, waits for them, and re-layouts: 48.1 us -> 24.1 us
  other arithmetic: 24.8 us -> 2.21 us
  starting transfers between devices: 23.3 us -> 1.92 us
  blocking collectives: 20.2 us -> 0 us
  between operations: 15.4 us -> 1.22 us
  matrix products: 8.63 us -> 0 us
    pallas_call x3, Pallas kernels: 86.9 us -> 164 us  [the longest x1 68.4 us: leave(): pl.pallas_call(functools.partial(leave_kernel, n, places, bits), out_shap...]
    all_gather x2 -> x0, blocking collectives: 20.2 us -> none  [the longest x1 10.3 us: on_device(): firsts = lax.all_gather(heads_out, 'seq', axis=0)]
    ppermute x6 -> x0, starting transfers between devices: 14.3 us -> none  [the longest x2 4.74 us: edge_swap(): other = lax.ppermute(mine, 'wt', [(i, i ^ 1) for i in range(shards)])]
    convert_element_type x9 -> x0, other arithmetic: 13 us -> none  [the longest x1 3.4 us: on_device(): o = (hr * gelu_y).astype(LOW)]
    pallas_call x1, Pallas kernels: 67.4 us -> 55.4 us  [close(): pl.pallas_call(functools.partial(close_kernel, n), out_shape=[jax.ShapeDt...]
    dot_general x12 -> x0, matrix products: 8.63 us -> none  [dot(): lax.dot_general(left, right, (((left_dim,), (right_dim,)), ((), ())), pre...]
    unnamed x114 -> x23, local copies, waits for them, and re-layouts: 19.8 us -> 13 us
  transfers between devices with their start and end apart: 10 -> 1, of which waited for: 2 -> 0; matrix products, arithmetic and copies ran while one was open for 8% -> 1% of each run, Pallas kernels for 11% -> 17%
where the time goes in v4:
time: 590 us; the launch traced here: 580 us
  Pallas kernels  551 us (93%)
  local copies, waits for them, and re-layouts  24.1 us (4%)
    pallas_call x1, Pallas kernels, ffn(): pl.pallas_call(functools.partial(ffn_kernel, n, places), out_shape=[jax.S...  103 us
    pallas_call x1, Pallas kernels, settle(): pl.pallas_call(functools.partial(settle_kernel, n, places, bits), out_sha...  97.4 us
    pallas_call x1, Pallas kernels, back_in(): pl.pallas_call(functools.partial(back_in_kernel, n, places, bits), out_sh...  81.4 us
    pallas_call x1, Pallas kernels, leave(): pl.pallas_call(functools.partial(leave_kernel, n, places, bits), out_shap...  68.4 us
    pallas_call x1, Pallas kernels, turn_back(): pl.pallas_call(functools.partial(turn_kernel, n, places, taps, bits), out...  60.4 us
    pallas_call x1, Pallas kernels, close(): pl.pallas_call(functools.partial(close_kernel, n), out_shape=[jax.ShapeDt...  55.4 us
    pallas_call x1, Pallas kernels, enter(): pl.pallas_call(functools.partial(enter_kernel, n), out_shape=[jax.ShapeDt...  49.1 us
    pallas_call x1, Pallas kernels, mid(): pl.pallas_call(functools.partial(mid_kernel, n, places, taps), out_shape=...  35.2 us
  transfers between devices with their start and end apart: 1, of which 0 were waited for; matrix products, arithmetic and copies ran while one was open for 1% of the time, Pallas kernels for 17%

profile of v4, /device:TPU:10, one launch (start us, length us, event | category | flops | bytes accessed | tf_op | source)
XLA Modules:
  0.0 580.0 jit_solution(10632582842563262964)
XLA Ops:
  0.7 0.8 dynamic_slice.16
  1.4 0.8 dynamic_slice.17
  2.2 0.8 fusion
  3.0 0.7 dynamic-slice_bitcast_fusion
  3.7 1.3 broadcast_in_dim.17.gain_ref
  5.0 1.3 broadcast_in_dim.18.gain_ref.refs_3_
  6.3 0.6 concatenate.6.rows_ref
  7.0 49.1 %shard_map.288 = (bf16[4,128,2560]{2,1,0:T(8,128)(2,1)}, bf16[4,128,640]{2,1,0:T(8,128)(2,1)}, f32[4,128,640]{2,1,0:T(8,128)}, s32[4,8,128]{2,1,0:T(8,128)}) custom-call(bf16[128,2560]{1,0:T(8,128)(2,1)} %bitcast.19, f32[1,2560]{1,0:T(1,128)} %broadcast_in_dim.17.gain_ref, s32[1,128]{1,0:T(1,128)} %doc_ref.1, bf16[2560,640]{1,0:T(8,128)(2,1)} %win_hbm.3, ...), custom_call_target="tpu_custom_call" | custom-call | flops 49999998976 | bytes 170000000 | tf_op jit(solution)/shard_map/pallas_call | solution.py:415
  56.1 35.2 %shard_map.289 = (bf16[4,128,640]{2,1,0:T(8,128)(2,1)}, bf16[4,128,768]{2,1,0:T(8,128)(2,1)}, f32[4,128,640]{2,1,0:T(8,128)}, f32[4,128,640]{2,1,0:T(8,128)}, f3...) custom-call(bf16[4,128,640]{2,1,0:T(8,128)(2,1)} %get-tuple-element., ...), custom_call_target="tpu_custom_call" | custom-call | flops 30000001024 | bytes 102000000 | tf_op jit(solution)/shard_map/pallas_call | solution.py:1559
  91.2 55.4 %shard_map.290 = (f32[128,2560]{1,0:T(8,128)}, bf16[128,2560]{1,0:T(8,128)(2,1)}, bf16[4,128,2560]{2,1,0:T(8,128)(2,1)}) custom-call(bf16[4,128,640]{2,1,0:T(8,128)(2,1)} %get-tuple-element.65.o_ref, bf16[128,2560]{1,0:T(8,128)(2,1)} %bitcast.20, f32[1,2560]{1,0:T(1,128)} %broadcast_in_dim.18.gain_ref.refs_3_, bf16[2560,640]{1,0:T(8,128)(2,1)} %refs_5_.1, ...), custom_call_target="tpu_custom_call" | custom-call | flops 54999998464 | bytes 187000000 | tf_op jit(solution)/shard_map/pallas_call | solution.py:486
  146.6 103.4 %shard_map.291 = (f32[128,2560]{1,0:T(8,128)}, bf16[4,128,1920]{2,1,0:T(8,128)(2,1)}, bf16[4,128,1920]{2,1,0:T(8,128)(2,1)}, bf16[4,128,1920]{2,1,0:T(8,128)(2,1...) custom-call(bf16[128,2560]{1,0:T(8,128)(2,1)} %get-tuple-element.67.xn2_ref, ...), custom_call_target="tpu_custom_call" | custom-call | flops 105000001536 | bytes 357000000 | tf_op jit(solution)/shard_map/pallas_call | solution.py:809
  250.0 81.4 %shard_map.292 = (f32[128,2560]{1,0:T(8,128)}, bf16[4,128,2560]{2,1,0:T(8,128)(2,1)}, f32[4,128,640]{2,1,0:T(8,128)}, f32[1,2560]{1,0:T(1,128)}, bf16[128,2560]{...) custom-call(f32[128,2560]{1,0:T(8,128)} %get-tuple-element.69.refs_0_, ...), custom_call_target="tpu_custom_call" | custom-call | flops 74999996416 | bytes 255000000 | tf_op jit(solution)/shard_map/pallas_call | solution.py:924
  331.4 60.4 %shard_map.293 = (bf16[4,128,640]{2,1,0:T(8,128)(2,1)}, bf16[4,128,640]{2,1,0:T(8,128)(2,1)}, bf16[640,640]{1,0:T(8,128)(2,1)}, f32[80,7680]{1,0:T(8,128)}, bf16[4,80,1920]{2,1,0:T(8,128)(2,1)}) custom-call(f32[4,128,640]{2,1,0:T(8,128)} %get-tuple-element.77.do_ref, f32[4,128,640]{2,1,0:T(8,128)} %get-tuple-element.63.y_ref, ...), custom_call_target="tpu_custom_call" | custom-call | flops 44999999488 | bytes 153000000 | tf_op jit(solution)/shard_map/pallas_call | solution.py:1901
  391.8 68.4 %shard_map.294 = (f32[128,2560]{1,0:T(8,128)}, f32[1,2560]{1,0:T(1,128)}, bf16[1280,1920]{1,0:T(8,128)(2,1)}, f32[80,640]{1,0:T(8,128)}, bf16[4,80,1920]{2,1,0:T(8,128)(2,1)}) custom-call(bf16[4,128,640]{2,1,0:T(8,128)(2,1)} %get-tuple-element.87.du_ref, bf16[4,128,640]{2,1,0:T(8,128)(2,1)} %get-tuple-element.88.dy_ref, ...), custom_call_target="tpu_custom_call" | custom-call | flops 60000002048 | bytes 204000000 | tf_op jit(solution)/shard_map/pallas_call | solution.py:1104
  460.2 1.9 collective-permute-start
  462.2 1.4 maximum_maximum_fusion.gains_ref
  463.6 97.4 %shard_map.295 = (f32[80,7680]{1,0:T(8,128)}, f32[80,7680]{1,0:T(8,128)}, f32[80,2560]{1,0:T(8,128)}, f32[80,2560]{1,0:T(8,128)}, f32[80,2560]{1,0:T(8,128)}, /*index=5*/f32[8,2560]{1,0:T(8,128)}) custom-call(bf16[4,80,1920]{2,1,0:T(8,128)(2,1)} %get-tuple-element.95.gate_hbm, bf16[4,80,1920]{2,1,0:T(8,128)(2,1)} %get-tuple-element.96.up_hbm, ...), custom_call_target="tpu_custom_call" | custom-call | flops 99999997952 | bytes 340000000 | tf_op jit(solution)/shard_map/pallas_call | solution.py:1271
  561.0 0.9 constant_dynamic-slice_fusion
  562.5 0.8 slice.32
  563.3 0.7 copy.34
  563.9 1.6 slice_reduce_fusion
  565.6 1.6 fusion.1
  567.2 2.0 copy.43
  569.2 1.1 copy.44
  570.3 0.9 copy.45
  571.2 0.9 copy.46
  572.1 0.9 copy.47
  572.9 1.4 copy.48
  574.4 1.1 copy-done.1
  575.5 1.4 copy.49
  577.0 1.1 copy-done
  578.1 1.4 copy.50
  (20 shorter events, 0.6 us)
Async XLA Ops:
  460.2 102.3 %collective-permute-start = (f32[80,640]{1,0:T(8,128)}, f32[80,640]{1,0:T(8,128)}, u32[]{:S(2)}, u32[]{:S(2)}) collective-permute-start(f32[80,640]{1,0:T(8,128)} %get-tuple-element.103), channel_id=1, source_target_pairs={{0,0},{1,8},{2,16},{3,24},{4,1},{5,9},{6,17},{7,25},{8,2},{9,10},{... | collective-permute-start | bytes 614408 | tf_op jit(solution)/shard_map/ppermute | solution.py:2066
  561.0 8.2 %copy-start.3 = (f32[128,2560]{1,0:T(8,128)S(1)}, f32[128,2560]{1,0:T(8,128)}, u32[]{:S(2)}) copy-start(f32[128,2560]{1,0:T(8,128)} %get-tuple-element.94) | copy-start | bytes 3932164
  561.0 9.2 %copy-start.6 = (f32[80,2560]{1,0:T(8,128)S(1)}, f32[80,2560]{1,0:T(8,128)}, u32[]{:S(2)}) copy-start(f32[80,2560]{1,0:T(8,128)} %get-tuple-element.168) | copy-start | bytes 2457604
  567.2 4.0 copy-start.5
  569.2 2.9 copy-start.4
  570.3 2.7 copy-start.2
  572.9 2.6 copy-start.1
  575.5 2.6 copy-start

commit v5 on v4

--- a/solution.py
+++ b/solution.py
@@ -94,6 +94,25 @@
             step = 1 << k
             other = {"seq": place + step * (1 - 2 * lax.rem(place // step, 2))}
             pl.semaphore_signal(barrier, 1, device_id=other, device_id_type=MESH)
+    pl.semaphore_wait(barrier, peers)
+
+
+def greet_all(n, me, places, more, away):
+    barrier = pltpu.get_barrier_semaphore()
+    seat = lax.axis_index("seq")
+    for by in range(1, n):
+        other = {"wt": lax.rem(me + by, n)}
+        pl.semaphore_signal(barrier, 1, device_id=other, device_id_type=MESH)
+    for by in range(1, places):
+        other = {"seq": lax.rem(seat + by, places)}
+        pl.semaphore_signal(barrier, 1, device_id=other, device_id_type=MESH)
+
+    @pl.when(away)
+    def _():
+        for other in more:
+            pl.semaphore_signal(barrier, 1, device_id=other, device_id_type=MESH)
+
+    peers = n + places - 2 + len(more) * away.astype(jnp.int32)
     pl.semaphore_wait(barrier, peers)
 
 
@@ -368,142 +387,6 @@
     )
 
 
-def enter_kernel(
-    n, x_ref, gain_ref, doc_ref, win_hbm, wbr_hbm, xn_ref, u_ref, y_ref, docs_ref, win, wbr, docs, sent, landed, dsent, dlanded, local
-):
-    me = lax.axis_index("wt")
-    loads = [
-        pltpu.make_async_copy(win_hbm, win, local.at[0]),
-        pltpu.make_async_copy(wbr_hbm, wbr, local.at[1]),
-    ]
-    for load in loads:
-        load.start()
-    docs[me] = jnp.broadcast_to(doc_ref[...], docs.shape[1:])
-    flat = x_ref[...].astype(FULL)
-    scale = lax.rsqrt(jnp.mean(flat * flat, axis=-1, keepdims=True) + EPSILON)
-    xn_ref[me] = (flat * scale * gain_ref[...]).astype(LOW)
-    greet(n, me)
-    notes = LineGather(n, me, docs, dsent, dlanded)
-    line = LineGather(n, me, xn_ref, sent, landed)
-    notes.start()
-    line.start()
-    for load in loads:
-        load.wait()
-
-    def use(q):
-        block = xn_ref[q]
-        u_ref[q] = dot(block, win[...]).astype(LOW)
-        y_ref[q] = dot(block, wbr[...])
-
-    use(me)
-
-    def step(d, carry):
-        notes.arrive(d)
-        line.arrive(d)
-        line.each(d, use)
-        return carry
-
-    lax.fori_loop(1, n, step, 0)
-    docs_ref[...] = docs[...]
-    notes.finish()
-    line.finish()
-
-
-def enter(n, x, gain, doc, win, wbr):
-    rows, model = x.shape
-    width = win.shape[1]
-    return pl.pallas_call(
-        functools.partial(enter_kernel, n),
-        out_shape=[
-            jax.ShapeDtypeStruct((n, rows, model), LOW),
-            jax.ShapeDtypeStruct((n, rows, width), LOW),
-            jax.ShapeDtypeStruct((n, rows, width), FULL),
-            jax.ShapeDtypeStruct((n, 8, rows), jnp.int32),
-        ],
-        in_specs=[VMEM, VMEM, VMEM, ANY, ANY],
-        out_specs=[VMEM, VMEM, VMEM, VMEM],
-        scratch_shapes=[
-            pltpu.VMEM(win.shape, LOW),
-            pltpu.VMEM(wbr.shape, LOW),
-            pltpu.VMEM((n, 8, rows), jnp.int32),
-        ]
-        + gather_sems(n)
-        + gather_sems(n)
-        + [pltpu.SemaphoreType.DMA((2,))],
-        compiler_params=comm_params(0),
-        cost_estimate=lasting(50),
-    )(x, gain, doc, win, wbr)
-
-
-def close_kernel(
-    n, o_ref, x_ref, gain_ref, w_ref, near_hbm, x1_ref, xn2_ref, dm_ref, parts, slots, sent, landed, gsent, glanded, local
-):
-    me = lax.axis_index("wt")
-    model = w_ref.shape[0]
-
-    def near(k, act):
-        q = me + k - 1
-
-        @pl.when((q >= 0) & (q < n))
-        def _():
-            act(pltpu.make_async_copy(near_hbm.at[k], dm_ref.at[q], local.at[k]))
-
-    for k in range(3):
-        near(k, lambda copy: copy.start())
-    greet(n, me)
-
-    def partial(q):
-        block = o_ref[q]
-
-        def tile(at):
-            parts[q, :, at] = dot(block, w_ref[at, :], 1, 1).astype(LOW)
-
-        tiles(model, tile_of(model, 512), tile)
-
-    def finish(total):
-        x1 = x_ref[...].astype(FULL) + total
-        x1_ref[...] = x1
-        scale = lax.rsqrt(jnp.mean(x1 * x1, axis=-1, keepdims=True) + EPSILON)
-        xn2_ref[...] = (x1 * scale * gain_ref[...]).astype(LOW)
-
-    back = LineReduce(n, me, parts, slots, sent, landed)
-    both = LineBoth(LineGather(n, me, dm_ref, gsent, glanded), back, 1)
-    for k in range(3):
-        near(k, lambda copy: copy.wait())
-    back.prepare(0, partial)
-    both.step(0)
-    for k in range(1, n - 1):
-        back.prepare(k, partial)
-    partial(me)
-    for t in range(1, n - 1):
-        both.step(t)
-    finish(back.total())
-    both.finish()
-
-
-def close(n, o, x, gain, weight, near):
-    rows, model = x.shape
-    return pl.pallas_call(
-        functools.partial(close_kernel, n),
-        out_shape=[
-            jax.ShapeDtypeStruct((rows, model), FULL),
-            jax.ShapeDtypeStruct((rows, model), LOW),
-            jax.ShapeDtypeStruct((n, rows, model), LOW),
-        ],
-        in_specs=[VMEM] * 4 + [ANY],
-        out_specs=[VMEM] * 3,
-        scratch_shapes=[
-            pltpu.VMEM((n, rows, model), LOW),
-            pltpu.VMEM((2, n - 1, rows, model), LOW),
-        ]
-        + reduce_sems(n)
-        + gather_sems(n)
-        + [pltpu.SemaphoreType.DMA((3,))],
-        compiler_params=comm_params(1),
-        cost_estimate=lasting(55),
-    )(o, x, gain, weight, near)
-
-
 class PairSum:
     def __init__(self, part, halves, landing, sent, landed, free, flush):
         self.me = lax.axis_index("seq")
@@ -610,9 +493,10 @@
 
 
 class PlaneReduce:
-    def __init__(self, blocks, landings, sent, landed):
+    def __init__(self, blocks, landings, sent, landed, tail=3):
         self.blocks, self.landings, self.sent, self.landed = blocks, landings, sent, landed
-        self.bits = len(blocks.shape) - 3
+        self.bits = len(blocks.shape) - tail
+        self.tail = tail
         self.me = lax.axis_index("seq")
         self.columns = column_halves(blocks.shape[-1])
 
@@ -636,13 +520,14 @@
             place[dim] = self.mine(dim)
         now = order[step]
         place[now] = self.mine(now) if own else 1 - self.mine(now)
-        return tuple(place) + (slice(None), slice(None), pl.ds(*self.columns[side]))
+        return tuple(place) + (slice(None),) * (self.tail - 1) + (pl.ds(*self.columns[side]),)
 
     def send(self, side, step, piece=0):
         at, landing = self.index(side, step, False), self.landings[2 * step + side]
         if step == 0:
-            count = self.blocks.shape[-3] // 2
-            rows = pl.ds(piece * count, count)
+            count = self.blocks.shape[self.bits]
+            first = count // 2 if self.tail == 3 else count // 32 * 16
+            rows = pl.ds(piece * first, count - first if piece else first)
             at = at[: self.bits] + (rows,) + at[self.bits + 1 :]
             landing = landing.at[(slice(None),) * (self.bits - 1) + (rows,)]
         return pltpu.make_async_remote_copy(
@@ -682,12 +567,12 @@
                     self.send(side, step, piece).wait_send()
 
 
-def plane_scratch(shape):
-    bits = len(shape) - 3
+def plane_scratch(shape, tail=3):
+    bits = len(shape) - tail
     landings = []
     for step in range(bits):
         for _, width in column_halves(shape[-1]):
-            rest = [2] * (bits - 1 - step) + [shape[-3], shape[-2], width]
+            rest = [2] * (bits - 1 - step) + list(shape[bits:-1]) + [width]
             landings.append(pltpu.VMEM(tuple(rest), LOW))
     return landings
 
@@ -890,15 +775,16 @@
     use(me)
     for load in loads[2:4]:
         load.wait()
-    back.prepare(0, partial)
+    for k in range(n - 2):
+        back.prepare(k, partial)
     work = pair.tasks(model // size, pair_dot(xall, dg, part, size), gate_hbm)
     work += pair.tasks(model // size, pair_dot(xall, dv, part, size), up_hbm)
-    share = -(-len(work) // (n - 1))
+    ends = [len(work) * max(4 * t - 1, 0) // (4 * (n - 1)) for t in range(n)]
+    ends[-1] = len(work)
     for t in range(1, n):
         both.step(t)
         if t == 1:
-            for k in range(1, n - 1):
-                back.prepare(k, partial)
+            back.prepare(n - 2, partial)
         if t >= 2 and t - 2 < bits:
             plane.advance(t - 2)
         line.each(t, use)
@@ -906,7 +792,7 @@
             partial(me)
             for load in loads[4:]:
                 load.wait()
-        for task in work[(t - 1) * share : t * share]:
+        for task in work[ends[t - 1] : ends[t]]:
             task()
     for step in range(max(n - 2, 0), bits):
         plane.advance(step)
@@ -992,151 +878,6 @@
             self.send(by).wait_send()
 
 
-def leave_kernel(
-    n,
-    places,
-    bits,
-    du_ref,
-    dy_ref,
-    o_ref,
-    x_ref,
-    dx1_ref,
-    gain_ref,
-    xn_hbm,
-    dz_hbm,
-    win_hbm,
-    wbr_hbm,
-    up_hbm,
-    small_ref,
-    grad_ref,
-    sum_ref,
-    mix_hbm,
-    passed_ref,
-    kept_ref,
-    xn,
-    dz,
-    win,
-    wbr,
-    parts,
-    slots,
-    halves,
-    landing,
-    psent,
-    planded,
-    free,
-    pflush,
-    sent,
-    landed,
-    lands,
-    ssent,
-    slanded,
-    local,
-    usent,
-    ulanded,
-    blocks,
-    *landings,
-):
-    me = lax.axis_index("wt")
-    loads = [
-        pltpu.make_async_copy(source, target, local.at[k])
-        for k, (source, target) in enumerate(
-            [(win_hbm, win), (wbr_hbm, wbr), (up_hbm, blocks), (xn_hbm, xn), (dz_hbm, dz)]
-        )
-    ]
-    for load in loads:
-        load.start()
-    greet(n, me, False, 0, places)
-    small = PlaneShare(places, small_ref, lands, ssent, slanded)
-    small.start()
-    plane = PlaneReduce(blocks, landings, usent, ulanded)
-    for load in loads[:2]:
-        load.wait()
-
-    def early():
-        loads[2].wait()
-        plane.begin()
-        for load in loads[3:]:
-            load.wait()
-
-    model = win.shape[0]
-
-    def partial(q):
-        def tile(at):
-            total = dot(du_ref[q], win[at, :], 1, 1) + dot(dy_ref[q], wbr[at, :], 1, 1)
-            parts[q, :, at] = total.astype(LOW)
-
-        tiles(model, tile_of(model, 512), tile)
-
-    part = model // places
-    size = pair_tile(model, places)
-    width = du_ref.shape[2]
-    pair = PairSum(part, halves, landing, psent, planded, free, pflush)
-
-    def compute(t, target):
-        for k, (left, right) in enumerate([(dz, o_ref), (xn, dy_ref), (xn, du_ref)]):
-            columns = pl.ds(k * width, width)
-            pair_dot(left, right, part, size)(t, target.at[:, :, columns])
-
-    work = pair.tasks(model // size, compute, mix_hbm)
-
-    def finish(total):
-        flat = x_ref[...].astype(FULL)
-        scale = lax.rsqrt(jnp.mean(flat * flat, axis=-1, keepdims=True) + EPSILON)
-        q1 = total * gain_ref[...]
-        pull = jnp.mean(q1 * flat, axis=-1, keepdims=True)
-        grad_ref[...] = dx1_ref[...] + scale * (q1 - flat * (scale * scale * pull))
-        sum_ref[...] = jnp.sum(total * flat * scale, axis=0, keepdims=True)
-
-    tasks = work[:-1] + [lambda: (work[-1](), plane.advance(0))]
-    line_reduce(n, me, parts, slots, sent, landed, partial, tasks, finish, early)
-    pair.finish(mix_hbm)
-    small.finish(passed_ref)
-    for step in range(1, bits):
-        plane.advance(step)
-    kept_ref[...] = plane.kept()[...]
-    plane.finish()
-
-
-def leave(n, places, du, dy, o, x, dx1, gain, xn, dz, win, wbr, up, small):
-    bits = len(up.shape) - 3
-    rows, model = x.shape
-    width = win.shape[1]
-    return pl.pallas_call(
-        functools.partial(leave_kernel, n, places, bits),
-        out_shape=[
-            jax.ShapeDtypeStruct((rows, model), FULL),
-            jax.ShapeDtypeStruct((1, model), FULL),
-            jax.ShapeDtypeStruct((model // 2, 3 * width), LOW),
-            jax.ShapeDtypeStruct(small.shape[1:], FULL),
-            jax.ShapeDtypeStruct(up.shape[bits:], LOW),
-        ],
-        in_specs=[VMEM] * 6 + [ANY] * 5 + [VMEM],
-        out_specs=[VMEM, VMEM, ANY, VMEM, VMEM],
-        scratch_shapes=[
-            pltpu.VMEM((n, rows, model), LOW),
-            pltpu.VMEM((n, rows, model), LOW),
-            pltpu.VMEM(win.shape, LOW),
-            pltpu.VMEM(wbr.shape, LOW),
-            pltpu.VMEM((n, rows, model), LOW),
-            pltpu.VMEM((2, n - 1, rows, model), LOW),
-        ]
-        + pair_scratch(pair_tile(model, places) // 2, 3 * width)
-        + reduce_sems(n)
-        + [
-            pltpu.VMEM(small.shape, LOW),
-            pltpu.SemaphoreType.DMA((places,)),
-            pltpu.SemaphoreType.DMA((places,)),
-            pltpu.SemaphoreType.DMA((5,)),
-            pltpu.SemaphoreType.DMA((2, 2 * bits)),
-            pltpu.SemaphoreType.DMA((2, 2 * bits)),
-            pltpu.VMEM(up.shape, LOW),
-        ]
-        + plane_scratch(up.shape),
-        compiler_params=comm_params(4),
-        cost_estimate=lasting(60),
-    )(du, dy, o, x, dx1, gain, xn, dz, win, wbr, up, small)
-
-
 class LineSpread:
     def __init__(self, n, me, source, lands, sent, landed):
         self.n, self.me, self.source, self.lands = n, me, source, lands
@@ -1165,36 +906,97 @@
             self.send(by).wait_send()
 
 
-def settle_kernel(n, places, bits, gate_hbm, up_hbm, mix_hbm, gains_ref, gate_ref, up_ref, out_ref, branch_ref, in_ref, total_ref, *scratch):
-    blocks, landings, scratch = scratch[0], scratch[1 : 1 + 2 * bits], scratch[1 + 2 * bits :]
-    lands, own, notes, around, psent, planded, ssent, slanded, gsent, glanded, local = scratch
+def leave_kernel(n, places, bits, *refs):
+    du_ref, dy_ref, o_ref, x_ref, dx1_ref, gain_ref, second_ref, small_ref = refs[:8]
+    xn_hbm, dz_hbm, win_hbm, wbr_hbm, up_hbm, gate_hbm = refs[8:14]
+    grad_ref, total_ref, moved_ref, gate_ref, up_ref, out_ref, branch_ref, in_ref, mix_hbm = refs[14:23]
+    xn, dz, win, wbr, parts, slots, blocks, kept, own, lands, notes, around, shares, passed = refs[23:37]
+    landings = refs[37 : 37 + 2 * bits]
+    others = refs[37 + 2 * bits : 37 + 4 * bits]
+    sems = refs[37 + 4 * bits :]
+    halves, landing, psent, planded, free, pflush, sent, landed, ssent, slanded = sems[:10]
+    usent, ulanded, msent, mlanded, asent, alanded, gsent, glanded, hsent, hlanded, local, fill = sems[10:]
     me = lax.axis_index("wt")
     seat = lax.axis_index("seq")
+    model, width = win.shape
+    units = gate_hbm.shape[-1]
+    part = kept.shape[1]
+    rows = n * part
+
+    def fills(source):
+        copies = []
+        for k in range(1 << bits):
+            place = tuple((k >> (bits - 1 - dim)) & 1 for dim in range(bits))
+            copies.append(
+                pltpu.make_async_copy(
+                    source.at[pl.ds(k * rows, rows), :], blocks.at[place], fill.at[k]
+                )
+            )
+        return copies
+
     loads = [
-        pltpu.make_async_copy(mix_hbm, blocks, local.at[0]),
-        pltpu.make_async_copy(gate_hbm.at[me], own.at[0], local.at[1]),
-        pltpu.make_async_copy(up_hbm.at[me], own.at[1], local.at[2]),
+        pltpu.make_async_copy(source, target, local.at[k])
+        for k, (source, target) in enumerate(
+            [(win_hbm, win), (wbr_hbm, wbr), (xn_hbm, xn), (dz_hbm, dz), (gate_hbm.at[me], own)]
+        )
     ]
-    for load in loads:
+    for load in loads[:2] + fills(up_hbm) + loads[2:]:
         load.start()
-    notes[me] = gains_ref[...]
-    barrier = pltpu.get_barrier_semaphore()
-    for by in range(1, n):
-        pl.semaphore_signal(
-            barrier, 1, device_id={"wt": lax.rem(me + by, n)}, device_id_type=MESH
-        )
-    for by in range(1, places):
-        pl.semaphore_signal(
-            barrier, 1, device_id={"seq": lax.rem(seat + by, places)}, device_id_type=MESH
-        )
-    pl.semaphore_wait(barrier, n + places - 2)
-    loads[0].wait()
-    plane = PlaneReduce(blocks, landings, psent, planded)
-    plane.begin()
+    flat_to, flat_from = me * places + seat, seat * n + me
+    goal = {"seq": flat_to // n, "wt": lax.rem(flat_to, n)}
+    origin = {"seq": lax.rem(flat_from, places), "wt": flat_from // places}
+    away = flat_to != flat_from
+    greet_all(n, me, places, [goal, origin], away)
+    small = PlaneShare(places, small_ref, shares, ssent, slanded)
+    small.start()
+    plane = PlaneReduce(blocks, landings, usent, ulanded, 2)
+    for load in loads[:2]:
+        load.wait()
+
+    def partial(q):
+        def tile(at):
+            total = dot(du_ref[q], win[at, :], 1, 1) + dot(dy_ref[q], wbr[at, :], 1, 1)
+            parts[q, :, at] = total.astype(LOW)
+
+        tiles(model, tile_of(model, 512), tile)
+
+    size = pair_tile(model, places)
+    pair = PairSum(rows, halves, landing, psent, planded, free, pflush)
+
+    def compute(t, target):
+        for k, (left, right) in enumerate([(dz, o_ref), (xn, dy_ref), (xn, du_ref)]):
+            columns = pl.ds(k * width, width)
+            pair_dot(left, right, rows, size)(t, target.at[:, :, columns])
+
+    def early():
+        for copy in fills(up_hbm):
+            copy.wait()
+        plane.begin()
+        for load in loads[2:]:
+            load.wait()
+
+    def finish(total):
+        flat = x_ref[...].astype(FULL)
+        scale = lax.rsqrt(jnp.mean(flat * flat, axis=-1, keepdims=True) + EPSILON)
+        q1 = total * gain_ref[...]
+        pull = jnp.mean(q1 * flat, axis=-1, keepdims=True)
+        grad_ref[...] = dx1_ref[...] + scale * (q1 - flat * (scale * scale * pull))
+        mine = jnp.sum(total * flat * scale, axis=0, keepdims=True)
+        blank = jnp.zeros((notes.shape[1] - 2, model), FULL)
+        notes[me] = jnp.concatenate([mine, second_ref[...], blank], axis=0)
+
+    def keep(k, source):
+        for q in range(n):
+            kept[k * n + q] = source[q * part : (q + 1) * part, :]
+
     spreads = [
-        LineSpread(n, me, source, lands.at[k], ssent.at[k], slanded.at[k])
-        for k, source in enumerate([gate_hbm, up_hbm])
+        LineSpread(n, me, source, lands.at[k], asent.at[k], alanded.at[k])
+        for k, source in enumerate([gate_hbm, kept.at[pl.ds(0, n)], kept.at[pl.ds(n, n)]])
     ]
+    work = pair.tasks(model // size, compute, mix_hbm)
+    tasks = work[:-1] + [lambda: (work[-1](), plane.advance(0), spreads[0].start())]
+    line_reduce(n, me, parts, slots, sent, landed, partial, tasks, finish, early)
+    pair.finish(mix_hbm)
 
     def note(by):
         to = lax.rem(me + by, n)
@@ -1202,31 +1004,65 @@
 
     for by in range(1, n):
         note(by).start()
-    for spread in spreads:
-        spread.start()
+    for step in range(1, bits):
+        plane.advance(step)
+    keep(0, plane.kept())
+    spreads[1].start()
+    plane.finish()
+    for copy in fills(mix_hbm):
+        copy.start()
+    for copy in fills(mix_hbm):
+        copy.wait()
+    mixing = PlaneReduce(blocks, others, msent, mlanded, 2)
+    mixing.begin()
+    small.finish(passed)
+    move = pltpu.make_async_remote_copy(
+        src_ref=passed,
+        dst_ref=moved_ref,
+        send_sem=hsent.at[0],
+        recv_sem=hlanded.at[0],
+        device_id=goal,
+        device_id_type=MESH,
+    )
+
+    @pl.when(away)
+    def _():
+        move.start()
+
+    @pl.when(jnp.logical_not(away))
+    def _():
+        moved_ref[...] = passed[...]
+
     for by in range(1, n):
         slot = notes.at[lax.rem(me + n - by, n)]
         remote(slot, slot, gsent.at[0, by], glanded.at[0, by], me).wait_recv()
     around[seat] = jnp.sum(notes[...], axis=0)
 
     def share(by):
-        to = lax.rem(seat + by, places)
         return pltpu.make_async_remote_copy(
             src_ref=around.at[seat],
             dst_ref=around.at[seat],
             send_sem=gsent.at[1, by],
             recv_sem=glanded.at[1, by],
-            device_id={"seq": to},
+            device_id={"seq": lax.rem(seat + by, places)},
             device_id_type=MESH,
         )
 
     for by in range(1, places):
         share(by).start()
+
+    def put_into(target):
+        def put(q, value):
+            target[:, pl.ds(pl.multiple_of(q * units, 128), units)] = value
+
+        return put
+
+    spreads[0].take(put_into(gate_ref), own)
     for step in range(bits):
-        plane.advance(step)
-    kept = plane.kept()
-    last = LineSpread(n, me, kept, lands.at[2], ssent.at[2], slanded.at[2])
-    last.start()
+        mixing.advance(step)
+    keep(1, mixing.kept())
+    spreads[2].start()
+    spreads[1].take(put_into(up_ref), kept.at[me])
     for by in range(1, places):
         slot = around.at[lax.rem(seat + places - by, places)]
         pltpu.make_async_remote_copy(
@@ -1238,59 +1074,88 @@
             device_id_type=MESH,
         ).wait_recv()
     total_ref[...] = jnp.sum(around[...], axis=0)
-    units = gate_hbm.shape[-1]
-    for k, (spread, target) in enumerate(zip(spreads, [gate_ref, up_ref])):
-        loads[1 + k].wait()
-
-        def put(q, value, target=target):
-            target[:, pl.ds(pl.multiple_of(q * units, 128), units)] = value.astype(FULL)
-
-        spread.take(put, own.at[k])
-    width = units // 3
 
     def put_mix(q, value):
         columns = pl.ds(pl.multiple_of(q * width, 128), width)
         for k, target in enumerate([out_ref, branch_ref, in_ref]):
-            target[:, columns] = value[:, k * width : (k + 1) * width].astype(FULL)
-
-    last.take(put_mix, kept.at[me])
-    plane.finish()
-    for spread in spreads + [last]:
+            target[:, columns] = value[:, k * width : (k + 1) * width]
+
+    spreads[2].take(put_mix, kept.at[n + me])
+    mixing.finish()
+    for spread in spreads:
         spread.finish()
     for by in range(1, n):
         note(by).wait_send()
     for by in range(1, places):
         share(by).wait_send()
 
-
-def settle(n, places, gate, up, mix, gains):
+    @pl.when(away)
+    def _():
+        move.wait()
+
+
+def leave(n, places, du, dy, o, x, dx1, gain, second, small, xn, dz, win, wbr, up, gate):
+    rows, model = x.shape
+    width = win.shape[1]
     _, part, units = gate.shape
-    bits = len(mix.shape) - 3
-    wide = jax.ShapeDtypeStruct((part, n * units), FULL)
-    thin = jax.ShapeDtypeStruct((part, n * units // 3), FULL)
+    bits = (model // 2 // (n * part)).bit_length() - 1
+    blocks = (2,) * bits + (n * part, units)
+    wide = jax.ShapeDtypeStruct((part, n * units), LOW)
+    thin = jax.ShapeDtypeStruct((part, n * width), LOW)
     return pl.pallas_call(
-        functools.partial(settle_kernel, n, places, bits),
-        out_shape=[wide, wide, thin, thin, thin, jax.ShapeDtypeStruct(gains.shape, FULL)],
-        in_specs=[ANY, ANY, ANY, VMEM],
-        out_specs=[VMEM] * 6,
-        scratch_shapes=[pltpu.VMEM(mix.shape, LOW)]
-        + plane_scratch(mix.shape)
+        functools.partial(leave_kernel, n, places, bits),
+        out_shape=[
+            jax.ShapeDtypeStruct((rows, model), FULL),
+            jax.ShapeDtypeStruct((8, model), FULL),
+            jax.ShapeDtypeStruct(small.shape[1:], FULL),
+            wide,
+            wide,
+            thin,
+            thin,
+            thin,
+            jax.ShapeDtypeStruct(up.shape, LOW),
+        ],
+        in_specs=[VMEM] * 8 + [ANY] * 6,
+        out_specs=[VMEM] * 8 + [ANY],
+        scratch_shapes=[
+            pltpu.VMEM((n, rows, model), LOW),
+            pltpu.VMEM((n, rows, model), LOW),
+            pltpu.VMEM(win.shape, LOW),
+            pltpu.VMEM(wbr.shape, LOW),
+            pltpu.VMEM((n, rows, model), LOW),
+            pltpu.VMEM((2, n - 1, rows, model), LOW),
+            pltpu.VMEM(blocks, LOW),
+            pltpu.VMEM((2 * n, part, units), LOW),
+            pltpu.VMEM((part, units), LOW),
+            pltpu.VMEM((3, n, part, units), LOW),
+            pltpu.VMEM((n, 8, model), FULL),
+            pltpu.VMEM((places, 8, model), FULL),
+            pltpu.VMEM(small.shape, LOW),
+            pltpu.VMEM(small.shape[1:], FULL),
+        ]
+        + plane_scratch(blocks, 2)
+        + plane_scratch(blocks, 2)
+        + pair_scratch(pair_tile(model, places) // 2, 3 * width)
+        + reduce_sems(n)
         + [
-            pltpu.VMEM((3, n, part, units), LOW),
-            pltpu.VMEM((2, part, units), LOW),
-            pltpu.VMEM((n,) + gains.shape, FULL),
-            pltpu.VMEM((places,) + gains.shape, FULL),
+            pltpu.SemaphoreType.DMA((places,)),
+            pltpu.SemaphoreType.DMA((places,)),
+            pltpu.SemaphoreType.DMA((2, 2 * bits)),
+            pltpu.SemaphoreType.DMA((2, 2 * bits)),
             pltpu.SemaphoreType.DMA((2, 2 * bits)),
             pltpu.SemaphoreType.DMA((2, 2 * bits)),
             pltpu.SemaphoreType.DMA((3, n)),
             pltpu.SemaphoreType.DMA((3, n)),
             pltpu.SemaphoreType.DMA((2, max(n, places))),
             pltpu.SemaphoreType.DMA((2, max(n, places))),
-            pltpu.SemaphoreType.DMA((3,)),
+            pltpu.SemaphoreType.DMA((1,)),
+            pltpu.SemaphoreType.DMA((1,)),
+            pltpu.SemaphoreType.DMA((5,)),
+            pltpu.SemaphoreType.DMA((1 << bits,)),
         ],
-        compiler_params=comm_params(5),
-        cost_estimate=lasting(100),
-    )(gate, up, mix, gains)
+        compiler_params=comm_params(4),
+        cost_estimate=lasting(140),
+    )(du, dy, o, x, dx1, gain, second, small, xn, dz, win, wbr, up, gate)
 
 
 def conv_masks(own, before, after, taps):
@@ -1302,6 +1167,103 @@
             lines.append((shifted == here).astype(FULL)[:1] if k else jnp.ones_like(here)[:1])
     lines.append(jnp.zeros((own.shape[1] - 2 * taps, own.shape[1]), FULL))
     return jnp.concatenate(lines, axis=0).T
+
+
+def pick_row(table, q):
+    place = lax.broadcasted_iota(jnp.int32, table.shape, 0)
+    return jnp.sum(jnp.where(place == q, table, 0.0), axis=0, keepdims=True)
+
+
+def mult_of(log_a, keep):
+    twice = 2.0 * log_a
+    gap = jnp.where(twice > -0.01, -expm1_small(twice), 1.0 - jnp.exp(twice))
+    return jnp.where(keep == 0.0, 1.0, jnp.sqrt(gap))
+
+
+def enter_kernel(
+    n, x_ref, gain_ref, doc_ref, win_hbm, wbr_hbm, xn_ref, u_ref, y_ref, docs_ref, win, wbr, docs, sent, landed, dsent, dlanded, local, places
+):
+    me = lax.axis_index("wt")
+    loads = [
+        pltpu.make_async_copy(win_hbm, win, local.at[0]),
+        pltpu.make_async_copy(wbr_hbm, wbr, local.at[1]),
+    ]
+    for load in loads:
+        load.start()
+    docs[me] = jnp.broadcast_to(doc_ref[...], docs.shape[1:])
+    flat = x_ref[...].astype(FULL)
+    scale = lax.rsqrt(jnp.mean(flat * flat, axis=-1, keepdims=True) + EPSILON)
+    xn_ref[me] = (flat * scale * gain_ref[...]).astype(LOW)
+    greet(n, me, False, 0, places)
+    notes = LineGather(n, me, docs, dsent, dlanded)
+    line = LineGather(n, me, xn_ref, sent, landed)
+    notes.start()
+    line.start()
+    for load in loads:
+        load.wait()
+
+    def use(q):
+        block = xn_ref[q]
+        u_ref[q] = dot(block, win[...]).astype(LOW)
+        y_ref[q] = dot(block, wbr[...])
+
+    use(me)
+
+    def step(d, carry):
+        notes.arrive(d)
+        line.arrive(d)
+        line.each(d, use)
+        return carry
+
+    lax.fori_loop(1, n, step, 0)
+    docs_ref[...] = docs[...]
+    notes.finish()
+    line.finish()
+
+
+def close_kernel(
+    n, o_ref, x_ref, gain_ref, w_hbm, near_ref, x1_ref, xn2_ref, dm_ref, parts, slots, sent, landed, gsent, glanded, local, w_ref
+):
+    me = lax.axis_index("wt")
+    model = w_ref.shape[0]
+
+    def near(k, act):
+        q = me + k - 1
+
+        @pl.when((q >= 0) & (q < n))
+        def _():
+            act(pltpu.make_async_copy(near_ref.at[k], dm_ref.at[q], local.at[k]))
+
+    for k in range(3):
+        near(k, lambda copy: copy.start())
+
+    def partial(q):
+        block = o_ref[q]
+
+        def tile(at):
+            parts[q, :, at] = dot(block, w_ref[at, :], 1, 1).astype(LOW)
+
+        tiles(model, tile_of(model, 512), tile)
+
+    def finish(total):
+        x1 = x_ref[...].astype(FULL) + total
+        x1_ref[...] = x1
+        scale = lax.rsqrt(jnp.mean(x1 * x1, axis=-1, keepdims=True) + EPSILON)
+        xn2_ref[...] = (x1 * scale * gain_ref[...]).astype(LOW)
+
+    back = LineReduce(n, me, parts, slots, sent, landed)
+    both = LineBoth(LineGather(n, me, dm_ref, gsent, glanded), back, 1)
+    for k in range(3):
+        near(k, lambda copy: copy.wait())
+    back.prepare(0, partial)
+    both.step(0)
+    for k in range(1, n - 1):
+        back.prepare(k, partial)
+    partial(me)
+    for t in range(1, n - 1):
+        both.step(t)
+    finish(back.total())
+    both.finish()
 
 
 def mid_kernel(
@@ -1358,7 +1320,6 @@
         load.start()
     partner = {"wt": me + 1 - 2 * odd}
     near_ref[1] = slope_ref[...].astype(LOW)
-    greet(n, me, False, 0, places)
 
     def neighbours(act, out):
         for k, (to, there) in enumerate([(me + 1, 0), (me - 1, 2)]):
@@ -1427,7 +1388,7 @@
                 body(q, b)
                 return deeper
 
-            return lax.fori_loop(0, width // block, inner, carried)
+            return lax.fori_loop(0, width // block, inner, carried, unroll=True)
 
         lax.fori_loop(0, n, outer, 0)
 
@@ -1540,26 +1501,41 @@
         share(by).wait_send()
 
 
-def pick_row(table, q):
-    place = lax.broadcasted_iota(jnp.int32, table.shape, 0)
-    return jnp.sum(jnp.where(place == q, table, 0.0), axis=0, keepdims=True)
-
-
-def mult_of(log_a, keep):
-    twice = 2.0 * log_a
-    gap = jnp.where(twice > -0.01, -expm1_small(twice), 1.0 - jnp.exp(twice))
-    return jnp.where(keep == 0.0, 1.0, jnp.sqrt(gap))
-
-
-def mid(n, places, taps, u, y, docs, rows8, gate_r, gate_i, slope):
-    _, rows, width = u.shape
+def head_kernel(n, places, taps, *refs):
+    x, gain, doc, rows8, slope, second, win_hbm, wbr_hbm, gr_hbm, gi_hbm, w_hbm = refs[:11]
+    xn, u, y, o, c, r, ii, h, edges, halo, mask, x1, xn2, dm = refs[11:25]
+    win, wbr, docs, seen, near, tr, ti, cum, carry, before, after, parts, slots, w = refs[25:39]
+    sems = refs[39:]
+    load = pltpu.make_async_copy(w_hbm, w, sems[-1].at[0])
+    load.start()
+    enter_kernel(
+        n, x, gain, doc, win_hbm, wbr_hbm, xn, u, y, seen, win, wbr, docs, *sems[:5], places
+    )
+    mid_kernel(
+        n, places, taps, u, y, seen, rows8, gr_hbm, gi_hbm, slope, o, c, r, ii, h, edges, halo, mask, near,
+        tr, ti, cum, carry, before, after, *sems[5:14]
+    )
+    load.wait()
+    close_kernel(n, o, x, second, w_hbm, near, x1, xn2, dm, parts, slots, *sems[14:19], w)
+
+
+def head_part(n, places, taps, x, gain, doc, rows8, slope, second, win, wbr, gate_r, gate_i, weight):
+    rows, model = x.shape
+    width = win.shape[1]
     head = gate_r.shape[1]
     ext = -(-width // head) * head
-    full = jax.ShapeDtypeStruct(u.shape, FULL)
+    full = jax.ShapeDtypeStruct((n, rows, width), FULL)
+    low = jax.ShapeDtypeStruct((n, rows, width), LOW)
+    long = jax.ShapeDtypeStruct((n, rows, model), LOW)
+    docs = pltpu.VMEM((n, 8, rows), jnp.int32)
+    pairs = [pltpu.SemaphoreType.DMA((count,)) for count in (3, 3, 1, 1, places, places, 2, 2, 2)]
     return pl.pallas_call(
-        functools.partial(mid_kernel, n, places, taps),
+        functools.partial(head_kernel, n, places, taps),
         out_shape=[
-            jax.ShapeDtypeStruct(u.shape, LOW),
+            long,
+            low,
+            full,
+            low,
             jax.ShapeDtypeStruct((n, rows, ext), LOW),
             full,
             full,
@@ -1567,30 +1543,38 @@
             jax.ShapeDtypeStruct((2 * n, width), FULL),
             jax.ShapeDtypeStruct((n, 16, width), LOW),
             jax.ShapeDtypeStruct((n, rows, rows), FULL),
-            jax.ShapeDtypeStruct((3,) + slope.shape, LOW),
+            jax.ShapeDtypeStruct((rows, model), FULL),
+            jax.ShapeDtypeStruct((rows, model), LOW),
+            long,
         ],
-        in_specs=[VMEM] * 4 + [ANY] * 2 + [VMEM],
-        out_specs=[VMEM] * 9,
+        in_specs=[VMEM] * 6 + [ANY] * 5,
+        out_specs=[VMEM] * 14,
         scratch_shapes=[
+            pltpu.VMEM(win.shape, LOW),
+            pltpu.VMEM(wbr.shape, LOW),
+            docs,
+            docs,
+            pltpu.VMEM((3, rows, model), LOW),
             pltpu.VMEM((ext, head), LOW),
             pltpu.VMEM((ext, head), LOW),
-            pltpu.VMEM(u.shape, FULL),
+            pltpu.VMEM((n, rows, width), FULL),
             pltpu.VMEM((places, 2 * n, width), FULL),
-            pltpu.VMEM(docs.shape, jnp.int32),
-            pltpu.VMEM(docs.shape, jnp.int32),
-            pltpu.SemaphoreType.DMA((3,)),
-            pltpu.SemaphoreType.DMA((3,)),
-            pltpu.SemaphoreType.DMA((1,)),
-            pltpu.SemaphoreType.DMA((1,)),
-            pltpu.SemaphoreType.DMA((places,)),
-            pltpu.SemaphoreType.DMA((places,)),
-            pltpu.SemaphoreType.DMA((2,)),
-            pltpu.SemaphoreType.DMA((2,)),
-            pltpu.SemaphoreType.DMA((2,)),
-        ],
-        compiler_params=comm_params(6),
-        cost_estimate=lasting(30),
-    )(u, y, docs, rows8, gate_r, gate_i, slope)
+            docs,
+            docs,
+            pltpu.VMEM((n, rows, model), LOW),
+            pltpu.VMEM((2, n - 1, rows, model), LOW),
+            pltpu.VMEM(weight.shape, LOW),
+        ]
+        + gather_sems(n)
+        + gather_sems(n)
+        + [pltpu.SemaphoreType.DMA((2,))]
+        + pairs
+        + reduce_sems(n)
+        + gather_sems(n)
+        + [pltpu.SemaphoreType.DMA((3,)), pltpu.SemaphoreType.DMA((1,))],
+        compiler_params=comm_params(0),
+        cost_estimate=lasting(135),
+    )(x, gain, doc, rows8, slope, second, win, wbr, gate_r, gate_i, weight)
 
 
 def turn_kernel(
@@ -1695,7 +1679,7 @@
                 body(q, b)
                 return deeper
 
-            return lax.fori_loop(0, width // block, inner, carried)
+            return lax.fori_loop(0, width // block, inner, carried, unroll=True)
 
         lax.fori_loop(0, n, outer, 0)
 
@@ -1871,7 +1855,7 @@
     units = down_hbm.shape[-1]
 
     def put(q, value):
-        down_ref[:, pl.ds(pl.multiple_of(q * units, 128), units)] = value.astype(FULL)
+        down_ref[:, pl.ds(pl.multiple_of(q * units, 128), units)] = value
 
     spread.take(put, own)
     for step in range(1, bits):
@@ -1904,7 +1888,7 @@
             low,
             low,
             jax.ShapeDtypeStruct((width, 2 * head + 128), LOW),
-            jax.ShapeDtypeStruct((part, n * units), FULL),
+            jax.ShapeDtypeStruct((part, n * units), LOW),
             jax.ShapeDtypeStruct(gate.shape[bits:], LOW),
         ],
         in_specs=[VMEM] * 11 + [ANY] * 4,
@@ -1942,6 +1926,26 @@
     )(do, y, r, ii, h, edges, c, u, halo, mask, rows8, gate_r, gate_i, down, gate)
 
 
+def widen_kernel(count, *refs):
+    for source, target in zip(refs[:count], refs[count:]):
+        target[...] = source[...].astype(target.dtype)
+
+
+def widen(n, terms, kept):
+    arrays = terms + kept
+    blocks = [
+        pl.BlockSpec((term.shape[0], term.shape[1] // n), lambda k: (0, k)) for term in arrays
+    ]
+    return pl.pallas_call(
+        functools.partial(widen_kernel, len(arrays)),
+        grid=(n,),
+        in_specs=blocks,
+        out_specs=blocks,
+        out_shape=[jax.ShapeDtypeStruct(term.shape, FULL) for term in terms]
+        + [jax.ShapeDtypeStruct(term.shape, term.dtype) for term in kept],
+    )(*arrays)
+
+
 def on_device(
     inputs,
     segment,
@@ -1978,18 +1982,28 @@
 
     x = inputs[0]
     slope = cotangent[0]
-    xn, u3, y, docs = enter(shards, x, mixer_gain[None], segment, input_weight, branch_weight)
     rate = mine(decay_rate)
     soft = -8.0 * jax.nn.softplus(rate)
     conv_mine = mine(conv_weight)
     rows8 = jnp.concatenate(
         [conv_mine.T, jnp.stack([mine(recur_bias), mine(input_bias), soft, rate])], axis=0
     )
-    y = y.reshape(u3.shape)
-    o, c_ext, r, ii, h, ends, halo, mask, near = mid(
-        shards, places, taps, u3, y, docs, rows8, recur_gate, input_gate, slope
+    xn, u3, y, o, c_ext, r, ii, h, ends, halo, mask, x1, xn2, dm = head_part(
+        shards,
+        places,
+        taps,
+        x,
+        mixer_gain[None],
+        segment,
+        rows8,
+        slope,
+        second_gain[None],
+        input_weight,
+        branch_weight,
+        recur_gate,
+        input_gate,
+        output_weight,
     )
-    x1, xn2, dm = close(shards, o, x, second_gain[None], output_weight, near)
     dxn2, hidden, dg, dv, xn2, down_term = ffn(
         shards, places, xn2, dm, gate_weight, up_weight, down_weight
     )
@@ -2031,7 +2045,7 @@
         down_kept,
         gate_term.reshape(cut),
     )
-    input_grad, mixer_gain_grad, mix_term, small, up_kept = leave(
+    input_grad, gains, small, gate_grad, up_grad, out_grad, branch_grad, input_weight_grad, _ = leave(
         shards,
         places,
         du,
@@ -2040,30 +2054,28 @@
         x,
         dx1,
         mixer_gain[None],
+        second_gain_grad,
+        small.reshape(places, -1, small.shape[1]),
         xn,
         dz,
         input_weight,
         branch_weight,
-        up_term.reshape(cut),
-        small.reshape(places, -1, small.shape[1]),
+        up_term,
+        gate_kept,
     )
-    gains = jnp.concatenate(
-        [mixer_gain_grad, second_gain_grad, jnp.zeros((6, model), FULL)], axis=0
-    )
-    gate_grad, up_grad, out_grad, branch_grad, input_weight_grad, gains = settle(
-        shards,
-        places,
-        gate_kept,
-        up_kept,
-        mix_term.reshape(cut),
-        gains,
-    )
+    terms = [down_grad, gate_grad, up_grad, out_grad, branch_grad, input_weight_grad]
+    (
+        down_grad,
+        gate_grad,
+        up_grad,
+        out_grad,
+        branch_grad,
+        input_weight_grad,
+        input_grad,
+        block_out,
+    ) = widen(shards, terms, [input_grad, block_out])
     gains = lax.dynamic_slice_in_dim(gains, (me_s * shards + me_w) * part, part, 1)
 
-    moves = [
-        (s * shards + w, w * places + s) for s in range(places) for w in range(shards)
-    ]
-    small = lax.ppermute(small, ("seq", "wt"), moves)
     at = 2 * head + taps
     return (
         block_out[None],

time: 590 us -> 563 us (0.954)
  local copies, waits for them, and re-layouts: 24.1 us -> 11.5 us
  Pallas kernels: 551 us -> 540 us
    pallas_call x1, Pallas kernels: 68.4 us -> 162 us  [leave(): pl.pallas_call(functools.partial(leave_kernel, n, places, bits), out_shap...]
    pallas_call x4 -> x2, Pallas kernels: 237 us -> 143 us  [the longest x1 136 us: head_part(): pl.pallas_call(functools.partial(head_kernel, n, places, taps), out_shape...]
    unnamed x23 -> x1, local copies, waits for them, and re-layouts: 13 us -> 0.65 us
    pallas_call x1, Pallas kernels: 81.4 us -> 71 us  [back_in(): pl.pallas_call(functools.partial(back_in_kernel, n, places, bits), out_sh...]
  transfers between devices with their start and end apart: 1 -> 0, of which waited for: 0 -> 0; matrix products, arithmetic and copies ran while one was open for 1% -> 0% of each run, Pallas kernels for 17% -> 0%
where the time goes in v5:
time: 563 us; the launch traced here: 554 us
  Pallas kernels  540 us (96%)
  local copies, waits for them, and re-layouts  11.5 us (2%)
    pallas_call x1, Pallas kernels, leave(): pl.pallas_call(functools.partial(leave_kernel, n, places, bits), out_shap...  162 us
    pallas_call x1, Pallas kernels, head_part(): pl.pallas_call(functools.partial(head_kernel, n, places, taps), out_shape...  136 us
    pallas_call x1, Pallas kernels, ffn(): pl.pallas_call(functools.partial(ffn_kernel, n, places), out_shape=[jax.S...  104 us
    pallas_call x1, Pallas kernels, back_in(): pl.pallas_call(functools.partial(back_in_kernel, n, places, bits), out_sh...  71 us
    pallas_call x1, Pallas kernels, turn_back(): pl.pallas_call(functools.partial(turn_kernel, n, places, taps, bits), out...  59.1 us

profile of v5, /device:TPU:10, one launch (start us, length us, event | category | flops | bytes accessed | tf_op | source)
XLA Modules:
  0.0 553.7 jit_solution(11101029556472350877)
XLA Ops:
  0.7 0.8 dynamic_slice.16
  1.4 0.8 dynamic_slice.17
  2.2 0.8 fusion
  3.0 0.7 dynamic-slice_bitcast_fusion
  3.7 0.6 concatenate.3.refs_3_.rows_ref
  4.4 1.3 broadcast_in_dim.14.refs_1_.refs_5_
  5.7 1.3 broadcast_in_dim.15.refs_5_.refs_3_
  7.0 135.5 %shard_map.288 = (bf16[4,128,2560]{2,1,0:T(8,128)(2,1)}, bf16[4,128,640]{2,1,0:T(8,128)(2,1)}, f32[4,128,640]{2,1,0:T(8,128)}, bf16[4,128,640]{2,1,0:T(8,128)(2,...) custom-call(bf16[128,2560]{1,0:T(8,128)(2,1)} %bitcast.16, ...), custom_call_target="tpu_custom_call" | custom-call | flops 134999998464 | bytes 459000000 | tf_op jit(solution)/shard_map/pallas_call | solution.py:1532
  142.5 104.5 %shard_map.289 = (f32[128,2560]{1,0:T(8,128)}, bf16[4,128,1920]{2,1,0:T(8,128)(2,1)}, bf16[4,128,1920]{2,1,0:T(8,128)(2,1)}, bf16[4,128,1920]{2,1,0:T(8,128)(2,1...) custom-call(bf16[128,2560]{1,0:T(8,128)(2,1)} %get-tuple-element.65.xn2_ref, ...), custom_call_target="tpu_custom_call" | custom-call | flops 105000001536 | bytes 357000000 | tf_op jit(solution)/shard_map/pallas_call | solution.py:694
  247.0 71.0 %shard_map.290 = (f32[128,2560]{1,0:T(8,128)}, bf16[4,128,2560]{2,1,0:T(8,128)(2,1)}, f32[4,128,640]{2,1,0:T(8,128)}, f32[1,2560]{1,0:T(1,128)}, bf16[128,2560]{...) custom-call(f32[128,2560]{1,0:T(8,128)} %get-tuple-element.67.refs_0_, ...), custom_call_target="tpu_custom_call" | custom-call | flops 74999996416 | bytes 255000000 | tf_op jit(solution)/shard_map/pallas_call | solution.py:810
  318.0 59.1 %shard_map.291 = (bf16[4,128,640]{2,1,0:T(8,128)(2,1)}, bf16[4,128,640]{2,1,0:T(8,128)(2,1)}, bf16[640,640]{1,0:T(8,128)(2,1)}, bf16[80,7680]{1,0:T(8,128)(2,1)}, bf16[4,80,1920]{2,1,0:T(8,128)(2,1)}) custom-call(f32[4,128,640]{2,1,0:T(8,128)} %get-tuple-element.74.do_ref, f32[4,128,640]{2,1,0:T(8,128)} %get-tuple-element.75.y_ref, ...), custom_call_target="tpu_custom_call" | custom-call | flops 44999999488 | bytes 153000000 | tf_op jit(solution)/shard_map/pallas_call | solution.py:1885
  377.2 162.3 %shard_map.292 = (f32[128,2560]{1,0:T(8,128)}, f32[8,2560]{1,0:T(8,128)}, f32[80,640]{1,0:T(8,128)}, bf16[80,7680]{1,0:T(8,128)(2,1)}, bf16[80,7680]{1,0:T(8,128...) custom-call(bf16[4,128,640]{2,1,0:T(8,128)(2,1)} %get-tuple-element., ...), custom_call_target="tpu_custom_call" | custom-call | flops 140000002048 | bytes 476000000 | tf_op jit(solution)/shard_map/pallas_call | solution.py:1105
  539.4 1.6 slice_reduce_fusion
  541.1 0.8 constant_dynamic-slice_fusion
  541.9 0.5 slice_bitcast_fusion
  542.4 0.8 slice.25
  543.2 1.6 fusion.1
  544.8 0.7 copy.34
  545.4 7.9 %shard_map.293 = (f32[80,7680]{1,0:T(8,128)}, f32[80,7680]{1,0:T(8,128)}, f32[80,7680]{1,0:T(8,128)}, f32[80,2560]{1,0:T(8,128)}, f32[80,2560]{1,0:T(8,128)}, /*...) custom-call(bf16[80,7680]{1,0:T(8,128)(2,1)} %get-tuple-element.86.refs_0_, ...), custom_call_target="tpu_custom_call" | custom-call | tf_op jit(solution)/shard_map/pallas_call | solution.py:1939
  (4 shorter events, 0.0 us)

commit v6 on v5

--- a/solution.py
+++ b/solution.py
@@ -744,7 +744,7 @@
     dxn2 = dxn2_ref[...]
     model = x1.shape[1]
     scale = lax.rsqrt(jnp.mean(x1 * x1, axis=-1, keepdims=True) + EPSILON)
-    q2 = dxn2 * gain_ref[...]
+    q2 = dxn2 * gain_ref[gain_ref.shape[0] - 1 :, :]
     pull = jnp.mean(q2 * x1, axis=-1, keepdims=True)
     dx1 = slope_ref[...] + scale * (q2 - x1 * (scale * scale * pull))
     dx1_ref[...] = dx1
@@ -978,7 +978,7 @@
     def finish(total):
         flat = x_ref[...].astype(FULL)
         scale = lax.rsqrt(jnp.mean(flat * flat, axis=-1, keepdims=True) + EPSILON)
-        q1 = total * gain_ref[...]
+        q1 = total * gain_ref[gain_ref.shape[0] - 2 : gain_ref.shape[0] - 1, :]
         pull = jnp.mean(q1 * flat, axis=-1, keepdims=True)
         grad_ref[...] = dx1_ref[...] + scale * (q1 - flat * (scale * scale * pull))
         mine = jnp.sum(total * flat * scale, axis=0, keepdims=True)
@@ -1502,10 +1502,14 @@
 
 
 def head_kernel(n, places, taps, *refs):
-    x, gain, doc, rows8, slope, second, win_hbm, wbr_hbm, gr_hbm, gi_hbm, w_hbm = refs[:11]
-    xn, u, y, o, c, r, ii, h, edges, halo, mask, x1, xn2, dm = refs[11:25]
-    win, wbr, docs, seen, near, tr, ti, cum, carry, before, after, parts, slots, w = refs[25:39]
-    sems = refs[39:]
+    x, doc, table, slope, win_hbm, wbr_hbm, gr_hbm, gi_hbm, w_hbm = refs[:9]
+    xn, u, y, o, c, r, ii, h, edges, halo, mask, x1, xn2, dm, rows8 = refs[9:24]
+    win, wbr, docs, seen, near, tr, ti, cum, carry, before, after, parts, slots, w = refs[24:38]
+    sems = refs[38:]
+    width = u.shape[2]
+    first = pl.multiple_of(lax.axis_index("wt") * width, 128)
+    rows8[...] = table[: taps + 4, pl.ds(first, width)]
+    gain, second = table.at[pl.ds(taps + 4, 1)], table.at[pl.ds(taps + 5, 1)]
     load = pltpu.make_async_copy(w_hbm, w, sems[-1].at[0])
     load.start()
     enter_kernel(
@@ -1519,7 +1523,7 @@
     close_kernel(n, o, x, second, w_hbm, near, x1, xn2, dm, parts, slots, *sems[14:19], w)
 
 
-def head_part(n, places, taps, x, gain, doc, rows8, slope, second, win, wbr, gate_r, gate_i, weight):
+def head_part(n, places, taps, x, doc, table, slope, win, wbr, gate_r, gate_i, weight):
     rows, model = x.shape
     width = win.shape[1]
     head = gate_r.shape[1]
@@ -1546,9 +1550,10 @@
             jax.ShapeDtypeStruct((rows, model), FULL),
             jax.ShapeDtypeStruct((rows, model), LOW),
             long,
+            jax.ShapeDtypeStruct((taps + 4, width), FULL),
         ],
-        in_specs=[VMEM] * 6 + [ANY] * 5,
-        out_specs=[VMEM] * 14,
+        in_specs=[VMEM] * 4 + [ANY] * 5,
+        out_specs=[VMEM] * 15,
         scratch_shapes=[
             pltpu.VMEM(win.shape, LOW),
             pltpu.VMEM(wbr.shape, LOW),
@@ -1574,7 +1579,7 @@
         + [pltpu.SemaphoreType.DMA((3,)), pltpu.SemaphoreType.DMA((1,))],
         compiler_params=comm_params(0),
         cost_estimate=lasting(135),
-    )(x, gain, doc, rows8, slope, second, win, wbr, gate_r, gate_i, weight)
+    )(x, doc, table, slope, win, wbr, gate_r, gate_i, weight)
 
 
 def turn_kernel(
@@ -1926,24 +1931,30 @@
     )(do, y, r, ii, h, edges, c, u, halo, mask, rows8, gate_r, gate_i, down, gate)
 
 
-def widen_kernel(count, *refs):
-    for source, target in zip(refs[:count], refs[count:]):
+def widen_kernel(count, head, *refs):
+    sources, targets = refs[: count + 1], refs[count + 1 :]
+    for source, target in zip(sources[:count], targets[:count]):
         target[...] = source[...].astype(target.dtype)
-
-
-def widen(n, terms, kept):
+    targets[count][...] = sources[count][:, :head]
+    targets[count + 1][...] = sources[count][:, head : 2 * head]
+
+
+def widen(n, head, terms, kept, small):
     arrays = terms + kept
+    part = small.shape[0]
+    gate = jax.ShapeDtypeStruct((part, head), FULL)
     blocks = [
         pl.BlockSpec((term.shape[0], term.shape[1] // n), lambda k: (0, k)) for term in arrays
     ]
     return pl.pallas_call(
-        functools.partial(widen_kernel, len(arrays)),
+        functools.partial(widen_kernel, len(arrays), head),
         grid=(n,),
-        in_specs=blocks,
-        out_specs=blocks,
+        in_specs=blocks + [pl.BlockSpec(small.shape, lambda k: (0, 0))],
+        out_specs=blocks + [pl.BlockSpec((part, head), lambda k: (0, 0))] * 2,
         out_shape=[jax.ShapeDtypeStruct(term.shape, FULL) for term in terms]
-        + [jax.ShapeDtypeStruct(term.shape, term.dtype) for term in kept],
-    )(*arrays)
+        + [jax.ShapeDtypeStruct(term.shape, term.dtype) for term in kept]
+        + [gate, gate],
+    )(*arrays, small)
 
 
 def on_device(
@@ -1977,27 +1988,19 @@
     edge = width % head
     rows = shards * part_len
 
-    def mine(vector):
-        return lax.dynamic_slice_in_dim(vector, me_w * width, width, 0)
-
     x = inputs[0]
     slope = cotangent[0]
-    rate = mine(decay_rate)
-    soft = -8.0 * jax.nn.softplus(rate)
-    conv_mine = mine(conv_weight)
-    rows8 = jnp.concatenate(
-        [conv_mine.T, jnp.stack([mine(recur_bias), mine(input_bias), soft, rate])], axis=0
-    )
-    xn, u3, y, o, c_ext, r, ii, h, ends, halo, mask, x1, xn2, dm = head_part(
+    soft = -8.0 * jax.nn.softplus(decay_rate)
+    vectors = [recur_bias, input_bias, soft, decay_rate, mixer_gain, second_gain]
+    table = jnp.concatenate([conv_weight.T, jnp.stack(vectors)], axis=0)
+    xn, u3, y, o, c_ext, r, ii, h, ends, halo, mask, x1, xn2, dm, rows8 = head_part(
         shards,
         places,
         taps,
         x,
-        mixer_gain[None],
         segment,
-        rows8,
+        table,
         slope,
-        second_gain[None],
         input_weight,
         branch_weight,
         recur_gate,
@@ -2016,7 +2019,7 @@
         dxn2,
         x1,
         slope,
-        second_gain[None],
+        table,
         down_term.reshape(cut),
         output_weight,
         down_weight,
@@ -2053,7 +2056,7 @@
         o,
         x,
         dx1,
-        mixer_gain[None],
+        table,
         second_gain_grad,
         small.reshape(places, -1, small.shape[1]),
         xn,
@@ -2073,7 +2076,9 @@
         input_weight_grad,
         input_grad,
         block_out,
-    ) = widen(shards, terms, [input_grad, block_out])
+        recur_grad,
+        gate_in_grad,
+    ) = widen(shards, head, terms, [input_grad, block_out], small)
     gains = lax.dynamic_slice_in_dim(gains, (me_s * shards + me_w) * part, part, 1)
 
     at = 2 * head + taps
@@ -2084,8 +2089,8 @@
         input_weight_grad,
         branch_grad,
         small[:, 2 * head : at],
-        small[:, :head],
-        small[:, head : 2 * head],
+        recur_grad,
+        gate_in_grad,
         small[:, at],
         small[:, at + 1],
         small[:, at + 2],

time: 563 us -> 560 us (level)
  no operation moved by 1% of the time
where the time goes in v6:
time: 560 us; the launch traced here: 551 us
  Pallas kernels  541 us (97%)
  local copies, waits for them, and re-layouts  8.41 us (2%)
    pallas_call x1, Pallas kernels, leave(): pl.pallas_call(functools.partial(leave_kernel, n, places, bits), out_shap...  162 us
    pallas_call x1, Pallas kernels, head_part(): pl.pallas_call(functools.partial(head_kernel, n, places, taps), out_shape...  136 us
    pallas_call x1, Pallas kernels, ffn(): pl.pallas_call(functools.partial(ffn_kernel, n, places), out_shape=[jax.S...  104 us
    pallas_call x1, Pallas kernels, back_in(): pl.pallas_call(functools.partial(back_in_kernel, n, places, bits), out_sh...  71.1 us
    pallas_call x1, Pallas kernels, turn_back(): pl.pallas_call(functools.partial(turn_kernel, n, places, taps, bits), out...  59.1 us

profile of v6, /device:TPU:10, one launch (start us, length us, event | category | flops | bytes accessed | tf_op | source)
XLA Modules:
  0.0 551.1 jit_solution(17078415312843265948)
XLA Ops:
  0.6 0.7 fusion
  1.4 0.7 stack.18
  2.1 0.7 stack.19
  2.8 0.7 stack.21
  3.5 0.7 stack.22
  4.3 0.7 stack.23
  5.0 2.1 concatenate.3.refs_2_.refs_3_.refs_5_
  7.1 135.6 %shard_map.288 = (bf16[4,128,2560]{2,1,0:T(8,128)(2,1)}, bf16[4,128,640]{2,1,0:T(8,128)(2,1)}, f32[4,128,640]{2,1,0:T(8,128)}, bf16[4,128,640]{2,1,0:T(8,128)(2,...) custom-call(bf16[128,2560]{1,0:T(8,128)(2,1)} %bitcast.16, ...), custom_call_target="tpu_custom_call" | custom-call | flops 134999998464 | bytes 459000000 | tf_op jit(solution)/shard_map/pallas_call | solution.py:1536
  142.7 104.4 %shard_map.289 = (f32[128,2560]{1,0:T(8,128)}, bf16[4,128,1920]{2,1,0:T(8,128)(2,1)}, bf16[4,128,1920]{2,1,0:T(8,128)(2,1)}, bf16[4,128,1920]{2,1,0:T(8,128)(2,1...) custom-call(bf16[128,2560]{1,0:T(8,128)(2,1)} %get-tuple-element.68.xn2_ref, ...), custom_call_target="tpu_custom_call" | custom-call | flops 105000001536 | bytes 357000000 | tf_op jit(solution)/shard_map/pallas_call | solution.py:694
  247.1 71.1 %shard_map.290 = (f32[128,2560]{1,0:T(8,128)}, bf16[4,128,2560]{2,1,0:T(8,128)(2,1)}, f32[4,128,640]{2,1,0:T(8,128)}, f32[1,2560]{1,0:T(1,128)}, bf16[128,2560]{...) custom-call(f32[128,2560]{1,0:T(8,128)} %get-tuple-element.70.refs_0_, ...), custom_call_target="tpu_custom_call" | custom-call | flops 74999996416 | bytes 255000000 | tf_op jit(solution)/shard_map/pallas_call | solution.py:810
  318.2 59.1 %shard_map.291 = (bf16[4,128,640]{2,1,0:T(8,128)(2,1)}, bf16[4,128,640]{2,1,0:T(8,128)(2,1)}, bf16[640,640]{1,0:T(8,128)(2,1)}, bf16[80,7680]{1,0:T(8,128)(2,1)}, bf16[4,80,1920]{2,1,0:T(8,128)(2,1)}) custom-call(f32[4,128,640]{2,1,0:T(8,128)} %get-tuple-element.77.do_ref, f32[4,128,640]{2,1,0:T(8,128)} %get-tuple-element.78.y_ref, ...), custom_call_target="tpu_custom_call" | custom-call | flops 44999999488 | bytes 153000000 | tf_op jit(solution)/shard_map/pallas_call | solution.py:1890
  377.3 162.3 %shard_map.292 = (f32[128,2560]{1,0:T(8,128)}, f32[8,2560]{1,0:T(8,128)}, f32[80,640]{1,0:T(8,128)}, bf16[80,7680]{1,0:T(8,128)(2,1)}, bf16[80,7680]{1,0:T(8,128...) custom-call(bf16[4,128,640]{2,1,0:T(8,128)(2,1)} %get-tuple-element., ...), custom_call_target="tpu_custom_call" | custom-call | flops 140000002048 | bytes 476000000 | tf_op jit(solution)/shard_map/pallas_call | solution.py:1105
  539.6 0.0 copy-start
  539.7 8.3 %shard_map.293 = (f32[80,7680]{1,0:T(8,128)}, f32[80,7680]{1,0:T(8,128)}, f32[80,7680]{1,0:T(8,128)}, f32[80,2560]{1,0:T(8,128)}, f32[80,2560]{1,0:T(8,128)}, /*...) custom-call(bf16[80,7680]{1,0:T(8,128)(2,1)} %get-tuple-element.90.r, ...), custom_call_target="tpu_custom_call" | custom-call | tf_op jit(solution)/shard_map/pallas_call | solution.py:1949
  547.9 0.0 copy-done
  548.0 0.7 copy.34
  548.6 0.8 constant_dynamic-slice_fusion
  549.4 0.5 slice_bitcast_fusion
  549.9 0.7 slice_reduce_fusion
  (2 shorter events, 0.0 us)
Async XLA Ops:
  539.6 8.3 %copy-start = (f32[80,640]{1,0:T(8,128)S(1)}, f32[80,640]{1,0:T(8,128)}, u32[]{:S(2)}) copy-start(f32[80,640]{1,0:T(8,128)} %get-tuple-element.108.refs_8_) | copy-start | bytes 614404

commit v7 on v6

--- a/solution.py
+++ b/solution.py
@@ -994,7 +994,10 @@
         for k, source in enumerate([gate_hbm, kept.at[pl.ds(0, n)], kept.at[pl.ds(n, n)]])
     ]
     work = pair.tasks(model // size, compute, mix_hbm)
-    tasks = work[:-1] + [lambda: (work[-1](), plane.advance(0), spreads[0].start())]
+    tasks = work[:-2] + [
+        lambda: (plane.advance(0), work[-2]()),
+        lambda: (work[-1](), spreads[0].start()),
+    ]
     line_reduce(n, me, parts, slots, sent, landed, partial, tasks, finish, early)
     pair.finish(mix_hbm)
 

time: 560 us -> 560 us (level)
  no operation moved by 1% of the time
where the time goes in v7:
time: 560 us; the launch traced here: 551 us
  Pallas kernels  541 us (97%)
  local copies, waits for them, and re-layouts  8.41 us (2%)
    pallas_call x1, Pallas kernels, leave(): pl.pallas_call(functools.partial(leave_kernel, n, places, bits), out_shap...  162 us
    pallas_call x1, Pallas kernels, head_part(): pl.pallas_call(functools.partial(head_kernel, n, places, taps), out_shape...  136 us
    pallas_call x1, Pallas kernels, ffn(): pl.pallas_call(functools.partial(ffn_kernel, n, places), out_shape=[jax.S...  104 us
    pallas_call x1, Pallas kernels, back_in(): pl.pallas_call(functools.partial(back_in_kernel, n, places, bits), out_sh...  71.1 us
    pallas_call x1, Pallas kernels, turn_back(): pl.pallas_call(functools.partial(turn_kernel, n, places, taps, bits), out...  59.1 us

profile of v7, /device:TPU:10, one launch (start us, length us, event | category | flops | bytes accessed | tf_op | source)
XLA Modules:
  0.0 551.1 jit_solution(16533844308862779724)
XLA Ops:
  0.6 0.7 fusion
  1.4 0.7 stack.18
  2.1 0.7 stack.19
  2.8 0.7 stack.21
  3.5 0.7 stack.22
  4.3 0.7 stack.23
  5.0 2.1 concatenate.3.refs_2_.refs_3_.refs_5_
  7.1 135.6 %shard_map.288 = (bf16[4,128,2560]{2,1,0:T(8,128)(2,1)}, bf16[4,128,640]{2,1,0:T(8,128)(2,1)}, f32[4,128,640]{2,1,0:T(8,128)}, bf16[4,128,640]{2,1,0:T(8,128)(2,...) custom-call(bf16[128,2560]{1,0:T(8,128)(2,1)} %bitcast.16, ...), custom_call_target="tpu_custom_call" | custom-call | flops 134999998464 | bytes 459000000 | tf_op jit(solution)/shard_map/pallas_call | solution.py:1539
  142.7 104.4 %shard_map.289 = (f32[128,2560]{1,0:T(8,128)}, bf16[4,128,1920]{2,1,0:T(8,128)(2,1)}, bf16[4,128,1920]{2,1,0:T(8,128)(2,1)}, bf16[4,128,1920]{2,1,0:T(8,128)(2,1...) custom-call(bf16[128,2560]{1,0:T(8,128)(2,1)} %get-tuple-element.68.xn2_ref, ...), custom_call_target="tpu_custom_call" | custom-call | flops 105000001536 | bytes 357000000 | tf_op jit(solution)/shard_map/pallas_call | solution.py:694
  247.1 71.1 %shard_map.290 = (f32[128,2560]{1,0:T(8,128)}, bf16[4,128,2560]{2,1,0:T(8,128)(2,1)}, f32[4,128,640]{2,1,0:T(8,128)}, f32[1,2560]{1,0:T(1,128)}, bf16[128,2560]{...) custom-call(f32[128,2560]{1,0:T(8,128)} %get-tuple-element.70.refs_0_, ...), custom_call_target="tpu_custom_call" | custom-call | flops 74999996416 | bytes 255000000 | tf_op jit(solution)/shard_map/pallas_call | solution.py:810
  318.2 59.1 %shard_map.291 = (bf16[4,128,640]{2,1,0:T(8,128)(2,1)}, bf16[4,128,640]{2,1,0:T(8,128)(2,1)}, bf16[640,640]{1,0:T(8,128)(2,1)}, bf16[80,7680]{1,0:T(8,128)(2,1)}, bf16[4,80,1920]{2,1,0:T(8,128)(2,1)}) custom-call(f32[4,128,640]{2,1,0:T(8,128)} %get-tuple-element.77.do_ref, f32[4,128,640]{2,1,0:T(8,128)} %get-tuple-element.78.y_ref, ...), custom_call_target="tpu_custom_call" | custom-call | flops 44999999488 | bytes 153000000 | tf_op jit(solution)/shard_map/pallas_call | solution.py:1893
  377.3 162.3 %shard_map.292 = (f32[128,2560]{1,0:T(8,128)}, f32[8,2560]{1,0:T(8,128)}, f32[80,640]{1,0:T(8,128)}, bf16[80,7680]{1,0:T(8,128)(2,1)}, bf16[80,7680]{1,0:T(8,128...) custom-call(bf16[4,128,640]{2,1,0:T(8,128)(2,1)} %get-tuple-element., ...), custom_call_target="tpu_custom_call" | custom-call | flops 140000002048 | bytes 476000000 | tf_op jit(solution)/shard_map/pallas_call | solution.py:1108
  539.6 0.0 copy-start
  539.7 8.3 %shard_map.293 = (f32[80,7680]{1,0:T(8,128)}, f32[80,7680]{1,0:T(8,128)}, f32[80,7680]{1,0:T(8,128)}, f32[80,2560]{1,0:T(8,128)}, f32[80,2560]{1,0:T(8,128)}, /*...) custom-call(bf16[80,7680]{1,0:T(8,128)(2,1)} %get-tuple-element.90.r, ...), custom_call_target="tpu_custom_call" | custom-call | tf_op jit(solution)/shard_map/pallas_call | solution.py:1952
  547.9 0.0 copy-done
  548.0 0.7 copy.34
  548.6 0.8 constant_dynamic-slice_fusion
  549.4 0.5 slice_bitcast_fusion
  549.9 0.7 slice_reduce_fusion
  (2 shorter events, 0.0 us)
Async XLA Ops:
  539.6 8.3 %copy-start = (f32[80,640]{1,0:T(8,128)S(1)}, f32[80,640]{1,0:T(8,128)}, u32[]{:S(2)}) copy-start(f32[80,640]{1,0:T(8,128)} %get-tuple-element.108.refs_8_) | copy-start | bytes 614404
